TPU v7x, 128 devices: a whole 4x4x4 slice. The times are simulated.
128 devices in a mesh: dp: 32 (over z, x, core), group: 4 (over y).
Axes of the slice: x: 4, y: 4, z: 4, core: 2. Of those that a mesh axis runs over, the one named last changes fastest.
Arguments:
- queries: bfloat16 [20480, 1024], P(('dp', 'group')), may hold values from -120 to 120
- passages: bfloat16 [20480, 1024], P(('dp', 'group')), may hold values from -12 to 12
- weight: bfloat16 [1024, 1024], P(('dp', 'group')), may hold values from -0.1875 to 0.1875
- block_list: int32 [128, 32], replicated, may hold values from 0 to 31, as said below
- list_len: int32 [128], replicated, may hold values from 2 to 32, as said below
Outputs:
- losses: float32 [20480], P(('dp', 'group'))
- grad_queries: bfloat16 [20480, 1024], P(('dp', 'group'))
- grad_passages: bfloat16 [20480, 1024], P(('dp', 'group'))
- grad_weight: float32 [1024, 1024], P(('dp', 'group'))
Inputs may be any that keep to these rules, and one draw needn't show every extreme that they name: `block_list`: each row is an order of 0 to 31 whose first entry is the device's own dp index d. `list_len`: some device scores all 32 blocks of its domain and some only 2.
All inputs are finite; a program needn't handle non-finite values.
Results may differ from a plain program's by a relative error of at most 0.011.
Values may be sent and summed in bfloat16 or wider, within the bound.
No kernel may reach another device: no remote copies, remote signals or barrier semaphores. Data moves between devices by JAX's collectives and lax.ppermute only.
A program may use at most 128 MiB of HBM per device.

v0:
```python
import math

import jax
import jax.numpy as jnp
from jax import lax
from jax.sharding import PartitionSpec as P


def local(queries, passages, weight, block_list, list_len):
    row_count, feat_width = queries.shape
    n_domain = lax.axis_size("dp")
    n_groups = lax.axis_size("group")
    my_dp = lax.axis_index("dp")
    my_group = lax.axis_index("group")
    logit_scale = 1.0 / math.sqrt(feat_width)
    contract_last = (((1,), (1,)), ((), ()))
    contract_first = (((0,), (0,)), ((), ()))
    full_weight = lax.all_gather(weight, ("dp", "group"), axis=0, tiled=True)
    query_emb = jnp.dot(queries, full_weight, preferred_element_type=jnp.float32).astype(
        jnp.bfloat16
    )
    passage_emb = jnp.dot(passages, full_weight, preferred_element_type=jnp.float32).astype(
        jnp.bfloat16
    )
    domain = lax.all_gather(passage_emb, "dp", axis=0, tiled=True)
    slot_ids = jnp.arange(n_domain, dtype=jnp.int32)
    domain_lists = lax.dynamic_index_in_dim(
        block_list.reshape(n_domain, n_groups, n_domain), my_group, 1, keepdims=False
    )
    domain_lens = lax.dynamic_index_in_dim(
        list_len.reshape(n_domain, n_groups), my_group, 1, keepdims=False
    )
    live_slots = slot_ids[None, :] < domain_lens[:, None]
    listed = jnp.any(
        (domain_lists[:, :, None] == slot_ids[None, None, :]) & live_slots[:, :, None], axis=1
    )
    mine = lax.dynamic_index_in_dim(listed, my_dp, 0, keepdims=False)
    scores = logit_scale * lax.dot_general(
        query_emb, domain, contract_last, preferred_element_type=jnp.float32
    )
    col_live = jnp.repeat(mine, row_count)
    masked = jnp.where(col_live[None, :], scores, -1e30)
    row_max = jnp.max(masked, axis=1)
    log_total = row_max + jnp.log(jnp.sum(jnp.exp(masked - row_max[:, None]), axis=1))
    probs = jnp.where(col_live[None, :], jnp.exp(scores - log_total[:, None]), 0.0)
    column_ids = jnp.arange(n_domain * row_count, dtype=jnp.int32)
    own_rows = my_dp * row_count + jnp.arange(row_count, dtype=jnp.int32)
    positive = column_ids[None, :] == own_rows[:, None]
    pos_score = jnp.sum(jnp.where(positive, scores, 0.0), axis=1)
    losses = log_total - pos_score
    grads = (probs - positive.astype(jnp.float32)).astype(jnp.bfloat16)
    query_grad = (logit_scale * jnp.dot(grads, domain, preferred_element_type=jnp.float32)).astype(
        jnp.bfloat16
    )
    passage_sum = lax.psum_scatter(
        logit_scale
        * lax.dot_general(grads, query_emb, contract_first, preferred_element_type=jnp.float32),
        "dp",
        scatter_dimension=0,
        tiled=True,
    )
    passage_grad = passage_sum.astype(jnp.bfloat16)
    grad_queries = lax.dot_general(
        query_grad, full_weight, contract_last, preferred_element_type=jnp.float32
    ).astype(jnp.bfloat16)
    grad_passages = lax.dot_general(
        passage_grad, full_weight, contract_last, preferred_element_type=jnp.float32
    ).astype(jnp.bfloat16)
    first_part = lax.dot_general(
        queries, query_grad, contract_first, preferred_element_type=jnp.float32
    )
    second_part = lax.dot_general(
        passages, passage_grad, contract_first, preferred_element_type=jnp.float32
    )
    grad_weight = lax.psum_scatter(
        first_part + second_part, ("dp", "group"), scatter_dimension=0, tiled=True
    )
    return (losses, grad_queries, grad_passages, grad_weight)


def solution(mesh):
    placed = (
        P(("dp", "group"), None),
        P(("dp", "group"), None),
        P(("dp", "group"), None),
        P(),
        P(),
    )
    return jax.shard_map(
        local,
        mesh=mesh,
        in_specs=placed,
        out_specs=(
            P(("dp", "group")),
            P(("dp", "group"), None),
            P(("dp", "group"), None),
            P(("dp", "group"), None),
        ),
        check_vma=False,
    )
```

profile of v0, /device:TPU:0, one launch (start us, length us, event | category | flops | bytes accessed | tf_op | source)
XLA Modules:
  0.0 943.2 jit_solution(14868005126344061702)
XLA Ops:
  7.2 0.0 copy-start
  7.2 0.0 all-gather.3.cloned.1.call-start
  7.2 0.7 all-gather.3.cloned.1.call-update
  7.9 0.0 all-gather.5.cloned.1.call-start
  8.0 70.7 %all-gather.3.cloned.1.call-done = bf16[1024,1024]{1,0:T(8,128)(2,1)} async-done(((bf16[8,1024]{1,0:T(8,128)(2,1)}), bf16[1024,1024]{1,0:T(8,128)(2,1)}) %all-gather.3.cloned.1.call-update) | async-done | bytes 2097168 | tf_op jit(solution)/shard_map/all_gather | solution.py:18
  78.7 0.0 copy-start.1
  78.7 3.1 convolution_convert_fusion.2
  81.8 0.0 all-gather.5.cloned.1.call-update
  81.8 0.0 reduce-scatter.5.cloned.1.call-start
  81.8 0.8 copy.14
  82.7 0.8 reshape.51
  83.4 0.2 dynamic-slice_reduce_fusion
  83.6 0.1 iota_compare_fusion.2
  83.7 0.4 fusion.2
  84.1 0.1 broadcast_in_dim.34
  84.2 0.1 broadcast_in_dim.35
  84.3 0.0 copy-done
  84.3 0.0 copy-done.1
  84.3 0.5 convolution_convert_fusion.3
  84.8 52.5 %all-gather.5.cloned.1.call-done = bf16[5120,1024]{1,0:T(8,128)(2,1)} async-done(((bf16[160,1024]{1,0:T(8,128)(2,1)}), bf16[5120,1024]{1,0:T(8,128)(2,1)}) %all-gather.5.cloned.1.call-update) | async-done | bytes 10485776 | tf_op jit(solution)/shard_map/all_gather | solution.py:25
  137.3 7.7 select_reduce_fusion.1
  145.1 0.0 copy-start.2
  145.1 1.3 select_reduce_fusion
  146.4 0.6 fusion.5
  147.0 0.0 copy-done.2
  147.0 8.8 convolution_multiply_fusion
  155.8 0.0 reduce-scatter.5.cloned.1.call-update
  155.8 0.2 reduce-scatter.7.cloned.1.call-start
  156.0 7.1 fusion
  163.2 0.0 copy-start.4
  163.2 2.7 fusion.6
  165.9 117.8 %reduce-scatter.5.cloned.1.call-done = f32[160,1024]{1,0:T(8,128)} async-done(((f32[5120,1024]{1,0:T(8,128)}), f32[160,1024]{1,0:T(8,128)}) %reduce-scatter.5.cloned.1.call-update) | async-done | bytes 655376 | tf_op jit(solution)/shard_map/reduce_scatter | solution.py:55
  283.7 0.0 copy-done.4
  283.7 5.1 add_bitcast_fusion
  288.8 5.3 copy.16
  294.2 0.0 copy-start.3
  294.2 0.0 reduce-scatter.7.cloned.1.call-update
  294.2 1.6 convolution_convert_fusion.1
  295.8 0.0 copy-done.3
  295.8 1.6 convolution_convert_fusion
  297.3 639.3 %reduce-scatter.7.cloned.1.call-done = f32[8,1024]{1,0:T(8,128)} async-done(((f32[1024,1024]{1,0:T(8,128)}), f32[8,1024]{1,0:T(8,128)}) %reduce-scatter.7.cloned.1.call-update) | async-done | bytes 32784
  (3 shorter events, 0.0 us)
Async XLA Ops:
  7.2 77.1 %copy-start = (bf16[160,1024]{1,0:T(8,128)(2,1)S(1)}, bf16[160,1024]{1,0:T(8,128)(2,1)}, u32[]{:S(2)}) copy-start(bf16[160,1024]{1,0:T(8,128)(2,1)} %param.5) | copy-start | bytes 983044
  7.2 71.5 %all-gather.3.cloned.1.call-start = ((), (), s32[]{:S(2)}) async-start(), calls=%async_computation.2 | async-start | bytes 2113536 | tf_op jit(solution)/shard_map/all_gather | solution.py:18
  7.9 129.4 %all-gather.5.cloned.1.call-start = ((), (), s32[]{:S(2)}) async-start(), calls=%async_computation.3 | async-start | bytes 10813440 | tf_op jit(solution)/shard_map/all_gather | solution.py:25
  78.7 5.6 copy-start.1
  81.8 201.9 %reduce-scatter.5.cloned.1.call-start = ((), (), s32[]{:S(2)}) async-start(), calls=%async_computation.4 | async-start | bytes 21626880 | tf_op jit(solution)/shard_map/reduce_scatter | solution.py:55
  145.1 1.9 copy-start.2
  155.8 780.8 %reduce-scatter.7.cloned.1.call-start = ((), (), s32[]{:S(2)}) async-start(), calls=%async_computation.5 | async-start | bytes 4227072
  163.2 120.5 %copy-start.4 = (bf16[160,1024]{1,0:T(8,128)(2,1)S(1)}, bf16[160,1024]{1,0:T(8,128)(2,1)}, u32[]{:S(2)}) copy-start(bf16[160,1024]{1,0:T(8,128)(2,1)} %param.6) | copy-start | bytes 983044
  294.2 1.6 copy-start.3
Sparse Core Ops, SparseCore 0:
  11.0 67.6 all-gather.2
  81.9 55.3 all-gather.4
  155.9 127.7 reduce-scatter.4
  294.3 642.3 reduce-scatter.6
where the time goes:
time: 943 us
  waiting for transfers between devices  881 us (93%)
  matrix products  38.2 us (4%)
  between operations  13.9 us (1%)
    unnamed x5, waiting for transfers between devices  640 us
    reduce_scatter x1, waiting for transfers between devices, local(): lax.psum_scatter(logit_scale * lax.dot_general(grads, query_emb, contract...  118 us
    all_gather x1, waiting for transfers between devices, local(): full_weight = lax.all_gather(weight, ('dp', 'group'), axis=0, tiled=True)  70.7 us
    all_gather x1, waiting for transfers between devices, local(): domain = lax.all_gather(passage_emb, 'dp', axis=0, tiled=True)  52.5 us
  transfers between devices with their start and end apart: 4, of which 4 were waited for; matrix products, arithmetic and copies ran while one was open for 2% of the time, Pallas kernels for 0%

commit v1 on v0

v1 whole, which is shorter than its diff:
```python
import math

import jax
import jax.numpy as jnp
from jax import lax
from jax.sharding import Mesh, PartitionSpec as P

SIZES = {"z": 4, "x": 4, "c": 2, "y": 4}
AXES = ("z", "x", "c", "y")
OFFSETS = (0, -1, 1, 2)
BF16 = jnp.bfloat16
F32 = jnp.float32
LAST = (((1,), (1,)), ((), ()))
FIRST = (((0,), (0,)), ((), ()))


def shift(value, axis, step):
    size = SIZES[axis]
    return lax.ppermute(value, axis, [(i, (i + step) % size) for i in range(size)])


def collect(value, axis):
    return [value] + [shift(value, axis, -step) for step in OFFSETS[1:]]


def hand_back(blocks, axis):
    return [blocks[0]] + [shift(block, axis, step) for block, step in zip(blocks[1:], OFFSETS[1:])]


def place(offset):
    return OFFSETS.index((offset + 1) % 4 - 1)


def by_offset(blocks, axis):
    me = lax.axis_index(axis)
    stacked = jnp.stack([blocks[place(o)] for o in range(4)])
    return jnp.concatenate([lax.dynamic_slice_in_dim(stacked, (i - me) % 4, 1, 0) for i in range(4)])


def dot(a, b, dims=(((1,), (0,)), ((), ()))):
    return lax.dot_general(a, b, dims, preferred_element_type=F32)


def gather_weight(weight):
    rows, width = weight.shape
    part = by_offset(collect(weight, "z"), "z")
    part = by_offset(collect(part, "x"), "x")
    part = by_offset(collect(part, "y"), "y")
    other = shift(part, "c", 1)
    core = lax.axis_index("c")
    both = jnp.stack([jnp.where(core == 0, part, other), jnp.where(core == 0, other, part)])
    return both.transpose(3, 2, 0, 1, 4, 5).reshape(-1, width)


def reduce_weight(total, rows):
    width = total.shape[1]
    parts = total.reshape(4, 4, 2, 4, rows, width).transpose(2, 3, 1, 0, 4, 5)
    core = lax.axis_index("c")
    mine = jnp.where(core == 0, parts[0], parts[1])
    theirs = jnp.where(core == 0, parts[1], parts[0])
    part = mine + shift(theirs.astype(BF16), "c", 1).astype(F32)
    for axis in ("y", "x", "z"):
        me = lax.axis_index(axis)
        pieces = [lax.dynamic_index_in_dim(part, (me + o) % 4, 0, keepdims=False) for o in OFFSETS]
        came = hand_back([pieces[0]] + [p.astype(BF16) for p in pieces[1:]], axis)
        part = sum(c.astype(F32) for c in came)
    return part


def local(queries, passages, weight, block_list, list_len):
    rows, width = queries.shape
    scale = 1.0 / math.sqrt(width)
    z, x, c, y = (lax.axis_index(a) for a in AXES)

    query_blocks = jnp.concatenate(collect(queries, "x"))
    passage_blocks = jnp.concatenate(collect(passages, "z"))
    full_weight = gather_weight(weight)

    owners = jnp.stack([(z * 4 + (x + o) % 4) * 2 + c for o in OFFSETS])
    lists = block_list[owners * 4 + y]
    lens = list_len[owners * 4 + y]
    live = jnp.arange(lists.shape[1])[None, :] < lens[:, None]

    def scored(core):
        blocks = jnp.stack([((z + o) % 4 * 4 + x) * 2 + core for o in OFFSETS])
        hit = jnp.any((lists[:, :, None] == blocks[None, None, :]) & live[:, :, None], axis=1)
        return jnp.repeat(hit, rows, axis=1)[:, None, :]

    passage_emb = dot(passage_blocks, full_weight).astype(BF16)
    other_emb = shift(passage_emb, "c", 1)
    query_emb = dot(query_blocks, full_weight).astype(BF16)

    def scores_of(emb):
        return (scale * dot(query_emb, emb, LAST)).reshape(4, rows, -1)

    scores = [scores_of(passage_emb), scores_of(other_emb)]
    masks = [scored(c), scored(1 - c)]
    own_max = jnp.maximum(*[jnp.max(jnp.where(m, s, -1e30), axis=2) for m, s in zip(masks, scores)])
    probs = [jnp.where(m, jnp.exp(s - own_max[:, :, None]), 0.0) for m, s in zip(masks, scores)]
    own_sum = sum(jnp.sum(p, axis=2) for p in probs)

    row_ids = lax.broadcasted_iota(jnp.int32, scores[0].shape, 0) * rows + lax.broadcasted_iota(
        jnp.int32, scores[0].shape, 1
    )
    col_ids = lax.broadcasted_iota(jnp.int32, scores[0].shape, 2)
    positive = (row_ids == col_ids) & (row_ids < rows)
    probs[0] = jnp.where(positive, 0.0, probs[0])
    pos_score = jnp.sum(jnp.where(positive[0], scores[0][0], 0.0), axis=1)
    probs = [p.reshape(4 * rows, -1).astype(BF16) for p in probs]

    stats = collect(jnp.stack([own_max, own_sum]), "x")
    stats = [
        jnp.stack([s[:, place(block - sender)] for block in OFFSETS], axis=1)
        for s, sender in zip(stats, OFFSETS)
    ]
    top = jnp.max(jnp.stack([s[0] for s in stats]), axis=0)
    log_total = top + jnp.log(sum(s[1] * jnp.exp(s[0] - top) for s in stats))
    factor = jnp.exp(own_max - log_total).reshape(-1, 1)
    losses = log_total[0] - pos_score
    pos_grad = (jnp.exp(pos_score - log_total[0]) - 1.0)[:, None]

    def blocks_of(value):
        return [value[i * rows : (i + 1) * rows] for i in range(4)]

    scaled_emb = (query_emb * factor).astype(BF16)
    other_part = dot(probs[1], scaled_emb, FIRST).astype(BF16)
    passage_part = dot(probs[0], scaled_emb, FIRST) + shift(other_part, "c", 1).astype(F32)
    passage_part = blocks_of(passage_part)
    passage_part[0] = passage_part[0] + pos_grad * query_emb[:rows]
    passage_low = [p.astype(BF16) for p in passage_part]
    passage_sum = sum(p.astype(F32) for p in hand_back([passage_part[0]] + passage_low[1:], "z"))

    query_part = factor * (dot(probs[0], passage_emb) + dot(probs[1], other_emb))
    query_part = blocks_of(query_part)
    query_part[0] = query_part[0] + pos_grad * passage_emb[:rows]
    query_low = [p.astype(BF16) for p in query_part]
    query_sum = sum(p.astype(F32) for p in hand_back([query_part[0]] + query_low[1:], "x"))

    weight_part = dot(query_blocks, jnp.concatenate(query_low), FIRST) + dot(
        passage_blocks, jnp.concatenate(passage_low), FIRST
    )
    grad_weight = scale * reduce_weight(weight_part, weight.shape[0])

    query_grad = (scale * query_sum).astype(BF16)
    passage_grad = (scale * passage_sum).astype(BF16)
    grad_queries = dot(query_grad, full_weight, LAST).astype(BF16)
    grad_passages = dot(passage_grad, full_weight, LAST).astype(BF16)
    return losses, grad_queries, grad_passages, grad_weight


def solution(mesh):
    grid = Mesh(mesh.devices.reshape([SIZES[a] for a in AXES]), AXES)
    table, line = P(AXES, None), P(AXES)
    return jax.shard_map(
        local,
        mesh=grid,
        in_specs=(table, table, table, P(), P()),
        out_specs=(line, table, table, table),
        check_vma=False,
    )
```

time: 943 us -> 156 us (0.17)
  waiting for transfers between devices: 881 us -> 47.8 us
  starting transfers between devices: 0.34 us -> 43.3 us
  between operations: 13.9 us -> 1.23 us
  other arithmetic: 2.38 us -> 13.6 us
  local copies, waits for them, and re-layouts: 7.33 us -> 17.7 us
    unnamed x5 -> x0, waiting for transfers between devices: 640 us -> none
    all_gather x2 -> x0, waiting for transfers between devices: 123 us -> none  [the longest x1 70.7 us: local(): full_weight = lax.all_gather(weight, ('dp', 'group'), axis=0, tiled=True)]
    reduce_scatter x1 -> x0, waiting for transfers between devices: 118 us -> none  [local(): lax.psum_scatter(logit_scale * lax.dot_general(grads, query_emb, contract...]
    ppermute x0 -> x37, waiting for transfers between devices: none -> 47.8 us  [shift(): lax.ppermute(value, axis, [(i, (i + step) % size) for i in range(size)])]
    ppermute x0 -> x37, starting transfers between devices: none -> 43.3 us  [shift(): lax.ppermute(value, axis, [(i, (i + step) % size) for i in range(size)])]
    dot_general x9 -> x12, matrix products: 38.2 us -> 31.1 us  [dot(): return lax.dot_general(a, b, dims, preferred_element_type=F32)]
  transfers between devices with their start and end apart: 4 -> 37, of which waited for: 4 -> 20; matrix products, arithmetic and copies ran while one was open for 2% -> 23% of each run, Pallas kernels for 0% -> 0%
where the time goes in v1:
time: 156 us; the launch traced here: 155 us
  waiting for transfers between devices  47.8 us (31%)
  starting transfers between devices  43.3 us (28%)
  matrix products  31.1 us (20%)
  local copies, waits for them, and re-layouts  17.7 us (11%)
  other arithmetic  13.6 us (9%)
    ppermute x37, waiting for transfers between devices, shift(): lax.ppermute(value, axis, [(i, (i + step) % size) for i in range(size)])  47.8 us
    ppermute x37, starting transfers between devices, shift(): lax.ppermute(value, axis, [(i, (i + step) % size) for i in range(size)])  43.3 us
    dot_general x12, matrix products, dot(): return lax.dot_general(a, b, dims, preferred_element_type=F32)  31.1 us
    unnamed x42, local copies, waits for them, and re-layouts  11 us
    reduce_sum x1, other arithmetic, local(): own_sum = sum((jnp.sum(p, axis=2) for p in probs))  3.92 us
    add x1, other arithmetic, reduce_weight(): part = mine + shift(theirs.astype(BF16), 'c', 1).astype(F32)  3.13 us
  transfers between devices with their start and end apart: 37, of which 20 were waited for; matrix products, arithmetic and copies ran while one was open for 23% of the time, Pallas kernels for 0%

profile of v1, /device:TPU:0, one launch (start us, length us, event | category | flops | bytes accessed | tf_op | source)
XLA Modules:
  0.0 154.8 jit_solution(7486586300786199246)
XLA Ops:
  0.7 4.2 %collective-permute-start.3 = (bf16[8,1024]{1,0:T(8,128)(2,1)}, bf16[8,1024]{1,0:T(8,128)(2,1)S(1)}, u32[]{:S(2)}, u32[]{:S(2)}) collective-permute-start(bf16[8,1024]{1,0:T(8,128)(2,1)} %param.7), channel_id=1, source_target_pairs={{0,96},{32,0},{64,32},{96,64},{1,97},{33,1},{65,33},{97,65},{2,98}... | collective-permute-start | bytes 49160 | tf_op jit(solution)/shard_map/ppermute | solution.py:19
  4.8 1.9 %collective-permute-start.4 = (bf16[8,1024]{1,0:T(8,128)(2,1)}, bf16[8,1024]{1,0:T(8,128)(2,1)S(1)}, u32[]{:S(2)}, u32[]{:S(2)}) collective-permute-start(bf16[8,1024]{1,0:T(8,128)(2,1)} %param.7), channel_id=1, source_target_pairs={{0,64},{32,96},{64,0},{96,32},{1,65},{33,97},{65,1},{97,33},{2,66}... | collective-permute-start | bytes 49160 | tf_op jit(solution)/shard_map/ppermute | solution.py:19
  6.7 3.3 %collective-permute-done.5 = bf16[8,1024]{1,0:T(8,128)(2,1)S(1)} collective-permute-done((bf16[8,1024]{1,0:T(8,128)(2,1)}, bf16[8,1024]{1,0:T(8,128)(2,1)S(1)}, u32[]{:S(2)}, u32[]{:S(2)}) %collective-permute-start.5) | collective-permute-done | bytes 16416 | tf_op jit(solution)/shard_map/ppermute | solution.py:19
  11.1 3.1 %collective-permute-start.7 = (bf16[4,8,1024]{2,1,0:T(8,128)(2,1)S(1)}, bf16[4,8,1024]{2,1,0:T(8,128)(2,1)S(1)}, u32[]{:S(2)}, u32[]{:S(2)}) collective-permute-start(bf16[4,8,1024]{2,1,0:T(8,128)(2,1)S(1)} %get-tuple-element.40), channel_id=1, source_target_pairs={{0,16},{8,24},{16,0},{24,8},{1,17},{9,25},{17,1},{25,9},{2,18},{10... | collective-permute-start | bytes 196616 | tf_op jit(solution)/shard_map/ppermute | solution.py:19
  14.2 1.1 collective-permute-start.6
  15.3 0.9 collective-permute-start.8
  16.9 1.5 collective-permute-done.6
  18.5 2.4 %collective-permute-done.8 = bf16[4,8,1024]{2,1,0:T(8,128)(2,1)S(1)} collective-permute-done((bf16[4,8,1024]{2,1,0:T(8,128)(2,1)S(1)}, bf16[4,8,1024]{2,1,0:T(8,128)(2,1)S(1)}, u32[]{:S(2)}, u32[]{:S(2)}) %collective-permute-start.8) | collective-permute-done | bytes 65568 | tf_op jit(solution)/shard_map/ppermute | solution.py:19
  20.9 3.3 %collective-permute-start.10 = (bf16[4,4,8,1024]{3,2,0,1:T(8,128)(2,1)S(1)}, bf16[4,4,8,1024]{3,2,0,1:T(8,128)(2,1)S(1)}, u32[]{:S(2)}, u32[]{:S(2)}) collective-permute-start(bf16[4,4,8,1024]{3,2,0,1:T(8,128)(2,1)S(1)} %get-tuple-element.31), channel_id=1, source_target_pairs={{0,2},{1,3},{2,0},{3,1},{4,6},{5,7},{6,4},{7,5},{8,10},{9,11},{10,... | collective-permute-start | bytes 786440 | tf_op jit(solution)/shard_map/ppermute | solution.py:19
  24.2 1.1 collective-permute-start.9
  25.3 1.0 collective-permute-start.11
  26.2 3.2 %collective-permute-start.14 = (bf16[160,1024]{1,0:T(8,128)(2,1)S(1)}, bf16[160,1024]{1,0:T(8,128)(2,1)}, u32[]{:S(2)}, u32[]{:S(2)}) collective-permute-start(bf16[160,1024]{1,0:T(8,128)(2,1)S(1)} %copy-done.13), channel_id=1, source_target_pairs={{0,96},{32,0},{64,32},{96,64},{1,97},{33,1},{65,33},{97,65},{2,98}... | collective-permute-start | bytes 983048 | tf_op jit(solution)/shard_map/ppermute | solution.py:19
  29.5 0.9 collective-permute-done.10
  30.3 1.8 %collective-permute-start.15 = (bf16[160,1024]{1,0:T(8,128)(2,1)S(1)}, bf16[160,1024]{1,0:T(8,128)(2,1)}, u32[]{:S(2)}, u32[]{:S(2)}) collective-permute-start(bf16[160,1024]{1,0:T(8,128)(2,1)S(1)} %copy-done.13), channel_id=1, source_target_pairs={{0,64},{32,96},{64,0},{96,32},{1,65},{33,97},{65,1},{97,33},{2,66}... | collective-permute-start | bytes 983048 | tf_op jit(solution)/shard_map/ppermute | solution.py:19
  32.2 1.3 collective-permute-done.9
  35.2 7.8 %collective-permute-done.13 = bf16[160,1024]{1,0:T(8,128)(2,1)} collective-permute-done((bf16[160,1024]{1,0:T(8,128)(2,1)S(1)}, bf16[160,1024]{1,0:T(8,128)(2,1)}, u32[]{:S(2)}, u32[]{:S(2)}) %collective-permute-start.13) | collective-permute-done | bytes 327712 | tf_op jit(solution)/shard_map/ppermute | solution.py:19
  43.0 1.0 constant_dynamic-update-slice_fusion.6
  44.0 1.6 %collective-permute-start.2 = (bf16[160,1024]{1,0:T(8,128)(2,1)}, bf16[160,1024]{1,0:T(8,128)(2,1)}, u32[]{:S(2)}, u32[]{:S(2)}) collective-permute-start(bf16[160,1024]{1,0:T(8,128)(2,1)} %param.5), channel_id=1, source_target_pairs={{0,16},{8,24},{16,0},{24,8},{1,17},{9,25},{17,1},{25,9},{2,18},{10... | collective-permute-start | bytes 983048 | tf_op jit(solution)/shard_map/ppermute | solution.py:19
  45.6 1.0 constant_dynamic-update-slice_fusion.5
  46.6 1.0 constant_dynamic-update-slice_fusion.4
  48.7 2.6 %convolution_convert_fusion = bf16[640,1024]{1,0:T(8,128)(2,1)} fusion(bf16[640,1024]{1,0:T(8,128)(2,1)S(1)} %constant_dynamic-update-slice_fusion.4, bf16[1024,1024]{1,0:T(8,128)(2,1)S(1)} %bitcast.164), kind=kOutput, calls=%fused_computation.19 | convolution fusion | flops 1342832640 | bytes 4718592 | tf_op jit(solution)/shard_map/dot_general | solution.py:41
  52.7 1.0 constant_dynamic-update-slice_fusion.3
  53.7 1.3 collective-permute-done
  55.1 1.0 constant_dynamic-update-slice_fusion.2
  56.1 1.0 constant_dynamic-update-slice_fusion.1
  57.1 1.0 constant_dynamic-update-slice_fusion
  58.1 1.1 copy-done.10
  59.2 1.6 %convolution_convert_fusion.1 = bf16[640,1024]{1,0:T(8,128)(2,1)S(1)} fusion(bf16[640,1024]{1,0:T(8,128)(2,1)S(1)} %constant_dynamic-update-slice_fusion, bf16[1024,1024]{1,0:T(8,128)(2,1)S(1)} %bitcast.165), kind=kOutput, calls=%fused_computation.20 | convolution fusion | flops 1342832640 | bytes 4718592 | tf_op jit(solution)/shard_map/dot_general | solution.py:41
  60.7 2.7 %fusion = (f32[640]{0:T(1024)S(1)}, f32[640,640]{1,0:T(8,128)S(1)}) fusion(pred[4,640]{1,0:T(4,128)(4,1)S(1)} %broadcast_in_dim.62, bf16[640,1024]{1,0:T(8,128)(2,1)S(1)} %convolution_convert_fusion.1, bf16[640,1024]{1,0:T(8,128)(2,1)} %convolution_convert_fusion), kind=kOutput, calls=%fused_computation.14 | convolution fusion | flops 840088960 | bytes 4264960 | tf_op jit(solution)/shard_map/dot_general | solution.py:41
  63.6 4.2 %fusion.1 = (f32[640]{0:T(1024)S(1)}, f32[640,640]{1,0:T(8,128)}) fusion(pred[4,640]{1,0:T(4,128)(4,1)S(1)} %broadcast_in_dim.67, bf16[640,1024]{1,0:T(8,128)(2,1)S(1)} %convolution_convert_fusion.1, bf16[640,1024]{1,0:T(8,128)(2,1)} %collective-permute-done.16), kind=kOutput, calls=%fused_computation.15 | convolution fusion | flops 840088960 | bytes 4264960 | tf_op jit(solution)/shard_map/dot_general | solution.py:41
  67.8 3.9 %fusion.12 = (f32[640]{0:T(1024)S(1)}, f32[640]{0:T(1024)S(1)}, bf16[640,640]{1,0:T(8,128)(2,1)}, bf16[640,640]{1,0:T(8,128)(2,1)}) fusion(f32[640,640]{1,0:T(8,128)} %get-tuple-element.76, f32[640]{0:T(1024)S(1)} %max.31, pred[4,640]{1,0:T(4,128)(4,1)S(1)} %broadcast_in_dim.67, f32[640,640]{1,0:T(8,128)} %copy-done.2, ...), kind=kLoop, calls=%fused_computation.32 | loop fusion | flops 4913920 | bytes 4931200 | tf_op jit(solution)/shard_map/reduce_sum | solution.py:100
  72.7 4.2 %fusion.68 = f32[640,1024]{1,0:T(8,128)} fusion(bf16[640,640]{1,0:T(8,128)(2,1)} %get-tuple-element.16, bf16[640,1024]{1,0:T(8,128)(2,1)} %convolution_convert_fusion), kind=kOutput, calls=%fused_computation.170 | convolution fusion | flops 838860800 | bytes 4751360 | tf_op jit(solution)/shard_map/dot_general | solution.py:41
  77.0 3.2 %collective-permute-start.18 = (f32[2,4,160]{2,1,0:T(4,128)S(1)}, f32[2,4,160]{2,1,0:T(4,128)S(1)}, u32[]{:S(2)}, u32[]{:S(2)}) collective-permute-start(f32[2,4,160]{2,1,0:T(4,128)S(1)} %constant_dynamic-update-slice_fusion.8), channel_id=1, source_target_pairs={{0,24},{8,0},{16,8},{24,16},{1,25},{9,1},{17,9},{25,17},{2,26},{10... | collective-permute-start | bytes 15368 | tf_op jit(solution)/shard_map/ppermute | solution.py:19
  80.3 1.3 collective-permute-done.18
  82.0 3.1 %collective-permute-done.17 = f32[2,4,160]{2,1,0:T(4,128)S(1)} collective-permute-done((f32[2,4,160]{2,1,0:T(4,128)S(1)}, f32[2,4,160]{2,1,0:T(4,128)S(1)}, u32[]{:S(2)}, u32[]{:S(2)}) %collective-permute-start.17) | collective-permute-done | bytes 5152 | tf_op jit(solution)/shard_map/ppermute | solution.py:19
  85.4 2.6 %convolution_convert_fusion.2 = bf16[640,1024]{1,0:T(8,128)(2,1)S(1)} fusion(bf16[640,640]{1,0:T(8,128)(2,1)} %get-tuple-element.15, bf16[640,1024]{1,0:T(8,128)(2,1)S(1)} %convolution_convert_fusion.1, f32[640]{0:T(1024)S(1)} %subtract_exponential_fusion), kind=kOutput, calls=%fused_computation.21 | convolution fusion | flops 841482240 | bytes 3443200 | tf_op jit(solution)/shard_map/dot_general | solution.py:41
  88.3 2.5 %fusion.66 = (bf16[640,1024]{1,0:T(8,128)(2,1)S(1)}, f32[640,1024]{1,0:T(8,128)S(1)}) fusion(f32[640,1024]{1,0:T(8,128)S(1)} %copy-done.12, bf16[640,640]{1,0:T(8,128)(2,1)S(1)} %copy-done.9, bf16[640,1024]{1,0:T(8,128)(2,1)} %collective-permute-done.16, f32[640]{0:T(1024)S(1)} %subtract_exponential_fusion), kind=kOutput, calls=%fused_computation.168 | convolution fusion | flops 840826880 | bytes 8686080 | tf_op jit(solution)/shard_map/dot_general | solution.py:41
  91.6 1.0 copy-done.8
  92.6 1.3 fusion.67
  94.1 1.6 %fusion.21 = (bf16[160,1024]{1,0:T(8,128)(2,1)S(1)}, bf16[160,1024]{1,0:T(8,128)(2,1)S(1)}) fusion(f32[640,1024]{1,0:T(8,128)S(1)} %get-tuple-element.78, f32[160]{0:T(256)S(1)} %get-tuple-element.69, bf16[640,1024]{1,0:T(8,128)(2,1)} %convolution_convert_fusion, bf16[640,1024]{1,0:T(8,128)(2,1)S(1)} %convolution_convert_fusion.1, ...), kind=kLoop, calls=%fused_computation.58 | loop fusion | flops 1310720 | bytes 2622080 | tf_op jit(solution)/shard_map/convert_element_type | solution.py:136
  96.7 1.9 %fusion.7 = f32[1024,1024]{1,0:T(8,128)S(1)} fusion(bf16[640,1024]{1,0:T(8,128)(2,1)S(1)} %copy-done.15, bf16[480,1024]{1,0:T(8,128)(2,1)S(1)} %slice.199, bf16[160,1024]{1,0:T(8,128)(2,1)S(1)} %get-tuple-element.72), kind=kOutput, calls=%fused_computation.27 | convolution fusion | flops 1344798720 | bytes 6815744 | tf_op jit(solution)/shard_map/dot_general | solution.py:41
  98.6 1.9 %convolution_add_fusion = f32[1024,1024]{1,0:T(8,128)S(1)} fusion(f32[1024,1024]{1,0:T(8,128)S(1)} %fusion.7, bf16[640,1024]{1,0:T(8,128)(2,1)S(1)} %copy-done.11, bf16[480,1024]{1,0:T(8,128)(2,1)S(1)} %slice.198, bf16[160,1024]{1,0:T(8,128)(2,1)S(1)} %get-tuple-element.71), kind=kOutput, calls=%fused_computation.13 | convolution fusion | flops 1345847296 | bytes 11010048 | tf_op jit(solution)/shard_map/dot_general | solution.py:41
  101.1 2.0 %copy-done.1 = f32[4,4,2,4,8,1024]{5,4,0,1,3,2:T(8,128)} copy-done((f32[4,4,2,4,8,1024]{5,4,0,1,3,2:T(8,128)}, f32[4,4,2,4,8,1024]{5,4,0,1,3,2:T(8,128)S(1)}, u32[]{:S(2)}) %copy-start.1) | copy-done | bytes 4194328
  103.1 1.2 fusion.13
  104.8 1.2 fusion.59
  107.0 1.2 collective-permute-start.21
  108.1 3.1 %bitcast_add_fusion = f32[4,4,4,8,1024]{4,3,2,1,0:T(8,128)S(1)} fusion(bf16[4,4,4,8,1024]{4,3,2,1,0:T(8,128)(2,1)} %collective-permute-done.27, f32[2,4,4,4,8,1024]{5,4,3,2,1,0:T(8,128)} %bitcast.162, pred[]{:T(512)S(6)} %eq.76), kind=kLoop, calls=%fused_computation.11 | loop fusion | flops 1572864 | bytes 7340033 | tf_op jit(solution)/shard_map/add | solution.py:61
  111.4 2.3 %collective-permute-start.28 = (bf16[4,4,8,1024]{3,2,1,0:T(8,128)(2,1)S(1)}, bf16[4,4,8,1024]{3,2,1,0:T(8,128)(2,1)S(1)}, u32[]{:S(2)}, u32[]{:S(2)}) collective-permute-start(bf16[4,4,8,1024]{3,2,1,0:T(8,128)(2,1)S(1)} %get-tuple-element.10), channel_id=1, source_target_pairs={{0,3},{1,0},{2,1},{3,2},{4,7},{5,4},{6,5},{7,6},{8,11},{9,8},{10,9... | collective-permute-start | bytes 786440 | tf_op jit(solution)/shard_map/ppermute | solution.py:19
  114.2 2.5 %collective-permute-done.20 = bf16[160,1024]{1,0:T(8,128)(2,1)S(1)} collective-permute-done((bf16[160,1024]{1,0:T(8,128)(2,1)S(1)}, bf16[160,1024]{1,0:T(8,128)(2,1)S(1)}, u32[]{:S(2)}, u32[]{:S(2)}) %collective-permute-start.20) | collective-permute-done | bytes 327712 | tf_op jit(solution)/shard_map/ppermute | solution.py:19
  117.4 1.3 collective-permute-done.22
  118.6 5.7 %collective-permute-done.21 = bf16[160,1024]{1,0:T(8,128)(2,1)S(1)} collective-permute-done((bf16[160,1024]{1,0:T(8,128)(2,1)S(1)}, bf16[160,1024]{1,0:T(8,128)(2,1)S(1)}, u32[]{:S(2)}, u32[]{:S(2)}) %collective-permute-start.21) | collective-permute-done | bytes 327712 | tf_op jit(solution)/shard_map/ppermute | solution.py:19
  124.4 2.9 %convolution_convert_fusion.4 = bf16[160,1024]{1,0:T(8,128)(2,1)} fusion(bf16[1024,1024]{1,0:T(8,128)(2,1)S(1)} %bitcast.166, bf16[160,1024]{1,0:T(8,128)(2,1)S(1)} %collective-permute-done.22, bf16[160,1024]{1,0:T(8,128)(2,1)S(1)} %collective-permute-done.21, bf16[160,1024]{1,0:T(8,128)(2,1)S(1)} %collective-permute-done.20, f32[640,1024]{1,0:T(8,128)} %copy-done.7, ...), kind=kOutput, calls=%fused_computation.34 | convolution fusion | flops 337510400 | bytes 4391552 | tf_op jit(solution)/shard_map/dot_general | solution.py:41
  127.3 1.1 collective-permute-done.29
  128.6 2.6 %collective-permute-start.31 = (bf16[4,8,1024]{2,1,0:T(8,128)(2,1)S(1)}, bf16[4,8,1024]{2,1,0:T(8,128)(2,1)S(1)}, u32[]{:S(2)}, u32[]{:S(2)}) collective-permute-start(bf16[4,8,1024]{2,1,0:T(8,128)(2,1)S(1)} %get-tuple-element.27), channel_id=1, source_target_pairs={{0,24},{8,0},{16,8},{24,16},{1,25},{9,1},{17,9},{25,17},{2,26},{10... | collective-permute-start | bytes 196616 | tf_op jit(solution)/shard_map/ppermute | solution.py:19
  131.2 1.2 collective-permute-start.33
  132.4 1.3 collective-permute-start.32
  134.0 1.8 %collective-permute-start.25 = (bf16[160,1024]{1,0:T(8,128)(2,1)S(1)}, bf16[160,1024]{1,0:T(8,128)(2,1)S(1)}, u32[]{:S(2)}, u32[]{:S(2)}) collective-permute-start(bf16[160,1024]{1,0:T(8,128)(2,1)S(1)} %get-tuple-element.19), channel_id=1, source_target_pairs={{0,32},{32,64},{64,96},{96,0},{1,33},{33,65},{65,97},{97,1},{2,34}... | collective-permute-start | bytes 983048 | tf_op jit(solution)/shard_map/ppermute | solution.py:19
  135.9 1.3 collective-permute-done.33
  138.0 1.3 collective-permute-start.34
  139.3 0.9 collective-permute-start.36
  140.2 4.2 %collective-permute-done.24 = bf16[160,1024]{1,0:T(8,128)(2,1)S(1)} collective-permute-done((bf16[160,1024]{1,0:T(8,128)(2,1)S(1)}, bf16[160,1024]{1,0:T(8,128)(2,1)S(1)}, u32[]{:S(2)}, u32[]{:S(2)}) %collective-permute-start.24) | collective-permute-done | bytes 327712 | tf_op jit(solution)/shard_map/ppermute | solution.py:19
  144.5 1.7 %collective-permute-done.26 = bf16[160,1024]{1,0:T(8,128)(2,1)S(1)} collective-permute-done((bf16[160,1024]{1,0:T(8,128)(2,1)S(1)}, bf16[160,1024]{1,0:T(8,128)(2,1)S(1)}, u32[]{:S(2)}, u32[]{:S(2)}) %collective-permute-start.26) | collective-permute-done | bytes 327712 | tf_op jit(solution)/shard_map/ppermute | solution.py:19
  146.2 5.2 %collective-permute-done.25 = bf16[160,1024]{1,0:T(8,128)(2,1)S(1)} collective-permute-done((bf16[160,1024]{1,0:T(8,128)(2,1)S(1)}, bf16[160,1024]{1,0:T(8,128)(2,1)S(1)}, u32[]{:S(2)}, u32[]{:S(2)}) %collective-permute-start.25) | collective-permute-done | bytes 327712 | tf_op jit(solution)/shard_map/ppermute | solution.py:19
  151.4 2.8 %convolution_convert_fusion.3 = bf16[160,1024]{1,0:T(8,128)(2,1)} fusion(bf16[1024,1024]{1,0:T(8,128)(2,1)S(1)} %bitcast.167, bf16[160,1024]{1,0:T(8,128)(2,1)S(1)} %collective-permute-done.26, bf16[160,1024]{1,0:T(8,128)(2,1)S(1)} %collective-permute-done.25, bf16[160,1024]{1,0:T(8,128)(2,1)S(1)} %collective-permute-done.24, f32[640,1024]{1,0:T(8,128)} %copy-done.6, ...), kind=kOutput, calls=%fused_computation.33 | convolution fusion | flops 337510400 | bytes 4391936 | tf_op jit(solution)/shard_map/dot_general | solution.py:41
  (135 shorter events, 15.3 us)
Async XLA Ops:
  0.6 33.9 %copy-start = (s32[128]{0:T(128)S(1)}, s32[128]{0:T(128)}, u32[]{:S(2)}) copy-start(s32[128]{0:T(128)} %param.9) | copy-start | bytes 1540
  0.6 25.6 %copy-start.13 = (bf16[160,1024]{1,0:T(8,128)(2,1)S(1)}, bf16[160,1024]{1,0:T(8,128)(2,1)}, u32[]{:S(2)}) copy-start(bf16[160,1024]{1,0:T(8,128)(2,1)} %param.6) | copy-start | bytes 983044
  0.7 6.1 %collective-permute-start.3 = (bf16[8,1024]{1,0:T(8,128)(2,1)}, bf16[8,1024]{1,0:T(8,128)(2,1)S(1)}, u32[]{:S(2)}, u32[]{:S(2)}) collective-permute-start(bf16[8,1024]{1,0:T(8,128)(2,1)} %param.7), channel_id=1, source_target_pairs={{0,96},{32,0},{64,32},{96,64},{1,97},{33,1},{65,33},{97,65},{2,98}... | collective-permute-start | bytes 49160 | tf_op jit(solution)/shard_map/ppermute | solution.py:19
  4.8 5.2 %collective-permute-start.5 = (bf16[8,1024]{1,0:T(8,128)(2,1)}, bf16[8,1024]{1,0:T(8,128)(2,1)S(1)}, u32[]{:S(2)}, u32[]{:S(2)}) collective-permute-start(bf16[8,1024]{1,0:T(8,128)(2,1)} %param.7), channel_id=1, source_target_pairs={{0,32},{32,64},{64,96},{96,0},{1,33},{33,65},{65,97},{97,1},{2,34}... | collective-permute-start | bytes 49160 | tf_op jit(solution)/shard_map/ppermute | solution.py:19
  4.8 5.5 %collective-permute-start.4 = (bf16[8,1024]{1,0:T(8,128)(2,1)}, bf16[8,1024]{1,0:T(8,128)(2,1)S(1)}, u32[]{:S(2)}, u32[]{:S(2)}) collective-permute-start(bf16[8,1024]{1,0:T(8,128)(2,1)} %param.7), channel_id=1, source_target_pairs={{0,64},{32,96},{64,0},{96,32},{1,65},{33,97},{65,1},{97,33},{2,66}... | collective-permute-start | bytes 49160 | tf_op jit(solution)/shard_map/ppermute | solution.py:19
  11.1 5.9 %collective-permute-start.7 = (bf16[4,8,1024]{2,1,0:T(8,128)(2,1)S(1)}, bf16[4,8,1024]{2,1,0:T(8,128)(2,1)S(1)}, u32[]{:S(2)}, u32[]{:S(2)}) collective-permute-start(bf16[4,8,1024]{2,1,0:T(8,128)(2,1)S(1)} %get-tuple-element.40), channel_id=1, source_target_pairs={{0,16},{8,24},{16,0},{24,8},{1,17},{9,25},{17,1},{25,9},{2,18},{10... | collective-permute-start | bytes 196616 | tf_op jit(solution)/shard_map/ppermute | solution.py:19
  14.2 4.3 %collective-permute-start.6 = (bf16[4,8,1024]{2,1,0:T(8,128)(2,1)S(1)}, bf16[4,8,1024]{2,1,0:T(8,128)(2,1)S(1)}, u32[]{:S(2)}, u32[]{:S(2)}) collective-permute-start(bf16[4,8,1024]{2,1,0:T(8,128)(2,1)S(1)} %get-tuple-element.40), channel_id=1, source_target_pairs={{0,24},{8,0},{16,8},{24,16},{1,25},{9,1},{17,9},{25,17},{2,26},{10... | collective-permute-start | bytes 196616 | tf_op jit(solution)/shard_map/ppermute | solution.py:19
  15.3 5.5 %collective-permute-start.8 = (bf16[4,8,1024]{2,1,0:T(8,128)(2,1)S(1)}, bf16[4,8,1024]{2,1,0:T(8,128)(2,1)S(1)}, u32[]{:S(2)}, u32[]{:S(2)}) collective-permute-start(bf16[4,8,1024]{2,1,0:T(8,128)(2,1)S(1)} %get-tuple-element.40), channel_id=1, source_target_pairs={{0,8},{8,16},{16,24},{24,0},{1,9},{9,17},{17,25},{25,1},{2,10},{10... | collective-permute-start | bytes 196616 | tf_op jit(solution)/shard_map/ppermute | solution.py:19
  20.9 9.4 %collective-permute-start.10 = (bf16[4,4,8,1024]{3,2,0,1:T(8,128)(2,1)S(1)}, bf16[4,4,8,1024]{3,2,0,1:T(8,128)(2,1)S(1)}, u32[]{:S(2)}, u32[]{:S(2)}) collective-permute-start(bf16[4,4,8,1024]{3,2,0,1:T(8,128)(2,1)S(1)} %get-tuple-element.31), channel_id=1, source_target_pairs={{0,2},{1,3},{2,0},{3,1},{4,6},{5,7},{6,4},{7,5},{8,10},{9,11},{10,... | collective-permute-start | bytes 786440 | tf_op jit(solution)/shard_map/ppermute | solution.py:19
  24.2 9.3 %collective-permute-start.9 = (bf16[4,4,8,1024]{3,2,0,1:T(8,128)(2,1)S(1)}, bf16[4,4,8,1024]{3,2,0,1:T(8,128)(2,1)S(1)}, u32[]{:S(2)}, u32[]{:S(2)}) collective-permute-start(bf16[4,4,8,1024]{3,2,0,1:T(8,128)(2,1)S(1)} %get-tuple-element.31), channel_id=1, source_target_pairs={{0,3},{1,0},{2,1},{3,2},{4,7},{5,4},{6,5},{7,6},{8,11},{9,8},{10,9... | collective-permute-start | bytes 786440 | tf_op jit(solution)/shard_map/ppermute | solution.py:19
  25.3 8.5 %collective-permute-start.11 = (bf16[4,4,8,1024]{3,2,0,1:T(8,128)(2,1)S(1)}, bf16[4,4,8,1024]{3,2,0,1:T(8,128)(2,1)S(1)}, u32[]{:S(2)}, u32[]{:S(2)}) collective-permute-start(bf16[4,4,8,1024]{3,2,0,1:T(8,128)(2,1)S(1)} %get-tuple-element.31), channel_id=1, source_target_pairs={{0,1},{1,2},{2,3},{3,0},{4,5},{5,6},{6,7},{7,4},{8,9},{9,10},{10,1... | collective-permute-start | bytes 786440 | tf_op jit(solution)/shard_map/ppermute | solution.py:19
  26.2 17.7 %collective-permute-start.14 = (bf16[160,1024]{1,0:T(8,128)(2,1)S(1)}, bf16[160,1024]{1,0:T(8,128)(2,1)}, u32[]{:S(2)}, u32[]{:S(2)}) collective-permute-start(bf16[160,1024]{1,0:T(8,128)(2,1)S(1)} %copy-done.13), channel_id=1, source_target_pairs={{0,96},{32,0},{64,32},{96,64},{1,97},{33,1},{65,33},{97,65},{2,98}... | collective-permute-start | bytes 983048 | tf_op jit(solution)/shard_map/ppermute | solution.py:19
  29.5 13.5 %collective-permute-start.13 = (bf16[160,1024]{1,0:T(8,128)(2,1)S(1)}, bf16[160,1024]{1,0:T(8,128)(2,1)}, u32[]{:S(2)}, u32[]{:S(2)}) collective-permute-start(bf16[160,1024]{1,0:T(8,128)(2,1)S(1)} %copy-done.13), channel_id=1, source_target_pairs={{0,32},{32,64},{64,96},{96,0},{1,33},{33,65},{65,97},{97,1},{2,34}... | collective-permute-start | bytes 983048 | tf_op jit(solution)/shard_map/ppermute | solution.py:19
  30.3 16.2 %collective-permute-start.15 = (bf16[160,1024]{1,0:T(8,128)(2,1)S(1)}, bf16[160,1024]{1,0:T(8,128)(2,1)}, u32[]{:S(2)}, u32[]{:S(2)}) collective-permute-start(bf16[160,1024]{1,0:T(8,128)(2,1)S(1)} %copy-done.13), channel_id=1, source_target_pairs={{0,64},{32,96},{64,0},{96,32},{1,65},{33,97},{65,1},{97,33},{2,66}... | collective-permute-start | bytes 983048 | tf_op jit(solution)/shard_map/ppermute | solution.py:19
  33.5 22.6 %collective-permute-start.1 = (bf16[160,1024]{1,0:T(8,128)(2,1)}, bf16[160,1024]{1,0:T(8,128)(2,1)}, u32[]{:S(2)}, u32[]{:S(2)}) collective-permute-start(bf16[160,1024]{1,0:T(8,128)(2,1)} %param.5), channel_id=1, source_target_pairs={{0,24},{8,0},{16,8},{24,16},{1,25},{9,1},{17,9},{25,17},{2,26},{10... | collective-permute-start | bytes 983048 | tf_op jit(solution)/shard_map/ppermute | solution.py:19
  34.1 13.4 %collective-permute-start.12 = (bf16[4,4,4,8,1024]{4,3,0,1,2:T(8,128)(2,1)S(1)}, bf16[4,4,4,8,1024]{4,3,0,1,2:T(8,128)(2,1)S(1)}, u32[]{:S(2)}, u32[]{:S(2)}) collective-permute-start(bf16[4,4,4,8,1024]{4,3,0,1,2:T(8,128)(2,1)S(1)} %pad_maximum_fusion.2), channel_id=1, source_target_pairs={{0,4},{4,0},{1,5},{5,1},{2,6},{6,2},{3,7},{7,3},{8,12},{12,8},{9,1... | collective-permute-start | bytes 3145736 | tf_op jit(solution)/shard_map/ppermute | solution.py:19
  43.0 12.1 %collective-permute-start = (bf16[160,1024]{1,0:T(8,128)(2,1)}, bf16[160,1024]{1,0:T(8,128)(2,1)}, u32[]{:S(2)}, u32[]{:S(2)}) collective-permute-start(bf16[160,1024]{1,0:T(8,128)(2,1)} %param.5), channel_id=1, source_target_pairs={{0,8},{8,16},{16,24},{24,0},{1,9},{9,17},{17,25},{25,1},{2,10},{10... | collective-permute-start | bytes 983048 | tf_op jit(solution)/shard_map/ppermute | solution.py:19
  44.0 13.1 %collective-permute-start.2 = (bf16[160,1024]{1,0:T(8,128)(2,1)}, bf16[160,1024]{1,0:T(8,128)(2,1)}, u32[]{:S(2)}, u32[]{:S(2)}) collective-permute-start(bf16[160,1024]{1,0:T(8,128)(2,1)} %param.5), channel_id=1, source_target_pairs={{0,16},{8,24},{16,0},{24,8},{1,17},{9,25},{17,1},{25,9},{2,18},{10... | collective-permute-start | bytes 983048 | tf_op jit(solution)/shard_map/ppermute | solution.py:19
  47.6 1.1 copy-start.14
  48.7 2.7 %copy-start.16 = (s32[128,32]{0,1:T(8,128)S(1)}, s32[128,32]{0,1:T(8,128)}, u32[]{:S(2)}) copy-start(s32[128,32]{0,1:T(8,128)} %param.8) | copy-start | bytes 49156
  51.3 12.3 %collective-permute-start.16 = (bf16[640,1024]{1,0:T(8,128)(2,1)}, bf16[640,1024]{1,0:T(8,128)(2,1)}, u32[]{:S(2)}, u32[]{:S(2)}) collective-permute-start(bf16[640,1024]{1,0:T(8,128)(2,1)} %convolution_convert_fusion), channel_id=1, source_target_pairs={{0,4},{4,0},{1,5},{5,1},{2,6},{6,2},{3,7},{7,3},{8,12},{12,8},{9,1... | collective-permute-start | bytes 3932168 | tf_op jit(solution)/shard_map/ppermute | solution.py:19
  58.1 1.1 copy-start.10
  63.4 4.4 %copy-start.2 = (f32[640,640]{1,0:T(8,128)}, f32[640,640]{1,0:T(8,128)S(1)}, u32[]{:S(2)}) copy-start(f32[640,640]{1,0:T(8,128)S(1)} %get-tuple-element.74) | copy-start | bytes 4915204
  71.9 8.4 %collective-permute-start.19 = (f32[2,4,160]{2,1,0:T(4,128)S(1)}, f32[2,4,160]{2,1,0:T(4,128)S(1)}, u32[]{:S(2)}, u32[]{:S(2)}) collective-permute-start(f32[2,4,160]{2,1,0:T(4,128)S(1)} %constant_dynamic-update-slice_fusion.8), channel_id=1, source_target_pairs={{0,16},{8,24},{16,0},{24,8},{1,17},{9,25},{17,1},{25,9},{2,18},{10... | collective-permute-start | bytes 15368 | tf_op jit(solution)/shard_map/ppermute | solution.py:19
  77.0 4.6 %collective-permute-start.18 = (f32[2,4,160]{2,1,0:T(4,128)S(1)}, f32[2,4,160]{2,1,0:T(4,128)S(1)}, u32[]{:S(2)}, u32[]{:S(2)}) collective-permute-start(f32[2,4,160]{2,1,0:T(4,128)S(1)} %constant_dynamic-update-slice_fusion.8), channel_id=1, source_target_pairs={{0,24},{8,0},{16,8},{24,16},{1,25},{9,1},{17,9},{25,17},{2,26},{10... | collective-permute-start | bytes 15368 | tf_op jit(solution)/shard_map/ppermute | solution.py:19
  80.3 4.9 %collective-permute-start.17 = (f32[2,4,160]{2,1,0:T(4,128)S(1)}, f32[2,4,160]{2,1,0:T(4,128)S(1)}, u32[]{:S(2)}, u32[]{:S(2)}) collective-permute-start(f32[2,4,160]{2,1,0:T(4,128)S(1)} %constant_dynamic-update-slice_fusion.8), channel_id=1, source_target_pairs={{0,8},{8,16},{16,24},{24,0},{1,9},{9,17},{17,25},{25,1},{2,10},{10... | collective-permute-start | bytes 15368 | tf_op jit(solution)/shard_map/ppermute | solution.py:19
  85.4 2.9 %copy-start.9 = (bf16[640,640]{1,0:T(8,128)(2,1)S(1)}, bf16[640,640]{1,0:T(8,128)(2,1)}, u32[]{:S(2)}) copy-start(bf16[640,640]{1,0:T(8,128)(2,1)} %get-tuple-element.15) | copy-start | bytes 2457604
  85.4 2.9 %copy-start.12 = (f32[640,1024]{1,0:T(8,128)S(1)}, f32[640,1024]{1,0:T(8,128)}, u32[]{:S(2)}) copy-start(f32[640,1024]{1,0:T(8,128)} %fusion.68) | copy-start | bytes 7864324
  88.0 3.6 %collective-permute-start.23 = (bf16[640,1024]{1,0:T(8,128)(2,1)S(1)}, bf16[640,1024]{1,0:T(8,128)(2,1)S(1)}, u32[]{:S(2)}, u32[]{:S(2)}) collective-permute-start(bf16[640,1024]{1,0:T(8,128)(2,1)S(1)} %convolution_convert_fusion.2), channel_id=1, source_target_pairs={{0,4},{4,0},{1,5},{5,1},{2,6},{6,2},{3,7},{7,3},{8,12},{12,8},{9,1... | collective-permute-start | bytes 3932168 | tf_op jit(solution)/shard_map/ppermute | solution.py:19
  90.9 3.1 %copy-start.5 = (bf16[640,1024]{1,0:T(8,128)(2,1)}, bf16[640,1024]{1,0:T(8,128)(2,1)S(1)}, u32[]{:S(2)}) copy-start(bf16[640,1024]{1,0:T(8,128)(2,1)S(1)} %get-tuple-element.77) | copy-start | bytes 3932164
  90.9 3.2 %copy-start.7 = (f32[640,1024]{1,0:T(8,128)}, f32[640,1024]{1,0:T(8,128)S(1)}, u32[]{:S(2)}) copy-start(f32[640,1024]{1,0:T(8,128)S(1)} %get-tuple-element.78) | copy-start | bytes 7864324
  90.9 1.8 %copy-start.8 = (bf16[640,640]{1,0:T(8,128)(2,1)S(1)}, bf16[640,640]{1,0:T(8,128)(2,1)}, u32[]{:S(2)}) copy-start(bf16[640,640]{1,0:T(8,128)(2,1)} %get-tuple-element.16) | copy-start | bytes 2457604
  94.0 1.7 %copy-start.3 = (bf16[640,1024]{1,0:T(8,128)(2,1)}, bf16[640,1024]{1,0:T(8,128)(2,1)S(1)}, u32[]{:S(2)}) copy-start(bf16[640,1024]{1,0:T(8,128)(2,1)S(1)} %get-tuple-element.79) | copy-start | bytes 3932164
  94.0 1.9 %copy-start.6 = (f32[640,1024]{1,0:T(8,128)}, f32[640,1024]{1,0:T(8,128)S(1)}, u32[]{:S(2)}) copy-start(f32[640,1024]{1,0:T(8,128)S(1)} %get-tuple-element.80) | copy-start | bytes 7864324
  94.0 2.6 %copy-start.15 = (bf16[640,1024]{1,0:T(8,128)(2,1)S(1)}, bf16[640,1024]{1,0:T(8,128)(2,1)}, u32[]{:S(2)}) copy-start(bf16[640,1024]{1,0:T(8,128)(2,1)} %copy-done.14) | copy-start | bytes 3932164
  96.7 1.9 %copy-start.11 = (bf16[640,1024]{1,0:T(8,128)(2,1)S(1)}, bf16[640,1024]{1,0:T(8,128)(2,1)}, u32[]{:S(2)}) copy-start(bf16[640,1024]{1,0:T(8,128)(2,1)} %copy-done.10) | copy-start | bytes 3932164
  101.1 2.0 %copy-start.1 = (f32[4,4,2,4,8,1024]{5,4,0,1,3,2:T(8,128)}, f32[4,4,2,4,8,1024]{5,4,0,1,3,2:T(8,128)S(1)}, u32[]{:S(2)}) copy-start(f32[4,4,2,4,8,1024]{5,4,0,1,3,2:T(8,128)S(1)} %copy.34) | copy-start | bytes 12582916
  104.3 3.8 %collective-permute-start.27 = (bf16[4,4,4,8,1024]{4,3,2,1,0:T(8,128)(2,1)}, bf16[4,4,4,8,1024]{4,3,2,1,0:T(8,128)(2,1)}, u32[]{:S(2)}, u32[]{:S(2)}) collective-permute-start(bf16[4,4,4,8,1024]{4,3,2,1,0:T(8,128)(2,1)} %fusion.13), channel_id=1, source_target_pairs={{0,4},{4,0},{1,5},{5,1},{2,6},{6,2},{3,7},{7,3},{8,12},{12,8},{9,1... | collective-permute-start | bytes 3145736 | tf_op jit(solution)/shard_map/ppermute | solution.py:19
  106.0 10.6 %collective-permute-start.20 = (bf16[160,1024]{1,0:T(8,128)(2,1)S(1)}, bf16[160,1024]{1,0:T(8,128)(2,1)S(1)}, u32[]{:S(2)}, u32[]{:S(2)}) collective-permute-start(bf16[160,1024]{1,0:T(8,128)(2,1)S(1)} %get-tuple-element.20), channel_id=1, source_target_pairs={{0,24},{8,0},{16,8},{24,16},{1,25},{9,1},{17,9},{25,17},{2,26},{10... | collective-permute-start | bytes 983048 | tf_op jit(solution)/shard_map/ppermute | solution.py:19
  106.5 12.2 %collective-permute-start.22 = (bf16[160,1024]{1,0:T(8,128)(2,1)S(1)}, bf16[160,1024]{1,0:T(8,128)(2,1)S(1)}, u32[]{:S(2)}, u32[]{:S(2)}) collective-permute-start(bf16[160,1024]{1,0:T(8,128)(2,1)S(1)} %get-tuple-element.21), channel_id=1, source_target_pairs={{0,16},{8,24},{16,0},{24,8},{1,17},{9,25},{17,1},{25,9},{2,18},{10... | collective-permute-start | bytes 983048 | tf_op jit(solution)/shard_map/ppermute | solution.py:19
  107.0 17.4 %collective-permute-start.21 = (bf16[160,1024]{1,0:T(8,128)(2,1)S(1)}, bf16[160,1024]{1,0:T(8,128)(2,1)S(1)}, u32[]{:S(2)}, u32[]{:S(2)}) collective-permute-start(bf16[160,1024]{1,0:T(8,128)(2,1)S(1)} %get-tuple-element.22), channel_id=1, source_target_pairs={{0,8},{8,16},{16,24},{24,0},{1,9},{9,17},{17,25},{25,1},{2,10},{10... | collective-permute-start | bytes 983048 | tf_op jit(solution)/shard_map/ppermute | solution.py:19
  111.4 15.9 %collective-permute-start.28 = (bf16[4,4,8,1024]{3,2,1,0:T(8,128)(2,1)S(1)}, bf16[4,4,8,1024]{3,2,1,0:T(8,128)(2,1)S(1)}, u32[]{:S(2)}, u32[]{:S(2)}) collective-permute-start(bf16[4,4,8,1024]{3,2,1,0:T(8,128)(2,1)S(1)} %get-tuple-element.10), channel_id=1, source_target_pairs={{0,3},{1,0},{2,1},{3,2},{4,7},{5,4},{6,5},{7,6},{8,11},{9,8},{10,9... | collective-permute-start | bytes 786440 | tf_op jit(solution)/shard_map/ppermute | solution.py:19
  113.7 13.6 %collective-permute-start.30 = (bf16[4,4,8,1024]{3,2,1,0:T(8,128)(2,1)S(1)}, bf16[4,4,8,1024]{3,2,1,0:T(8,128)(2,1)S(1)}, u32[]{:S(2)}, u32[]{:S(2)}) collective-permute-start(bf16[4,4,8,1024]{3,2,1,0:T(8,128)(2,1)S(1)} %get-tuple-element.11), channel_id=1, source_target_pairs={{0,2},{1,3},{2,0},{3,1},{4,6},{5,7},{6,4},{7,5},{8,10},{9,11},{10,... | collective-permute-start | bytes 786440 | tf_op jit(solution)/shard_map/ppermute | solution.py:19
  116.7 11.8 %collective-permute-start.29 = (bf16[4,4,8,1024]{3,2,1,0:T(8,128)(2,1)S(1)}, bf16[4,4,8,1024]{3,2,1,0:T(8,128)(2,1)S(1)}, u32[]{:S(2)}, u32[]{:S(2)}) collective-permute-start(bf16[4,4,8,1024]{3,2,1,0:T(8,128)(2,1)S(1)} %get-tuple-element.12), channel_id=1, source_target_pairs={{0,1},{1,2},{2,3},{3,0},{4,5},{5,6},{6,7},{7,4},{8,9},{9,10},{10,1... | collective-permute-start | bytes 786440 | tf_op jit(solution)/shard_map/ppermute | solution.py:19
  127.3 6.4 %copy-start.4 = (bf16[640,1024]{1,0:T(8,128)(2,1)S(1)}, bf16[640,1024]{1,0:T(8,128)(2,1)}, u32[]{:S(2)}) copy-start(bf16[640,1024]{1,0:T(8,128)(2,1)} %copy-done.3) | copy-start | bytes 3932164
  128.6 5.4 %collective-permute-start.31 = (bf16[4,8,1024]{2,1,0:T(8,128)(2,1)S(1)}, bf16[4,8,1024]{2,1,0:T(8,128)(2,1)S(1)}, u32[]{:S(2)}, u32[]{:S(2)}) collective-permute-start(bf16[4,8,1024]{2,1,0:T(8,128)(2,1)S(1)} %get-tuple-element.27), channel_id=1, source_target_pairs={{0,24},{8,0},{16,8},{24,16},{1,25},{9,1},{17,9},{25,17},{2,26},{10... | collective-permute-start | bytes 196616 | tf_op jit(solution)/shard_map/ppermute | solution.py:19
  131.2 6.0 %collective-permute-start.33 = (bf16[4,8,1024]{2,1,0:T(8,128)(2,1)S(1)}, bf16[4,8,1024]{2,1,0:T(8,128)(2,1)S(1)}, u32[]{:S(2)}, u32[]{:S(2)}) collective-permute-start(bf16[4,8,1024]{2,1,0:T(8,128)(2,1)S(1)} %get-tuple-element.28), channel_id=1, source_target_pairs={{0,16},{8,24},{16,0},{24,8},{1,17},{9,25},{17,1},{25,9},{2,18},{10... | collective-permute-start | bytes 196616 | tf_op jit(solution)/shard_map/ppermute | solution.py:19
  132.4 5.5 %collective-permute-start.32 = (bf16[4,8,1024]{2,1,0:T(8,128)(2,1)S(1)}, bf16[4,8,1024]{2,1,0:T(8,128)(2,1)S(1)}, u32[]{:S(2)}, u32[]{:S(2)}) collective-permute-start(bf16[4,8,1024]{2,1,0:T(8,128)(2,1)S(1)} %get-tuple-element.29), channel_id=1, source_target_pairs={{0,8},{8,16},{16,24},{24,0},{1,9},{9,17},{17,25},{25,1},{2,10},{10... | collective-permute-start | bytes 196616 | tf_op jit(solution)/shard_map/ppermute | solution.py:19
  133.8 10.7 %collective-permute-start.24 = (bf16[160,1024]{1,0:T(8,128)(2,1)S(1)}, bf16[160,1024]{1,0:T(8,128)(2,1)S(1)}, u32[]{:S(2)}, u32[]{:S(2)}) collective-permute-start(bf16[160,1024]{1,0:T(8,128)(2,1)S(1)} %get-tuple-element.17), channel_id=1, source_target_pairs={{0,96},{32,0},{64,32},{96,64},{1,97},{33,1},{65,33},{97,65},{2,98}... | collective-permute-start | bytes 983048 | tf_op jit(solution)/shard_map/ppermute | solution.py:19
  134.0 12.2 %collective-permute-start.26 = (bf16[160,1024]{1,0:T(8,128)(2,1)S(1)}, bf16[160,1024]{1,0:T(8,128)(2,1)S(1)}, u32[]{:S(2)}, u32[]{:S(2)}) collective-permute-start(bf16[160,1024]{1,0:T(8,128)(2,1)S(1)} %get-tuple-element.18), channel_id=1, source_target_pairs={{0,64},{32,96},{64,0},{96,32},{1,65},{33,97},{65,1},{97,33},{2,66}... | collective-permute-start | bytes 983048 | tf_op jit(solution)/shard_map/ppermute | solution.py:19
  134.0 17.4 %collective-permute-start.25 = (bf16[160,1024]{1,0:T(8,128)(2,1)S(1)}, bf16[160,1024]{1,0:T(8,128)(2,1)S(1)}, u32[]{:S(2)}, u32[]{:S(2)}) collective-permute-start(bf16[160,1024]{1,0:T(8,128)(2,1)S(1)} %get-tuple-element.19), channel_id=1, source_target_pairs={{0,32},{32,64},{64,96},{96,0},{1,33},{33,65},{65,97},{97,1},{2,34}... | collective-permute-start | bytes 983048 | tf_op jit(solution)/shard_map/ppermute | solution.py:19
  138.0 16.2 %collective-permute-start.34 = (bf16[8,1024]{1,0:T(8,128)(2,1)S(1)}, bf16[8,1024]{1,0:T(8,128)(2,1)S(1)}, u32[]{:S(2)}, u32[]{:S(2)}) collective-permute-start(bf16[8,1024]{1,0:T(8,128)(2,1)S(1)} %get-tuple-element.36), channel_id=1, source_target_pairs={{0,96},{32,0},{64,32},{96,64},{1,97},{33,1},{65,33},{97,65},{2,98}... | collective-permute-start | bytes 49160 | tf_op jit(solution)/shard_map/ppermute | solution.py:19
  139.3 14.9 %collective-permute-start.36 = (bf16[8,1024]{1,0:T(8,128)(2,1)S(1)}, bf16[8,1024]{1,0:T(8,128)(2,1)S(1)}, u32[]{:S(2)}, u32[]{:S(2)}) collective-permute-start(bf16[8,1024]{1,0:T(8,128)(2,1)S(1)} %get-tuple-element.37), channel_id=1, source_target_pairs={{0,64},{32,96},{64,0},{96,32},{1,65},{33,97},{65,1},{97,33},{2,66}... | collective-permute-start | bytes 49160 | tf_op jit(solution)/shard_map/ppermute | solution.py:19
  144.5 9.7 %collective-permute-start.35 = (bf16[8,1024]{1,0:T(8,128)(2,1)S(1)}, bf16[8,1024]{1,0:T(8,128)(2,1)S(1)}, u32[]{:S(2)}, u32[]{:S(2)}) collective-permute-start(bf16[8,1024]{1,0:T(8,128)(2,1)S(1)} %get-tuple-element.38), channel_id=1, source_target_pairs={{0,32},{32,64},{64,96},{96,0},{1,33},{33,65},{65,97},{97,1},{2,34}... | collective-permute-start | bytes 49160 | tf_op jit(solution)/shard_map/ppermute | solution.py:19

commit v2 on v1

v2 whole, which is shorter than its diff:
```python
import math

import jax
import jax.numpy as jnp
from jax import lax
from jax.experimental import pallas as pl
from jax.experimental.pallas import tpu as pltpu
from jax.sharding import Mesh, PartitionSpec as P

SIZES = {"z": 4, "x": 4, "c": 2, "y": 4}
AXES = ("z", "x", "c", "y")
OFFSETS = (0, -1, 1, 2)
BF16 = jnp.bfloat16
F32 = jnp.float32
LAST = (((1,), (1,)), ((), ()))
FIRST = (((0,), (0,)), ((), ()))


def swap(value):
    return lax.ppermute(value, "c", [(0, 1), (1, 0)])


def shift(value, axis, step):
    names = tuple(a for a in AXES if a in (axis, "c"))
    spots = {(i, c): 4 * c + i if axis == "y" else 2 * i + c for i in range(4) for c in range(2)}
    pairs = [(spots[i, c], spots[(i + (step, -step)[c]) % 4, c]) for i, c in spots]
    return lax.ppermute(value, names, pairs)


def collect(value, axis):
    before, after = shift(value, axis, 1), shift(value, axis, -1)
    return [value, before, after, shift(before, axis, 1)]


def place(offset):
    return OFFSETS.index((offset + 1) % 4 - 1)


def dot(a, b, dims=(((1,), (0,)), ((), ()))):
    return lax.dot_general(a, b, dims, preferred_element_type=F32)


def gather_all(weight, queries, passages):
    rows, width = weight.shape
    ring = [shift(queries, "x", 1), shift(queries, "x", -1), shift(passages, "z", 1), shift(passages, "z", -1)]
    part = lax.all_to_all(jnp.broadcast_to(weight, (16, rows, width)), ("z", "x"), 0, 0)
    part, *ring = lax.optimization_barrier((part, *ring))
    before, after = shift(part, "y", 1), shift(part, "y", -1)
    last = [shift(ring[0], "x", 1), shift(ring[2], "z", 1)]
    before, *last = lax.optimization_barrier((before, *last))
    far = shift(before, "y", 1)
    query_blocks = [queries, *ring[:2], last[0]]
    passage_blocks = [passages, *ring[2:], last[1]]
    swapped = [swap(block) for block in passage_blocks]
    far, *swapped = lax.optimization_barrier((far, *swapped))
    passage_blocks += swapped
    near = jnp.stack([part, after, before])
    near, far = (near, swap(near)), (far, swap(far))
    c, y = lax.axis_index("c"), lax.axis_index("y")
    pieces = []
    for core in range(2):
        near_one = jnp.where(c == core, near[0], near[1])
        stacked = jnp.stack([near_one[0], near_one[1], jnp.where(c == core, far[0], far[1]), near_one[2]])
        spots = [((1 - 2 * core) * (i - y)) % 4 for i in range(4)]
        pieces.append(jnp.stack([lax.dynamic_index_in_dim(stacked, spot, 0, keepdims=False) for spot in spots], axis=1))
    return jnp.stack(pieces, axis=1).reshape(-1, width), query_blocks, passage_blocks


def score_kernel(*refs):
    blocks, weight, live, raw, emb, probs, stats, own_score, scores = refs[:12], *refs[12:]
    rows, width = blocks[0].shape
    part = 4 * rows
    for i, ref in enumerate(blocks):
        raw[pl.ds(i * rows, rows), :] = ref[...]
    for i in range(3):
        for j in range(4):
            cols = pl.ds(j * width // 4, width // 4)
            emb[pl.ds(i * part, part), cols] = dot(raw[pl.ds(i * part, part), :], weight[:, cols]).astype(BF16)
    query_emb = emb[pl.ds(0, part), :]
    scale = 1.0 / math.sqrt(width)
    top = jnp.full((1, part), -1e30, F32)
    for i in range(4):
        piece = scale * dot(emb[pl.ds(part + 2 * i * rows, 2 * rows), :], query_emb, LAST)
        scores[pl.ds(2 * i * rows, 2 * rows), :] = piece
        for j in range(2):
            best = jnp.max(piece[j * rows : (j + 1) * rows], axis=0, keepdims=True)
            top = jnp.maximum(top, jnp.where(live[pl.ds(2 * i + j, 1), :] > 0.0, best, -1e30))
    total = jnp.zeros((1, part), F32)
    stats[...] = jnp.zeros_like(stats)
    own_score[...] = jnp.zeros_like(own_score)
    for i in range(8):
        base = jnp.where(live[pl.ds(i, 1), :] > 0.0, top, 1e30)
        piece = scores[pl.ds(i * rows, rows), :]
        prob = jnp.exp(piece - base)
        total = total + jnp.sum(prob, axis=0, keepdims=True)
        if i == 0:
            own = lax.broadcasted_iota(jnp.int32, prob.shape, 0) == lax.broadcasted_iota(jnp.int32, prob.shape, 1)
            prob = jnp.where(own, 0.0, prob)
            own_score[pl.ds(0, 1), :rows] = jnp.sum(jnp.where(own, piece, 0.0), axis=0, keepdims=True)[:, :rows]
        probs[pl.ds(i * rows, rows), :] = prob.astype(BF16)
    for i in range(4):
        stats[pl.ds(i, 1), :rows] = top[:, i * rows : (i + 1) * rows]
        stats[pl.ds(4 + i, 1), :rows] = total[:, i * rows : (i + 1) * rows]


def grad_kernel(
    core, here, before, after, opposite, own_score, raw, emb, probs, query_sum,
    losses, query_own, query_back, query_next, query_ahead, passage_own, passage_back, passage_next, passage_ahead,
    passage_other, mine, theirs, scaled, parts,
):
    rows, width = query_own.shape
    part = 4 * rows
    came = (here, before, after, opposite)
    columns = []
    for block in OFFSETS:
        tops = [s[pl.ds(place(block - sender), 1), :] for s, sender in zip(came, OFFSETS)]
        sums = [s[pl.ds(4 + place(block - sender), 1), :] for s, sender in zip(came, OFFSETS)]
        top = jnp.maximum(jnp.maximum(tops[0], tops[1]), jnp.maximum(tops[2], tops[3]))
        log_total = top + jnp.log(sum(s * jnp.exp(t - top) for s, t in zip(sums, tops)))
        columns.append(jnp.exp(tops[0] - log_total))
        if block == 0:
            loss = log_total - own_score[pl.ds(0, 1), :]
    columns.append(jnp.exp(-loss) - 1.0)
    losses[...] = jnp.broadcast_to(loss, losses.shape)
    columns = jnp.concatenate(columns + [jnp.zeros_like(loss)] * 3, axis=0).T
    factors = [columns[:rows, i : i + 1] for i in range(4)]
    own_factor = columns[:rows, 4:5]

    for i in range(4):
        span = pl.ds(i * rows, rows)
        scaled[span, :] = (emb[span, :].astype(F32) * factors[i]).astype(BF16)
    other = dot(probs[pl.ds(part, part), :], scaled[...]).astype(BF16)
    passage_other[...] = other
    parts[pl.ds(2 * part, part), :] = other
    for i, out in enumerate((query_own, query_back, query_next, query_ahead)):
        span = pl.ds(i * rows, rows)
        value = query_sum[span, :] * factors[i]
        if i == 0:
            value = value + own_factor * emb[pl.ds(part, rows), :].astype(F32)
        out[...] = value.astype(out.dtype)
        parts[span, :] = value.astype(BF16)
    for i, out in enumerate((passage_own, passage_back, passage_next, passage_ahead)):
        value = dot(probs[pl.ds(i * rows, rows), :], scaled[...])
        if i == 0:
            value = value + own_factor * emb[pl.ds(0, rows), :].astype(F32)
        out[...] = value.astype(out.dtype)
        parts[pl.ds(part + i * rows, rows), :] = value.astype(BF16)
    first = core[0] == 0
    for i in range(4):
        total = dot(raw[:, pl.ds(i * width // 4, width // 4)], parts[...], FIRST)
        for j in range(width // 256):
            low, high = total[64 * j : 64 * j + 32], total[64 * j + 32 : 64 * j + 64]
            span = pl.ds((i * (width // 256) + j) * 32, 32)
            mine[span, :] = jnp.where(first, low, high)
            theirs[span, :] = jnp.where(first, high, low).astype(BF16)


def local(queries, passages, weight, block_list, list_len):
    rows, width = queries.shape
    scale = 1.0 / math.sqrt(width)
    z, x, c, y = (lax.axis_index(a) for a in AXES)
    way = 1 - 2 * c

    full_weight, query_blocks, passage_blocks = gather_all(weight, queries, passages)

    owners = jnp.stack([(z * 4 + (x + way * o) % 4) * 2 + c for o in OFFSETS])
    lists = block_list[owners * 4 + y]
    lens = list_len[owners * 4 + y]
    blocks = jnp.stack(
        [((z + d * o) % 4 * 4 + x) * 2 + core for core, d in ((c, way), (1 - c, -way)) for o in OFFSETS]
    )
    live = jnp.arange(lists.shape[1])[None, :] < lens[:, None]
    hit = jnp.any((lists[None, :, :] == blocks[:, None, None]) & live[None, :, :], axis=2)
    hit = jnp.repeat(hit.astype(F32), rows, axis=1)

    shape = jax.ShapeDtypeStruct
    raw, emb, probs, stats, own_score = pl.pallas_call(
        score_kernel,
        out_shape=(
            shape((12 * rows, width), BF16),
            shape((12 * rows, width), BF16),
            shape((8 * rows, 4 * rows), BF16),
            shape((8, 256), F32),
            shape((8, 256), F32),
        ),
        scratch_shapes=[pltpu.VMEM((8 * rows, 4 * rows), F32)],
        compiler_params=pltpu.CompilerParams(vmem_limit_bytes=26 * 2**20),
        cost_estimate=pl.CostEstimate(flops=6 * 10**9, bytes_accessed=10**7, transcendentals=10**6),
        name="scores",
    )(*query_blocks, *passage_blocks, full_weight, hit)

    came = [shift(stats, "x", -o) for o in OFFSETS[1:]]
    query_sum = dot(probs, emb[4 * rows :], FIRST)
    query_sum, *came = lax.optimization_barrier((query_sum, *came))

    low, high = shape((rows, width), BF16), shape((rows, width), F32)
    losses, *query_part, own, back, following, ahead, passage_other, mine, theirs = pl.pallas_call(
        grad_kernel,
        out_shape=(
            shape((8, 256), F32),
            *(high, low, high, low) * 2,
            shape((4 * rows, width), BF16),
            shape((width // 2, width), F32),
            shape((width // 2, width), BF16),
        ),
        in_specs=[pl.BlockSpec(memory_space=pltpu.SMEM)] + [pl.BlockSpec(memory_space=pltpu.VMEM)] * 9,
        scratch_shapes=[pltpu.VMEM((4 * rows, width), BF16), pltpu.VMEM((12 * rows, width), BF16)],
        compiler_params=pltpu.CompilerParams(vmem_limit_bytes=34 * 2**20),
        cost_estimate=pl.CostEstimate(flops=6 * 10**9, bytes_accessed=10**7, transcendentals=10**4),
        name="grads",
    )(jnp.reshape(c, (1,)), stats, *came, own_score, raw, emb, probs, query_sum)

    mine = (mine + swap(theirs).astype(F32)).astype(BF16)
    weight_sum = lax.all_to_all(mine.reshape(64, -1, width), ("z", "x", "y"), 0, 0)
    grad_weight = scale * jnp.sum(weight_sum.astype(F32), axis=0)

    def finish(part, axis):
        own, back, following, ahead = part
        ahead, back = shift(ahead, axis, 1).astype(F32), shift(back, axis, -1).astype(F32)
        last = shift((following + ahead).astype(BF16), axis, 1).astype(F32)
        return dot((scale * (own + back + last)).astype(BF16), full_weight, LAST).astype(BF16)

    grad_queries = finish(query_part, "x")
    came = swap(passage_other).astype(F32)
    own, back, following, ahead = (
        (part.astype(F32) + came[i * rows : (i + 1) * rows]).astype(part.dtype)
        for i, part in enumerate((own, back, following, ahead))
    )
    grad_passages = finish((own, back, following, ahead), "z")
    return losses[0, :rows], grad_queries, grad_passages, grad_weight


def solution(mesh):
    grid = Mesh(mesh.devices.reshape([SIZES[a] for a in AXES]), AXES)
    table, line = P(AXES, None), P(AXES)
    return jax.shard_map(
        local,
        mesh=grid,
        in_specs=(table, table, table, P(), P()),
        out_specs=(line, table, table, table),
        check_vma=False,
    )
```

time: 156 us -> 114 us (0.73)
  matrix products: 31.1 us -> 7.15 us
  waiting for transfers between devices: 47.8 us -> 27.5 us
  blocking collectives: 0 us -> 14.4 us
  Pallas kernels: 0 us -> 14.1 us
  starting transfers between devices: 43.3 us -> 29.5 us
  local copies, waits for them, and re-layouts: 17.7 us -> 5.39 us
    dot_general x12 -> x3, matrix products: 31.1 us -> 7.15 us  [dot(): return lax.dot_general(a, b, dims, preferred_element_type=F32)]
    ppermute x37 -> x26, waiting for transfers between devices: 47.8 us -> 27.5 us  [the longest x18 25.6 us: shift(): return lax.ppermute(value, names, pairs)]
    ppermute x37 -> x26, starting transfers between devices: 43.3 us -> 23.9 us  [the longest x18 22.3 us: shift(): return lax.ppermute(value, names, pairs)]
    all_to_all x0 -> x1, blocking collectives: none -> 14.4 us  [gather_all(): lax.all_to_all(jnp.broadcast_to(weight, (16, rows, width)), ('z', 'x'), 0...]
    pallas_call x0 -> x2, Pallas kernels: none -> 14.1 us  [the longest x1 7.1 us: local(): pl.pallas_call(grad_kernel, out_shape=(shape((8, 256), F32), *(high, low,...]
    unnamed x42 -> x41, local copies, waits for them, and re-layouts: 11 us -> 2.28 us
    all_to_all x0 -> x1, starting transfers between devices: none -> 5.52 us  [local(): lax.all_to_all(mine.reshape(64, -1, width), ('z', 'x', 'y'), 0, 0)]
    add x6 -> x0, other arithmetic: 3.4 us -> none  [the longest x1 3.13 us: reduce_weight(): part = mine + shift(theirs.astype(BF16), 'c', 1).astype(F32)]
  transfers between devices with their start and end apart: 37 -> 27, of which waited for: 20 -> 8; matrix products, arithmetic and copies ran while one was open for 23% -> 18% of each run, Pallas kernels for 0% -> 0%
where the time goes in v2:
time: 114 us; the launch traced here: 112 us
  starting transfers between devices  29.5 us (26%)
  waiting for transfers between devices  27.5 us (24%)
  blocking collectives  14.4 us (13%)
  Pallas kernels  14.1 us (12%)
  other arithmetic  13.3 us (12%)
  matrix products  7.15 us (6%)
  local copies, waits for them, and re-layouts  5.39 us (5%)
    ppermute x18, waiting for transfers between devices, shift(): return lax.ppermute(value, names, pairs)  25.6 us
    ppermute x18, starting transfers between devices, shift(): return lax.ppermute(value, names, pairs)  22.3 us
    all_to_all x1, blocking collectives, gather_all(): lax.all_to_all(jnp.broadcast_to(weight, (16, rows, width)), ('z', 'x'), 0...  14.4 us
    dot_general x3, matrix products, dot(): return lax.dot_general(a, b, dims, preferred_element_type=F32)  7.15 us
    pallas_call x1, Pallas kernels, local(): pl.pallas_call(grad_kernel, out_shape=(shape((8, 256), F32), *(high, low,...  7.1 us
    pallas_call x1, Pallas kernels, local(): pl.pallas_call(score_kernel, out_shape=(shape((12 * rows, width), BF16),...  7.03 us
    all_to_all x1, starting transfers between devices, local(): lax.all_to_all(mine.reshape(64, -1, width), ('z', 'x', 'y'), 0, 0)  5.52 us
    convert_element_type x2, other arithmetic, finish(): last = shift((following + ahead).astype(BF16), axis, 1).astype(F32)  2.55 us
  transfers between devices with their start and end apart: 27, of which 8 were waited for; matrix products, arithmetic and copies ran while one was open for 18% of the time, Pallas kernels for 0%

profile of v2, /device:TPU:0, one launch (start us, length us, event | category | flops | bytes accessed | tf_op | source)
XLA Modules:
  0.0 112.3 jit_solution(16451178552172412418)
XLA Ops:
  0.6 1.6 %collective-permute-start = (bf16[160,1024]{1,0:T(8,128)(2,1)}, bf16[160,1024]{1,0:T(8,128)(2,1)S(1)}, u32[]{:S(2)}, u32[]{:S(2)}) collective-permute-start(bf16[160,1024]{1,0:T(8,128)(2,1)} %refs_0_.1), channel_id=1, source_target_pairs={{0,8},{4,28},{8,16},{12,4},{16,24},{20,12},{24,0},{28,20},{1,9},{5... | collective-permute-start | bytes 983048 | tf_op jit(solution)/shard_map/ppermute | solution.py:27
  2.3 1.7 %collective-permute-start.1 = (bf16[160,1024]{1,0:T(8,128)(2,1)}, bf16[160,1024]{1,0:T(8,128)(2,1)S(1)}, u32[]{:S(2)}, u32[]{:S(2)}) collective-permute-start(bf16[160,1024]{1,0:T(8,128)(2,1)} %refs_0_.1), channel_id=1, source_target_pairs={{0,24},{4,12},{8,0},{12,20},{16,8},{20,28},{24,16},{28,4},{1,25},{... | collective-permute-start | bytes 983048 | tf_op jit(solution)/shard_map/ppermute | solution.py:27
  4.0 4.1 %collective-permute-start.3 = (bf16[160,1024]{1,0:T(8,128)(2,1)}, bf16[160,1024]{1,0:T(8,128)(2,1)S(1)}, u32[]{:S(2)}, u32[]{:S(2)}) collective-permute-start(bf16[160,1024]{1,0:T(8,128)(2,1)} %refs_4_.1), channel_id=1, source_target_pairs={{0,96},{4,36},{32,0},{36,68},{64,32},{68,100},{96,64},{100,4},{1,9... | collective-permute-start | bytes 983048 | tf_op jit(solution)/shard_map/ppermute | solution.py:27
  8.1 0.7 broadcast_in_dim.4
  8.8 14.4 %all_to_all.10 = bf16[16,8,1024]{2,1,0:T(8,128)(2,1)S(1)} all-to-all(bf16[16,8,1024]{2,1,0:T(8,128)(2,1)S(1)} %broadcast_in_dim.4), channel_id=1, replica_groups=mesh['z'=4,'x'=4,'c'=2,'y'=4] {'z','x'}, dimensions={0} | all-to-all | bytes 524288 | tf_op jit(solution)/shard_map/all_to_all | solution.py:46
  23.2 0.6 collective-permute-start.5
  23.8 1.6 %collective-permute-start.4 = (bf16[16,8,1024]{2,1,0:T(8,128)(2,1)S(1)}, bf16[16,8,1024]{2,1,0:T(8,128)(2,1)}, u32[]{:S(2)}, u32[]{:S(2)}) collective-permute-start(bf16[16,8,1024]{2,1,0:T(8,128)(2,1)S(1)} %all_to_all.10), channel_id=1, source_target_pairs={{0,1},{4,7},{1,2},{5,4},{2,3},{6,5},{3,0},{7,6},{8,9},{12,15},{9,1... | collective-permute-start | bytes 786440 | tf_op jit(solution)/shard_map/ppermute | solution.py:27
  25.4 1.7 %collective-permute-start.12 = (bf16[16,8,1024]{2,1,0:T(8,128)(2,1)S(1)}, bf16[16,8,1024]{2,1,0:T(8,128)(2,1)}, u32[]{:S(2)}, u32[]{:S(2)}) collective-permute-start(bf16[16,8,1024]{2,1,0:T(8,128)(2,1)S(1)} %all_to_all.10), channel_id=1, source_target_pairs={{0,3},{4,5},{1,0},{5,6},{2,1},{6,7},{3,2},{7,4},{8,11},{12,13},{9,... | collective-permute-start | bytes 786440 | tf_op jit(solution)/shard_map/ppermute | solution.py:27
  27.1 0.8 copy.11
  27.9 6.3 %collective-permute-done.4 = bf16[16,8,1024]{2,1,0:T(8,128)(2,1)} collective-permute-done((bf16[16,8,1024]{2,1,0:T(8,128)(2,1)S(1)}, bf16[16,8,1024]{2,1,0:T(8,128)(2,1)}, u32[]{:S(2)}, u32[]{:S(2)}) %collective-permute-start.4) | collective-permute-done | bytes 262176 | tf_op jit(solution)/shard_map/ppermute | solution.py:27
  34.2 0.5 collective-permute-start.10
  34.8 0.2 collective-permute-start.11
  34.9 2.1 %pad_maximum_fusion.3 = bf16[3,16,8,1024]{3,2,1,0:T(8,128)(2,1)} fusion(bf16[1,16,8,1024]{3,2,1,0:T(8,128)(2,1)} %bitcast.3, bf16[1,16,8,1024]{3,2,1,0:T(8,128)(2,1)} %bitcast.2, bf16[1,16,8,1024]{3,2,1,0:T(8,128)(2,1)} %bitcast.52), kind=kLoop, calls=%fused_computation.14 | loop fusion | flops 786432 | bytes 1572864 | tf_op jit(solution)/shard_map/stack | solution.py:57
  37.0 0.4 collective-permute-start.13
  37.5 0.6 gather_fusion.1
  38.2 0.6 gather_fusion
  38.7 0.1 stack.141
  38.9 3.8 %collective-permute-done.7 = bf16[16,8,1024]{2,1,0:T(8,128)(2,1)} collective-permute-done((bf16[16,8,1024]{2,1,0:T(8,128)(2,1)}, bf16[16,8,1024]{2,1,0:T(8,128)(2,1)}, u32[]{:S(2)}, u32[]{:S(2)}) %collective-permute-start.7) | collective-permute-done | bytes 262176 | tf_op jit(solution)/shard_map/ppermute | solution.py:27
  42.7 0.2 and_reduce_fusion
  42.9 0.1 copy.12
  43.1 0.1 reshape.121.refs_13_
  43.2 1.3 %collective-permute-done.14 = bf16[16,8,1024]{2,1,0:T(8,128)(2,1)} collective-permute-done((bf16[16,8,1024]{2,1,0:T(8,128)(2,1)}, bf16[16,8,1024]{2,1,0:T(8,128)(2,1)}, u32[]{:S(2)}, u32[]{:S(2)}) %collective-permute-start.14) | collective-permute-done | bytes 262176 | tf_op jit(solution)/shard_map/ppermute | solution.py:20
  44.5 1.1 select_bitcast_fusion.1
  45.6 1.5 %broadcast_select_fusion.1 = (bf16[3,16,8,1024]{3,2,1,0:T(8,128)(2,1)S(1)}, bf16[3,16,8,1024]{3,2,1,0:T(8,128)(2,1)S(1)}) fusion(bf16[3,16,8,1024]{3,2,1,0:T(8,128)(2,1)} %collective-permute-done.13, pred[]{:T(512)S(6)} %eq.42, bf16[1,16,8,1024]{3,2,1,0:T(8,128)(2,1)} %bitcast.3, bf16[1,16,8,1024]{3,2,1,0:T(8,128)(2,1)} %bitcast.2, ...), kind=kLoop, calls=%fused_computation.16 | loop fusion | flops 1572864 | bytes 3145730 | tf_op jit(solution)/shard_map/jit(_where)/select_n | solution.py:62
  47.3 0.2 pad_maximum_fusion.1
  47.6 0.1 maximum_bitcast_fusion
  47.8 0.1 maximum_bitcast_fusion.1
  48.1 0.2 pad_maximum_fusion
  48.3 0.7 copy-done.4
  49.0 0.1 copy-done.5
  49.1 0.1 copy-done.7
  49.2 0.1 copy-done.9
  49.3 0.1 copy-done.11
  49.4 0.1 copy-done.13
  49.5 0.1 copy-done.15
  49.6 0.1 copy-done.17
  49.7 7.0 %scores.1 = (bf16[1920,1024]{1,0:T(8,128)(2,1)S(1)}, bf16[1920,1024]{1,0:T(8,128)(2,1)S(1)}, bf16[1280,640]{1,0:T(8,128)(2,1)S(1)}, f32[8,256]{1,0:T(8,128)S(1)}, f32[8,256]{1,0:T(8,128)S(1)}) custom-call(bf16[160,1024]{1,0:T(8,128)(2,1)S(1)} %copy-done.4, bf16[160,1024]{1,0:T(8,128)(2,1)S(1)} %collective-permute-done.refs_1_, ...), custom_call_target="tpu_custom_call" | custom-call | flops 6000000000 | bytes 10000000 | tf_op jit(solution)/shard_map/scores/pallas_call | solution.py:177
  56.7 1.3 %collective-permute-start.17 = (f32[8,256]{1,0:T(8,128)S(1)}, f32[8,256]{1,0:T(8,128)S(1)}, u32[]{:S(2)}, u32[]{:S(2)}) collective-permute-start(f32[8,256]{1,0:T(8,128)S(1)} %get-tuple-element.51.here), channel_id=1, source_target_pairs={{0,16},{4,20},{8,24},{12,28},{16,0},{20,4},{24,8},{28,12},{1,17},{... | collective-permute-start | bytes 24584 | tf_op jit(solution)/shard_map/ppermute | solution.py:27
  58.0 2.1 %collective-permute-start.16 = (f32[8,256]{1,0:T(8,128)S(1)}, f32[8,256]{1,0:T(8,128)S(1)}, u32[]{:S(2)}, u32[]{:S(2)}) collective-permute-start(f32[8,256]{1,0:T(8,128)S(1)} %get-tuple-element.51.here), channel_id=1, source_target_pairs={{0,24},{4,12},{8,0},{12,20},{16,8},{20,28},{24,16},{28,4},{1,25},{... | collective-permute-start | bytes 24584 | tf_op jit(solution)/shard_map/ppermute | solution.py:27
  60.1 1.9 %fusion.query_sum = f32[640,1024]{1,0:T(8,128)S(1)} fusion(bf16[1280,640]{1,0:T(8,128)(2,1)S(1)} %get-tuple-element.52.probs, bf16[1920,1024]{1,0:T(8,128)(2,1)S(1)} %get-tuple-element.53.emb), kind=kOutput, calls=%fused_computation.2 | convolution fusion | flops 1677721600 | bytes 6881280 | tf_op jit(solution)/shard_map/dot_general | solution.py:40
  62.0 2.9 %collective-permute-done.15.before = f32[8,256]{1,0:T(8,128)S(1)} collective-permute-done((f32[8,256]{1,0:T(8,128)S(1)}, f32[8,256]{1,0:T(8,128)S(1)}, u32[]{:S(2)}, u32[]{:S(2)}) %collective-permute-start.15) | collective-permute-done | bytes 8224 | tf_op jit(solution)/shard_map/ppermute | solution.py:27
  64.9 7.1 %grads.1 = (f32[8,256]{1,0:T(8,128)S(1)}, f32[160,1024]{1,0:T(8,128)S(1)}, bf16[160,1024]{1,0:T(8,128)(2,1)}, f32[160,1024]{1,0:T(8,128)S(1)}, bf16[160,1024]{1,...) custom-call(s32[1]{0:T(128)} %bitcast.core, ...), custom_call_target="tpu_custom_call" | custom-call | flops 6000000000 | bytes 10000000 | tf_op jit(solution)/shard_map/grads/pallas_call | solution.py:197
  72.0 0.1 collective-permute-start.21
  72.1 0.5 collective-permute-start.25
  72.6 0.3 collective-permute-start.18
  73.0 1.7 %collective-permute-start.19 = (bf16[160,1024]{1,0:T(8,128)(2,1)}, bf16[160,1024]{1,0:T(8,128)(2,1)}, u32[]{:S(2)}, u32[]{:S(2)}) collective-permute-start(bf16[160,1024]{1,0:T(8,128)(2,1)} %get-tuple-element.64), channel_id=1, source_target_pairs={{0,8},{4,28},{8,16},{12,4},{16,24},{20,12},{24,0},{28,20},{1,9},{5... | collective-permute-start | bytes 983048 | tf_op jit(solution)/shard_map/ppermute | solution.py:27
  74.7 0.5 collective-permute-done.21
  75.2 0.3 convert_element_type.70
  75.5 1.3 %fusion.6 = (bf16[160,1024]{1,0:T(8,128)(2,1)}, bf16[160,1024]{1,0:T(8,128)(2,1)}) fusion(f32[640,1024]{1,0:T(8,128)S(1)} %convert_element_type.70, bf16[160,1024]{1,0:T(8,128)(2,1)S(1)} %get-tuple-element.67, bf16[160,1024]{1,0:T(8,128)(2,1)S(1)} %get-tuple-element.69), kind=kLoop, calls=%fused_computation.23 | loop fusion | flops 983040 | bytes 2621440 | tf_op jit(solution)/shard_map/convert_element_type | solution.py:226
  76.8 1.0 collective-permute-start.23
  77.9 1.3 %fusion.2 = bf16[64,8,1024]{2,1,0:T(8,128)(2,1)} fusion(f32[512,1024]{1,0:T(8,128)S(1)} %get-tuple-element.70, bf16[512,1024]{1,0:T(8,128)(2,1)S(1)} %collective-permute-done.25), kind=kLoop, calls=%fused_computation.9 | loop fusion | flops 1572864 | bytes 4194304 | tf_op jit(solution)/shard_map/reshape | solution.py:214
  79.2 5.5 %all-to-all-start.1 = ((bf16[64,8,1024]{2,1,0:T(8,128)(2,1)}), bf16[64,8,1024]{2,1,0:T(8,128)(2,1)}, u32[]{:S(2)}, u32[]{:S(2)}) async-start(bf16[64,8,1024]{2,1,0:T(8,128)(2,1)} %fusion.2), calls=%async_computation.1 | async-start | bytes 2097152 | tf_op jit(solution)/shard_map/all_to_all | solution.py:214
  84.7 1.1 add_convert_fusion.1
  85.8 1.5 %collective-permute-start.20 = (bf16[160,1024]{1,0:T(8,128)(2,1)S(1)}, bf16[160,1024]{1,0:T(8,128)(2,1)S(1)}, u32[]{:S(2)}, u32[]{:S(2)}) collective-permute-start(bf16[160,1024]{1,0:T(8,128)(2,1)S(1)} %add_convert_fusion.1), channel_id=1, source_target_pairs={{0,8},{4,28},{8,16},{12,4},{16,24},{20,12},{24,0},{28,20},{1,9},{5... | collective-permute-start | bytes 983048 | tf_op jit(solution)/shard_map/ppermute | solution.py:27
  87.3 3.0 %collective-permute-start.22 = (bf16[160,1024]{1,0:T(8,128)(2,1)}, bf16[160,1024]{1,0:T(8,128)(2,1)S(1)}, u32[]{:S(2)}, u32[]{:S(2)}) collective-permute-start(bf16[160,1024]{1,0:T(8,128)(2,1)} %get-tuple-element.72), channel_id=1, source_target_pairs={{0,96},{4,36},{32,0},{36,68},{64,32},{68,100},{96,64},{100,4},{1,9... | collective-permute-start | bytes 983048 | tf_op jit(solution)/shard_map/ppermute | solution.py:27
  90.3 1.5 %fusion.5 = bf16[160,1024]{1,0:T(8,128)(2,1)S(1)} fusion(f32[160,1024]{1,0:T(8,128)} %copy-done.1, f32[640,1024]{1,0:T(8,128)} %copy-done.18, bf16[160,1024]{1,0:T(8,128)(2,1)} %collective-permute-done.23), kind=kLoop, calls=%fused_computation.21 | loop fusion | flops 655360 | bytes 1966080 | tf_op jit(solution)/shard_map/convert_element_type | solution.py:220
  91.9 0.6 slice.39
  92.4 9.5 %collective-permute-done.20 = bf16[160,1024]{1,0:T(8,128)(2,1)S(1)} collective-permute-done((bf16[160,1024]{1,0:T(8,128)(2,1)S(1)}, bf16[160,1024]{1,0:T(8,128)(2,1)S(1)}, u32[]{:S(2)}, u32[]{:S(2)}) %collective-permute-start.20) | collective-permute-done | bytes 327712 | tf_op jit(solution)/shard_map/ppermute | solution.py:27
  102.0 2.6 %convolution_convert_fusion.1 = bf16[160,1024]{1,0:T(8,128)(2,1)} fusion(bf16[1024,1024]{1,0:T(8,128)(2,1)S(1)} %bitcast.50, bf16[160,1024]{1,0:T(8,128)(2,1)S(1)} %collective-permute-done.20, f32[160,1024]{1,0:T(8,128)S(1)} %get-tuple-element.61, bf16[160,1024]{1,0:T(8,128)(2,1)} %collective-permute-done.18), kind=kOutput, calls=%fused_computation.8 | convolution fusion | flops 336691200 | bytes 3735552 | tf_op jit(solution)/shard_map/dot_general | solution.py:40
  104.5 1.1 collective-permute-done.22
  105.6 2.0 %collective-permute-done.24 = bf16[160,1024]{1,0:T(8,128)(2,1)S(1)} collective-permute-done((bf16[160,1024]{1,0:T(8,128)(2,1)S(1)}, bf16[160,1024]{1,0:T(8,128)(2,1)S(1)}, u32[]{:S(2)}, u32[]{:S(2)}) %collective-permute-start.24) | collective-permute-done | bytes 327712 | tf_op jit(solution)/shard_map/ppermute | solution.py:27
  107.6 2.7 %convolution_convert_fusion = bf16[160,1024]{1,0:T(8,128)(2,1)} fusion(bf16[1024,1024]{1,0:T(8,128)(2,1)S(1)} %bitcast.51, f32[160,1024]{1,0:T(8,128)S(1)} %copy-done.3, f32[640,1024]{1,0:T(8,128)} %copy-done.18, bf16[160,1024]{1,0:T(8,128)(2,1)S(1)} %collective-permute-done.24, bf16[160,1024]{1,0:T(8,128)(2,1)S(1)} %collective-permute-done.22), kind=kOutput, calls=%fused_computation.7 | convolution fusion | flops 336855040 | bytes 4390912 | tf_op jit(solution)/shard_map/dot_general | solution.py:40
  110.3 1.4 %convert_reduce_fusion = f32[8,1024]{1,0:T(8,128)S(1)} fusion(bf16[64,8,1024]{2,1,0:T(8,128)(2,1)} %all-to-all-done.1), kind=kLoop, calls=%fused_computation.5 | loop fusion | flops 1040384 | bytes 1081344 | tf_op jit(solution)/shard_map/reduce_sum | solution.py:215
  111.7 0.6 broadcast_multiply_fusion
  (70 shorter events, 0.7 us)
Async XLA Ops:
  0.6 36.9 %copy-start = (s32[128]{0:T(128)S(1)}, s32[128]{0:T(128)}, u32[]{:S(2)}) copy-start(s32[128]{0:T(128)} %param.9) | copy-start | bytes 1540
  0.6 22.5 %collective-permute-start = (bf16[160,1024]{1,0:T(8,128)(2,1)}, bf16[160,1024]{1,0:T(8,128)(2,1)S(1)}, u32[]{:S(2)}, u32[]{:S(2)}) collective-permute-start(bf16[160,1024]{1,0:T(8,128)(2,1)} %refs_0_.1), channel_id=1, source_target_pairs={{0,8},{4,28},{8,16},{12,4},{16,24},{20,12},{24,0},{28,20},{1,9},{5... | collective-permute-start | bytes 983048 | tf_op jit(solution)/shard_map/ppermute | solution.py:27
  2.3 20.9 %collective-permute-start.1 = (bf16[160,1024]{1,0:T(8,128)(2,1)}, bf16[160,1024]{1,0:T(8,128)(2,1)S(1)}, u32[]{:S(2)}, u32[]{:S(2)}) collective-permute-start(bf16[160,1024]{1,0:T(8,128)(2,1)} %refs_0_.1), channel_id=1, source_target_pairs={{0,24},{4,12},{8,0},{12,20},{16,8},{20,28},{24,16},{28,4},{1,25},{... | collective-permute-start | bytes 983048 | tf_op jit(solution)/shard_map/ppermute | solution.py:27
  4.0 19.2 %collective-permute-start.3 = (bf16[160,1024]{1,0:T(8,128)(2,1)}, bf16[160,1024]{1,0:T(8,128)(2,1)S(1)}, u32[]{:S(2)}, u32[]{:S(2)}) collective-permute-start(bf16[160,1024]{1,0:T(8,128)(2,1)} %refs_4_.1), channel_id=1, source_target_pairs={{0,96},{4,36},{32,0},{36,68},{64,32},{68,100},{96,64},{100,4},{1,9... | collective-permute-start | bytes 983048 | tf_op jit(solution)/shard_map/ppermute | solution.py:27
  8.1 15.1 %collective-permute-start.2 = (bf16[160,1024]{1,0:T(8,128)(2,1)}, bf16[160,1024]{1,0:T(8,128)(2,1)S(1)}, u32[]{:S(2)}, u32[]{:S(2)}) collective-permute-start(bf16[160,1024]{1,0:T(8,128)(2,1)} %refs_4_.1), channel_id=1, source_target_pairs={{0,32},{4,100},{32,64},{36,4},{64,96},{68,36},{96,0},{100,68},{1,3... | collective-permute-start | bytes 983048 | tf_op jit(solution)/shard_map/ppermute | solution.py:27
  23.2 11.6 %copy-start.19 = (bf16[16,8,1024]{2,1,0:T(8,128)(2,1)}, bf16[16,8,1024]{2,1,0:T(8,128)(2,1)S(1)}, u32[]{:S(2)}) copy-start(bf16[16,8,1024]{2,1,0:T(8,128)(2,1)S(1)} %all_to_all.10) | copy-start | bytes 786436
  23.2 11.0 %collective-permute-start.5 = (bf16[160,1024]{1,0:T(8,128)(2,1)S(1)}, bf16[160,1024]{1,0:T(8,128)(2,1)S(1)}, u32[]{:S(2)}, u32[]{:S(2)}) collective-permute-start(bf16[160,1024]{1,0:T(8,128)(2,1)S(1)} %collective-permute-done.refs_1_), channel_id=1, source_target_pairs={{0,8},{4,28},{8,16},{12,4},{16,24},{20,12},{24,0},{28,20},{1,9},{5... | collective-permute-start | bytes 983048 | tf_op jit(solution)/shard_map/ppermute | solution.py:27
  23.8 10.9 %collective-permute-start.6 = (bf16[160,1024]{1,0:T(8,128)(2,1)S(1)}, bf16[160,1024]{1,0:T(8,128)(2,1)S(1)}, u32[]{:S(2)}, u32[]{:S(2)}) collective-permute-start(bf16[160,1024]{1,0:T(8,128)(2,1)S(1)} %collective-permute-done.2.refs_5_), channel_id=1, source_target_pairs={{0,32},{4,100},{32,64},{36,4},{64,96},{68,36},{96,0},{100,68},{1,3... | collective-permute-start | bytes 983048 | tf_op jit(solution)/shard_map/ppermute | solution.py:27
  23.8 10.4 %collective-permute-start.4 = (bf16[16,8,1024]{2,1,0:T(8,128)(2,1)S(1)}, bf16[16,8,1024]{2,1,0:T(8,128)(2,1)}, u32[]{:S(2)}, u32[]{:S(2)}) collective-permute-start(bf16[16,8,1024]{2,1,0:T(8,128)(2,1)S(1)} %all_to_all.10), channel_id=1, source_target_pairs={{0,1},{4,7},{1,2},{5,4},{2,3},{6,5},{3,0},{7,6},{8,9},{12,15},{9,1... | collective-permute-start | bytes 786440 | tf_op jit(solution)/shard_map/ppermute | solution.py:27
  25.4 9.3 %collective-permute-start.12 = (bf16[16,8,1024]{2,1,0:T(8,128)(2,1)S(1)}, bf16[16,8,1024]{2,1,0:T(8,128)(2,1)}, u32[]{:S(2)}, u32[]{:S(2)}) collective-permute-start(bf16[16,8,1024]{2,1,0:T(8,128)(2,1)S(1)} %all_to_all.10), channel_id=1, source_target_pairs={{0,3},{4,5},{1,0},{5,6},{2,1},{6,7},{3,2},{7,4},{8,11},{12,13},{9,... | collective-permute-start | bytes 786440 | tf_op jit(solution)/shard_map/ppermute | solution.py:27
  27.1 9.9 %collective-permute-start.8 = (bf16[160,1024]{1,0:T(8,128)(2,1)}, bf16[160,1024]{1,0:T(8,128)(2,1)S(1)}, u32[]{:S(2)}, u32[]{:S(2)}) collective-permute-start(bf16[160,1024]{1,0:T(8,128)(2,1)} %refs_4_.1), channel_id=1, source_target_pairs={{0,4},{4,0},{1,5},{5,1},{2,6},{6,2},{3,7},{7,3},{8,12},{12,8},{9,1... | collective-permute-start | bytes 983048 | tf_op jit(solution)/shard_map/ppermute | solution.py:20
  34.2 4.6 %collective-permute-start.9 = (bf16[160,1024]{1,0:T(8,128)(2,1)S(1)}, bf16[160,1024]{1,0:T(8,128)(2,1)S(1)}, u32[]{:S(2)}, u32[]{:S(2)}) collective-permute-start(bf16[160,1024]{1,0:T(8,128)(2,1)S(1)} %collective-permute-done.2.refs_5_), channel_id=1, source_target_pairs={{0,4},{4,0},{1,5},{5,1},{2,6},{6,2},{3,7},{7,3},{8,12},{12,8},{9,1... | collective-permute-start | bytes 983048 | tf_op jit(solution)/shard_map/ppermute | solution.py:20
  34.2 12.9 %copy-start.6 = (bf16[160,1024]{1,0:T(8,128)(2,1)}, bf16[160,1024]{1,0:T(8,128)(2,1)S(1)}, u32[]{:S(2)}) copy-start(bf16[160,1024]{1,0:T(8,128)(2,1)S(1)} %collective-permute-done.5.refs_3_) | copy-start | bytes 983044
  34.2 4.6 %collective-permute-start.10 = (bf16[160,1024]{1,0:T(8,128)(2,1)S(1)}, bf16[160,1024]{1,0:T(8,128)(2,1)S(1)}, u32[]{:S(2)}, u32[]{:S(2)}) collective-permute-start(bf16[160,1024]{1,0:T(8,128)(2,1)S(1)} %collective-permute-done.3.refs_6_), channel_id=1, source_target_pairs={{0,4},{4,0},{1,5},{5,1},{2,6},{6,2},{3,7},{7,3},{8,12},{12,8},{9,1... | collective-permute-start | bytes 983048 | tf_op jit(solution)/shard_map/ppermute | solution.py:20
  34.7 12.4 %copy-start.8 = (bf16[160,1024]{1,0:T(8,128)(2,1)}, bf16[160,1024]{1,0:T(8,128)(2,1)S(1)}, u32[]{:S(2)}) copy-start(bf16[160,1024]{1,0:T(8,128)(2,1)S(1)} %collective-permute-done.6.refs_7_) | copy-start | bytes 983044
  34.7 7.9 %collective-permute-start.7 = (bf16[16,8,1024]{2,1,0:T(8,128)(2,1)}, bf16[16,8,1024]{2,1,0:T(8,128)(2,1)}, u32[]{:S(2)}, u32[]{:S(2)}) collective-permute-start(bf16[16,8,1024]{2,1,0:T(8,128)(2,1)} %collective-permute-done.4), channel_id=1, source_target_pairs={{0,1},{4,7},{1,2},{5,4},{2,3},{6,5},{3,0},{7,6},{8,9},{12,15},{9,1... | collective-permute-start | bytes 786440 | tf_op jit(solution)/shard_map/ppermute | solution.py:27
  34.8 7.9 %collective-permute-start.11 = (bf16[160,1024]{1,0:T(8,128)(2,1)S(1)}, bf16[160,1024]{1,0:T(8,128)(2,1)S(1)}, u32[]{:S(2)}, u32[]{:S(2)}) collective-permute-start(bf16[160,1024]{1,0:T(8,128)(2,1)S(1)} %collective-permute-done.6.refs_7_), channel_id=1, source_target_pairs={{0,4},{4,0},{1,5},{5,1},{2,6},{6,2},{3,7},{7,3},{8,12},{12,8},{9,1... | collective-permute-start | bytes 983048 | tf_op jit(solution)/shard_map/ppermute | solution.py:20
  37.0 10.1 %copy-start.10 = (bf16[160,1024]{1,0:T(8,128)(2,1)}, bf16[160,1024]{1,0:T(8,128)(2,1)S(1)}, u32[]{:S(2)}) copy-start(bf16[160,1024]{1,0:T(8,128)(2,1)S(1)} %collective-permute-done.8.refs_8_) | copy-start | bytes 983044
  37.0 8.6 %collective-permute-start.13 = (bf16[3,16,8,1024]{3,2,1,0:T(8,128)(2,1)}, bf16[3,16,8,1024]{3,2,1,0:T(8,128)(2,1)}, u32[]{:S(2)}, u32[]{:S(2)}) collective-permute-start(bf16[3,16,8,1024]{3,2,1,0:T(8,128)(2,1)} %pad_maximum_fusion.3), channel_id=1, source_target_pairs={{0,4},{4,0},{1,5},{5,1},{2,6},{6,2},{3,7},{7,3},{8,12},{12,8},{9,1... | collective-permute-start | bytes 2359304 | tf_op jit(solution)/shard_map/ppermute | solution.py:20
  38.8 8.3 %copy-start.14 = (bf16[160,1024]{1,0:T(8,128)(2,1)}, bf16[160,1024]{1,0:T(8,128)(2,1)S(1)}, u32[]{:S(2)}) copy-start(bf16[160,1024]{1,0:T(8,128)(2,1)S(1)} %collective-permute-done.10.refs_10_) | copy-start | bytes 983044
  38.9 8.3 %copy-start.12 = (bf16[160,1024]{1,0:T(8,128)(2,1)}, bf16[160,1024]{1,0:T(8,128)(2,1)S(1)}, u32[]{:S(2)}) copy-start(bf16[160,1024]{1,0:T(8,128)(2,1)S(1)} %collective-permute-done.9.refs_9_) | copy-start | bytes 983044
  42.6 4.5 %copy-start.16 = (bf16[160,1024]{1,0:T(8,128)(2,1)}, bf16[160,1024]{1,0:T(8,128)(2,1)S(1)}, u32[]{:S(2)}) copy-start(bf16[160,1024]{1,0:T(8,128)(2,1)S(1)} %collective-permute-done.11.refs_11_) | copy-start | bytes 983044
  42.6 1.9 %collective-permute-start.14 = (bf16[16,8,1024]{2,1,0:T(8,128)(2,1)}, bf16[16,8,1024]{2,1,0:T(8,128)(2,1)}, u32[]{:S(2)}, u32[]{:S(2)}) collective-permute-start(bf16[16,8,1024]{2,1,0:T(8,128)(2,1)} %collective-permute-done.7), channel_id=1, source_target_pairs={{0,4},{4,0},{1,5},{5,1},{2,6},{6,2},{3,7},{7,3},{8,12},{12,8},{9,1... | collective-permute-start | bytes 786440 | tf_op jit(solution)/shard_map/ppermute | solution.py:20
  48.0 1.0 copy-start.4
  48.0 1.1 copy-start.5
  48.0 1.2 %copy-start.7 = (bf16[160,1024]{1,0:T(8,128)(2,1)S(1)}, bf16[160,1024]{1,0:T(8,128)(2,1)}, u32[]{:S(2)}) copy-start(bf16[160,1024]{1,0:T(8,128)(2,1)} %copy-done.6) | copy-start | bytes 983044
  48.0 1.2 %copy-start.9 = (bf16[160,1024]{1,0:T(8,128)(2,1)S(1)}, bf16[160,1024]{1,0:T(8,128)(2,1)}, u32[]{:S(2)}) copy-start(bf16[160,1024]{1,0:T(8,128)(2,1)} %copy-done.8) | copy-start | bytes 983044
  48.0 1.3 %copy-start.11 = (bf16[160,1024]{1,0:T(8,128)(2,1)S(1)}, bf16[160,1024]{1,0:T(8,128)(2,1)}, u32[]{:S(2)}) copy-start(bf16[160,1024]{1,0:T(8,128)(2,1)} %copy-done.10) | copy-start | bytes 983044
  48.0 1.4 %copy-start.13 = (bf16[160,1024]{1,0:T(8,128)(2,1)S(1)}, bf16[160,1024]{1,0:T(8,128)(2,1)}, u32[]{:S(2)}) copy-start(bf16[160,1024]{1,0:T(8,128)(2,1)} %copy-done.12) | copy-start | bytes 983044
  48.1 1.5 %copy-start.15 = (bf16[160,1024]{1,0:T(8,128)(2,1)S(1)}, bf16[160,1024]{1,0:T(8,128)(2,1)}, u32[]{:S(2)}) copy-start(bf16[160,1024]{1,0:T(8,128)(2,1)} %copy-done.14) | copy-start | bytes 983044
  48.1 1.6 %copy-start.17 = (bf16[160,1024]{1,0:T(8,128)(2,1)S(1)}, bf16[160,1024]{1,0:T(8,128)(2,1)}, u32[]{:S(2)}) copy-start(bf16[160,1024]{1,0:T(8,128)(2,1)} %copy-done.16) | copy-start | bytes 983044
  56.7 5.3 %collective-permute-start.17 = (f32[8,256]{1,0:T(8,128)S(1)}, f32[8,256]{1,0:T(8,128)S(1)}, u32[]{:S(2)}, u32[]{:S(2)}) collective-permute-start(f32[8,256]{1,0:T(8,128)S(1)} %get-tuple-element.51.here), channel_id=1, source_target_pairs={{0,16},{4,20},{8,24},{12,28},{16,0},{20,4},{24,8},{28,12},{1,17},{... | collective-permute-start | bytes 24584 | tf_op jit(solution)/shard_map/ppermute | solution.py:27
  58.0 4.0 %collective-permute-start.16 = (f32[8,256]{1,0:T(8,128)S(1)}, f32[8,256]{1,0:T(8,128)S(1)}, u32[]{:S(2)}, u32[]{:S(2)}) collective-permute-start(f32[8,256]{1,0:T(8,128)S(1)} %get-tuple-element.51.here), channel_id=1, source_target_pairs={{0,24},{4,12},{8,0},{12,20},{16,8},{20,28},{24,16},{28,4},{1,25},{... | collective-permute-start | bytes 24584 | tf_op jit(solution)/shard_map/ppermute | solution.py:27
  60.1 4.9 %collective-permute-start.15 = (f32[8,256]{1,0:T(8,128)S(1)}, f32[8,256]{1,0:T(8,128)S(1)}, u32[]{:S(2)}, u32[]{:S(2)}) collective-permute-start(f32[8,256]{1,0:T(8,128)S(1)} %get-tuple-element.51.here), channel_id=1, source_target_pairs={{0,8},{4,28},{8,16},{12,4},{16,24},{20,12},{24,0},{28,20},{1,9},{5... | collective-permute-start | bytes 24584 | tf_op jit(solution)/shard_map/ppermute | solution.py:27
  72.0 4.8 %copy-start.1 = (f32[160,1024]{1,0:T(8,128)}, f32[160,1024]{1,0:T(8,128)S(1)}, u32[]{:S(2)}) copy-start(f32[160,1024]{1,0:T(8,128)S(1)} %get-tuple-element.68) | copy-start | bytes 1966084
  72.0 4.8 %copy-start.2 = (f32[160,1024]{1,0:T(8,128)}, f32[160,1024]{1,0:T(8,128)S(1)}, u32[]{:S(2)}) copy-start(f32[160,1024]{1,0:T(8,128)S(1)} %get-tuple-element.65) | copy-start | bytes 1966084
  72.0 3.1 %collective-permute-start.21 = (bf16[640,1024]{1,0:T(8,128)(2,1)S(1)}, bf16[640,1024]{1,0:T(8,128)(2,1)S(1)}, u32[]{:S(2)}, u32[]{:S(2)}) collective-permute-start(bf16[640,1024]{1,0:T(8,128)(2,1)S(1)} %get-tuple-element.66), channel_id=1, source_target_pairs={{0,4},{4,0},{1,5},{5,1},{2,6},{6,2},{3,7},{7,3},{8,12},{12,8},{9,1... | collective-permute-start | bytes 3932168 | tf_op jit(solution)/shard_map/ppermute | solution.py:20
  72.1 5.7 %collective-permute-start.25 = (bf16[512,1024]{1,0:T(8,128)(2,1)S(1)}, bf16[512,1024]{1,0:T(8,128)(2,1)S(1)}, u32[]{:S(2)}, u32[]{:S(2)}) collective-permute-start(bf16[512,1024]{1,0:T(8,128)(2,1)S(1)} %get-tuple-element.71), channel_id=1, source_target_pairs={{0,4},{4,0},{1,5},{5,1},{2,6},{6,2},{3,7},{7,3},{8,12},{12,8},{9,1... | collective-permute-start | bytes 3145736 | tf_op jit(solution)/shard_map/ppermute | solution.py:20
  72.6 19.8 %collective-permute-start.18 = (bf16[160,1024]{1,0:T(8,128)(2,1)}, bf16[160,1024]{1,0:T(8,128)(2,1)}, u32[]{:S(2)}, u32[]{:S(2)}) collective-permute-start(bf16[160,1024]{1,0:T(8,128)(2,1)} %get-tuple-element.62), channel_id=1, source_target_pairs={{0,24},{4,12},{8,0},{12,20},{16,8},{20,28},{24,16},{28,4},{1,25},{... | collective-permute-start | bytes 983048 | tf_op jit(solution)/shard_map/ppermute | solution.py:27
  73.0 11.8 %collective-permute-start.19 = (bf16[160,1024]{1,0:T(8,128)(2,1)}, bf16[160,1024]{1,0:T(8,128)(2,1)}, u32[]{:S(2)}, u32[]{:S(2)}) collective-permute-start(bf16[160,1024]{1,0:T(8,128)(2,1)} %get-tuple-element.64), channel_id=1, source_target_pairs={{0,8},{4,28},{8,16},{12,4},{16,24},{20,12},{24,0},{28,20},{1,9},{5... | collective-permute-start | bytes 983048 | tf_op jit(solution)/shard_map/ppermute | solution.py:27
  75.5 2.4 %copy-start.18 = (f32[640,1024]{1,0:T(8,128)}, f32[640,1024]{1,0:T(8,128)S(1)}, u32[]{:S(2)}) copy-start(f32[640,1024]{1,0:T(8,128)S(1)} %convert_element_type.70) | copy-start | bytes 7864324
  76.8 13.4 %collective-permute-start.23 = (bf16[160,1024]{1,0:T(8,128)(2,1)}, bf16[160,1024]{1,0:T(8,128)(2,1)}, u32[]{:S(2)}, u32[]{:S(2)}) collective-permute-start(bf16[160,1024]{1,0:T(8,128)(2,1)} %get-tuple-element.73), channel_id=1, source_target_pairs={{0,32},{4,100},{32,64},{36,4},{64,96},{68,36},{96,0},{100,68},{1,3... | collective-permute-start | bytes 983048 | tf_op jit(solution)/shard_map/ppermute | solution.py:27
  79.2 31.1 %all-to-all-start.1 = ((bf16[64,8,1024]{2,1,0:T(8,128)(2,1)}), bf16[64,8,1024]{2,1,0:T(8,128)(2,1)}, u32[]{:S(2)}, u32[]{:S(2)}) async-start(bf16[64,8,1024]{2,1,0:T(8,128)(2,1)} %fusion.2), calls=%async_computation.1 | async-start | bytes 2097152 | tf_op jit(solution)/shard_map/all_to_all | solution.py:214
  85.8 16.2 %collective-permute-start.20 = (bf16[160,1024]{1,0:T(8,128)(2,1)S(1)}, bf16[160,1024]{1,0:T(8,128)(2,1)S(1)}, u32[]{:S(2)}, u32[]{:S(2)}) collective-permute-start(bf16[160,1024]{1,0:T(8,128)(2,1)S(1)} %add_convert_fusion.1), channel_id=1, source_target_pairs={{0,8},{4,28},{8,16},{12,4},{16,24},{20,12},{24,0},{28,20},{1,9},{5... | collective-permute-start | bytes 983048 | tf_op jit(solution)/shard_map/ppermute | solution.py:27
  87.3 18.4 %collective-permute-start.22 = (bf16[160,1024]{1,0:T(8,128)(2,1)}, bf16[160,1024]{1,0:T(8,128)(2,1)S(1)}, u32[]{:S(2)}, u32[]{:S(2)}) collective-permute-start(bf16[160,1024]{1,0:T(8,128)(2,1)} %get-tuple-element.72), channel_id=1, source_target_pairs={{0,96},{4,36},{32,0},{36,68},{64,32},{68,100},{96,64},{100,4},{1,9... | collective-permute-start | bytes 983048 | tf_op jit(solution)/shard_map/ppermute | solution.py:27
  91.8 15.8 %copy-start.3 = (f32[160,1024]{1,0:T(8,128)S(1)}, f32[160,1024]{1,0:T(8,128)}, u32[]{:S(2)}) copy-start(f32[160,1024]{1,0:T(8,128)} %copy-done.2) | copy-start | bytes 1966084
  91.8 15.8 %collective-permute-start.24 = (bf16[160,1024]{1,0:T(8,128)(2,1)S(1)}, bf16[160,1024]{1,0:T(8,128)(2,1)S(1)}, u32[]{:S(2)}, u32[]{:S(2)}) collective-permute-start(bf16[160,1024]{1,0:T(8,128)(2,1)S(1)} %fusion.5), channel_id=1, source_target_pairs={{0,32},{4,100},{32,64},{36,4},{64,96},{68,36},{96,0},{100,68},{1,3... | collective-permute-start | bytes 983048 | tf_op jit(solution)/shard_map/ppermute | solution.py:27

commit v3 on v2

--- a/solution.py
+++ b/solution.py
@@ -9,6 +9,7 @@
 
 SIZES = {"z": 4, "x": 4, "c": 2, "y": 4}
 AXES = ("z", "x", "c", "y")
+WAYS = (1, -1)
 OFFSETS = (0, -1, 1, 2)
 BF16 = jnp.bfloat16
 F32 = jnp.float32
@@ -23,7 +24,7 @@
 def shift(value, axis, step):
     names = tuple(a for a in AXES if a in (axis, "c"))
     spots = {(i, c): 4 * c + i if axis == "y" else 2 * i + c for i in range(4) for c in range(2)}
-    pairs = [(spots[i, c], spots[(i + (step, -step)[c]) % 4, c]) for i, c in spots]
+    pairs = [(spots[i, c], spots[(i + step * WAYS[c]) % 4, c]) for i, c in spots]
     return lax.ppermute(value, names, pairs)
 
 
@@ -45,24 +46,17 @@
     ring = [shift(queries, "x", 1), shift(queries, "x", -1), shift(passages, "z", 1), shift(passages, "z", -1)]
     part = lax.all_to_all(jnp.broadcast_to(weight, (16, rows, width)), ("z", "x"), 0, 0)
     part, *ring = lax.optimization_barrier((part, *ring))
-    before, after = shift(part, "y", 1), shift(part, "y", -1)
     last = [shift(ring[0], "x", 1), shift(ring[2], "z", 1)]
-    before, *last = lax.optimization_barrier((before, *last))
-    far = shift(before, "y", 1)
-    query_blocks = [queries, *ring[:2], last[0]]
-    passage_blocks = [passages, *ring[2:], last[1]]
-    swapped = [swap(block) for block in passage_blocks]
-    far, *swapped = lax.optimization_barrier((far, *swapped))
-    passage_blocks += swapped
-    near = jnp.stack([part, after, before])
-    near, far = (near, swap(near)), (far, swap(far))
-    c, y = lax.axis_index("c"), lax.axis_index("y")
-    pieces = []
-    for core in range(2):
-        near_one = jnp.where(c == core, near[0], near[1])
-        stacked = jnp.stack([near_one[0], near_one[1], jnp.where(c == core, far[0], far[1]), near_one[2]])
-        spots = [((1 - 2 * core) * (i - y)) % 4 for i in range(4)]
-        pieces.append(jnp.stack([lax.dynamic_index_in_dim(stacked, spot, 0, keepdims=False) for spot in spots], axis=1))
+    swapped = [swap(block) for block in (passages, *ring[2:])]
+    part = lax.all_to_all(jnp.broadcast_to(part, (4, 16, rows, width)), "y", 0, 0)
+    part, *near = lax.optimization_barrier((part, *ring, *last, *swapped))
+    query_blocks = [queries, near[0], near[1], near[4]]
+    passage_blocks = [passages, near[2], near[3], near[5]]
+    passage_blocks += near[6:] + [swap(block) for block in passage_blocks[len(near) - 6 :]]
+    other = swap(part)
+    first = lax.axis_index("c") == 0
+    pieces = [jnp.where(first, part, other), jnp.where(first, other, part)]
+    pieces = [piece.transpose(1, 0, 2, 3) for piece in pieces]
     return jnp.stack(pieces, axis=1).reshape(-1, width), query_blocks, passage_blocks
 
 
@@ -104,12 +98,12 @@
 
 
 def grad_kernel(
-    core, here, before, after, opposite, own_score, raw, emb, probs, query_sum,
+    places, here, before, after, opposite, own_score, raw, emb, probs, query_sum,
     losses, query_own, query_back, query_next, query_ahead, passage_own, passage_back, passage_next, passage_ahead,
     passage_other, mine, theirs, scaled, parts,
 ):
     rows, width = query_own.shape
-    part = 4 * rows
+    part, scale = 4 * rows, 1.0 / math.sqrt(width)
     came = (here, before, after, opposite)
     columns = []
     for block in OFFSETS:
@@ -145,21 +139,28 @@
             value = value + own_factor * emb[pl.ds(0, rows), :].astype(F32)
         out[...] = value.astype(out.dtype)
         parts[pl.ds(part + i * rows, rows), :] = value.astype(BF16)
-    first = core[0] == 0
-    for i in range(4):
-        total = dot(raw[:, pl.ds(i * width // 4, width // 4)], parts[...], FIRST)
-        for j in range(width // 256):
-            low, high = total[64 * j : 64 * j + 32], total[64 * j + 32 : 64 * j + 64]
-            span = pl.ds((i * (width // 256) + j) * 32, 32)
-            mine[span, :] = jnp.where(first, low, high)
-            theirs[span, :] = jnp.where(first, high, low).astype(BF16)
+    first = places[0] == 0
+    count = width // 256
+    for i in range(4):
+        total = scale * dot(raw[:, pl.ds(i * width // 4, width // 4)], parts[...], FIRST)
+        for j in range(4):
+            low, high = (
+                jnp.concatenate([total[64 * k + 32 * c + 8 * j : 64 * k + 32 * c + 8 * j + 8] for k in range(count)])
+                for c in range(2)
+            )
+            for out, value, spot in (
+                (mine, jnp.where(first, low, high), places[1 + j]),
+                (theirs, jnp.where(first, high, low), places[5 + j]),
+            ):
+                start = pl.multiple_of(spot * (width // 8) + i * 8 * count, 8 * count)
+                out[pl.ds(start, 8 * count), :] = value.astype(BF16)
 
 
 def local(queries, passages, weight, block_list, list_len):
     rows, width = queries.shape
     scale = 1.0 / math.sqrt(width)
     z, x, c, y = (lax.axis_index(a) for a in AXES)
-    way = 1 - 2 * c
+    way, other_way = (WAYS[i] + c * (WAYS[1 - i] - WAYS[i]) for i in range(2))
 
     full_weight, query_blocks, passage_blocks = gather_all(weight, queries, passages)
 
@@ -167,7 +168,7 @@
     lists = block_list[owners * 4 + y]
     lens = list_len[owners * 4 + y]
     blocks = jnp.stack(
-        [((z + d * o) % 4 * 4 + x) * 2 + core for core, d in ((c, way), (1 - c, -way)) for o in OFFSETS]
+        [((z + d * o) % 4 * 4 + x) * 2 + core for core, d in ((c, way), (1 - c, other_way)) for o in OFFSETS]
     )
     live = jnp.arange(lists.shape[1])[None, :] < lens[:, None]
     hit = jnp.any((lists[None, :, :] == blocks[:, None, None]) & live[None, :, :], axis=2)
@@ -193,6 +194,8 @@
     query_sum = dot(probs, emb[4 * rows :], FIRST)
     query_sum, *came = lax.optimization_barrier((query_sum, *came))
 
+    spots = [(d * (jnp.arange(4) - y)) % 4 for d in (way, other_way)]
+    places = jnp.concatenate([c[None]] + [jnp.where(o == 0, 0, jnp.where(o == 3, 1, o + 1)) for o in spots])
     low, high = shape((rows, width), BF16), shape((rows, width), F32)
     losses, *query_part, own, back, following, ahead, passage_other, mine, theirs = pl.pallas_call(
         grad_kernel,
@@ -200,7 +203,7 @@
             shape((8, 256), F32),
             *(high, low, high, low) * 2,
             shape((4 * rows, width), BF16),
-            shape((width // 2, width), F32),
+            shape((width // 2, width), BF16),
             shape((width // 2, width), BF16),
         ),
         in_specs=[pl.BlockSpec(memory_space=pltpu.SMEM)] + [pl.BlockSpec(memory_space=pltpu.VMEM)] * 9,
@@ -208,25 +211,40 @@
         compiler_params=pltpu.CompilerParams(vmem_limit_bytes=34 * 2**20),
         cost_estimate=pl.CostEstimate(flops=6 * 10**9, bytes_accessed=10**7, transcendentals=10**4),
         name="grads",
-    )(jnp.reshape(c, (1,)), stats, *came, own_score, raw, emb, probs, query_sum)
-
-    mine = (mine + swap(theirs).astype(F32)).astype(BF16)
-    weight_sum = lax.all_to_all(mine.reshape(64, -1, width), ("z", "x", "y"), 0, 0)
-    grad_weight = scale * jnp.sum(weight_sum.astype(F32), axis=0)
-
-    def finish(part, axis):
+    )(places, stats, *came, own_score, raw, emb, probs, query_sum)
+
+    def begin(part, axis):
         own, back, following, ahead = part
-        ahead, back = shift(ahead, axis, 1).astype(F32), shift(back, axis, -1).astype(F32)
-        last = shift((following + ahead).astype(BF16), axis, 1).astype(F32)
-        return dot((scale * (own + back + last)).astype(BF16), full_weight, LAST).astype(BF16)
-
-    grad_queries = finish(query_part, "x")
-    came = swap(passage_other).astype(F32)
-    own, back, following, ahead = (
-        (part.astype(F32) + came[i * rows : (i + 1) * rows]).astype(part.dtype)
-        for i, part in enumerate((own, back, following, ahead))
+        return own, shift(back, axis, -1), following, shift(ahead, axis, 1)
+
+    def go_on(part, axis):
+        own, back, following, ahead = part
+        last = shift((following + ahead.astype(F32)).astype(BF16), axis, 1)
+        return own + back.astype(F32), last
+
+    def finish(part, last):
+        return dot((scale * (part + last.astype(F32))).astype(BF16), full_weight, LAST).astype(BF16)
+
+    queries_part = begin(query_part, "x")
+    theirs, passage_other = swap(theirs), swap(passage_other)
+    weight_part = [
+        (mine[i : i + width // 8].astype(F32) + theirs[i : i + width // 8].astype(F32)).astype(kind)
+        for i, kind in zip(range(0, width // 2, width // 8), (F32, BF16, F32, BF16))
+    ]
+    weight_part[1], weight_part[3], passage_other = lax.optimization_barrier((weight_part[1], weight_part[3], passage_other))
+    weight_part = begin(weight_part, "y")
+    passages_part = begin(
+        [
+            (part.astype(F32) + passage_other[i * rows : (i + 1) * rows].astype(F32)).astype(part.dtype)
+            for i, part in enumerate((own, back, following, ahead))
+        ],
+        "z",
     )
-    grad_passages = finish((own, back, following, ahead), "z")
+    weight_sum, weight_last = go_on(weight_part, "y")
+    (query_sum, query_last), (passage_sum, passage_last) = go_on(queries_part, "x"), go_on(passages_part, "z")
+    weight_sum = (weight_sum + weight_last.astype(F32)).astype(BF16).reshape(16, -1, width)
+    grad_weight = jnp.sum(lax.all_to_all(weight_sum, ("z", "x"), 0, 0).astype(F32), axis=0)
+    grad_queries, grad_passages = finish(query_sum, query_last), finish(passage_sum, passage_last)
     return losses[0, :rows], grad_queries, grad_passages, grad_weight
 
 

time: 114 us -> 110 us (0.965)
  other arithmetic: 13.3 us -> 5.35 us
  waiting for transfers between devices: 27.5 us -> 31.7 us
  Pallas kernels: 14.1 us -> 15.8 us
    all_to_all x1 -> x2, waiting for transfers between devices: 0.01 us -> 8.76 us  [the longest x1 5.91 us: local(): lax.all_to_all(weight_sum, ('z', 'x'), 0, 0).astype(F32)]
    ppermute x18, waiting for transfers between devices: 25.6 us -> 21 us  [shift(): return lax.ppermute(value, names, pairs)]
    ppermute x18, starting transfers between devices: 22.3 us -> 18.5 us  [shift(): return lax.ppermute(value, names, pairs)]
    all_to_all x1 -> x2, starting transfers between devices: 5.52 us -> 9.06 us  [the longest x1 4.59 us: local(): lax.all_to_all(weight_sum, ('z', 'x'), 0, 0).astype(F32)]
    another operation x3 -> x0, other arithmetic: 3.39 us -> none  [the longest x1 2.09 us: gather_all(): near = jnp.stack([part, after, before])]
    convert_element_type x4 -> x5, other arithmetic: 4.21 us -> 1.47 us  [the longest x1 0.95 us: local(): (part.astype(F32) + passage_other[i * rows:(i + 1) * rows].astype(F32)).a...]
    select_n x1, other arithmetic: 1.48 us -> 0.01 us  [local(): jnp.where(o == 0, 0, jnp.where(o == 3, 1, o + 1))]
    another operation x3 -> x2, other arithmetic: 0.46 us -> 1.87 us  [gather_all(): jnp.stack(pieces, axis=1).reshape(-1, width)]
  transfers between devices with their start and end apart: 27 -> 27, of which waited for: 8 -> 12; matrix products, arithmetic and copies ran while one was open for 18% -> 13% of each run, Pallas kernels for 0% -> 0%
where the time goes in v3:
time: 110 us; the launch traced here: 109 us
  waiting for transfers between devices  31.7 us (29%)
  starting transfers between devices  29.1 us (26%)
  Pallas kernels  15.8 us (14%)
  blocking collectives  14.4 us (13%)
  matrix products  6.27 us (6%)
  local copies, waits for them, and re-layouts  5.51 us (5%)
  other arithmetic  5.35 us (5%)
    ppermute x18, waiting for transfers between devices, shift(): return lax.ppermute(value, names, pairs)  21 us
    ppermute x18, starting transfers between devices, shift(): return lax.ppermute(value, names, pairs)  18.5 us
    all_to_all x1, blocking collectives, gather_all(): lax.all_to_all(jnp.broadcast_to(weight, (16, rows, width)), ('z', 'x'), 0...  14.4 us
    pallas_call x1, Pallas kernels, local(): pl.pallas_call(score_kernel, out_shape=(shape((12 * rows, width), BF16),...  8.03 us
    pallas_call x1, Pallas kernels, local(): pl.pallas_call(grad_kernel, out_shape=(shape((8, 256), F32), *(high, low,...  7.76 us
    dot_general x3, matrix products, dot(): return lax.dot_general(a, b, dims, preferred_element_type=F32)  6.27 us
    all_to_all x1, waiting for transfers between devices, local(): lax.all_to_all(weight_sum, ('z', 'x'), 0, 0).astype(F32)  5.91 us
    all_to_all x1, starting transfers between devices, local(): lax.all_to_all(weight_sum, ('z', 'x'), 0, 0).astype(F32)  4.59 us
  transfers between devices with their start and end apart: 27, of which 12 were waited for; matrix products, arithmetic and copies ran while one was open for 13% of the time, Pallas kernels for 0%

profile of v3, /device:TPU:0, one launch (start us, length us, event | category | flops | bytes accessed | tf_op | source)
XLA Modules:
  0.0 109.1 jit_solution(11763446994841190707)
XLA Ops:
  0.7 1.6 %collective-permute-start = (bf16[160,1024]{1,0:T(8,128)(2,1)}, bf16[160,1024]{1,0:T(8,128)(2,1)S(1)}, u32[]{:S(2)}, u32[]{:S(2)}) collective-permute-start(bf16[160,1024]{1,0:T(8,128)(2,1)} %refs_0_.1), channel_id=1, source_target_pairs={{0,8},{4,28},{8,16},{12,4},{16,24},{20,12},{24,0},{28,20},{1,9},{5... | collective-permute-start | bytes 983048 | tf_op jit(solution)/shard_map/ppermute | solution.py:28
  2.3 1.7 %collective-permute-start.1 = (bf16[160,1024]{1,0:T(8,128)(2,1)}, bf16[160,1024]{1,0:T(8,128)(2,1)S(1)}, u32[]{:S(2)}, u32[]{:S(2)}) collective-permute-start(bf16[160,1024]{1,0:T(8,128)(2,1)} %refs_0_.1), channel_id=1, source_target_pairs={{0,24},{4,12},{8,0},{12,20},{16,8},{20,28},{24,16},{28,4},{1,25},{... | collective-permute-start | bytes 983048 | tf_op jit(solution)/shard_map/ppermute | solution.py:28
  4.0 4.1 %collective-permute-start.3 = (bf16[160,1024]{1,0:T(8,128)(2,1)}, bf16[160,1024]{1,0:T(8,128)(2,1)S(1)}, u32[]{:S(2)}, u32[]{:S(2)}) collective-permute-start(bf16[160,1024]{1,0:T(8,128)(2,1)} %refs_4_.1), channel_id=1, source_target_pairs={{0,96},{4,36},{32,0},{36,68},{64,32},{68,100},{96,64},{100,4},{1,9... | collective-permute-start | bytes 983048 | tf_op jit(solution)/shard_map/ppermute | solution.py:28
  8.1 0.7 broadcast_in_dim.28
  8.8 14.4 %all_to_all.15 = bf16[16,8,1024]{2,1,0:T(8,128)(2,1)S(1)} all-to-all(bf16[16,8,1024]{2,1,0:T(8,128)(2,1)S(1)} %broadcast_in_dim.28), channel_id=1, replica_groups=mesh['z'=4,'x'=4,'c'=2,'y'=4] {'z','x'}, dimensions={0} | all-to-all | bytes 524288 | tf_op jit(solution)/shard_map/all_to_all | solution.py:47
  23.2 1.1 %broadcast_in_dim.29 = bf16[4,16,8,1024]{3,2,1,0:T(8,128)(2,1)} broadcast(bf16[16,8,1024]{2,1,0:T(8,128)(2,1)S(1)} %all_to_all.15), dimensions={1,2,3} | broadcast | bytes 1310720 | tf_op jit(solution)/shard_map/broadcast_in_dim | solution.py:51
  24.4 4.5 %all-to-all-start.1 = ((bf16[4,16,8,1024]{3,2,1,0:T(8,128)(2,1)}), bf16[4,16,8,1024]{3,2,1,0:T(8,128)(2,1)}, u32[]{:S(2)}, u32[]{:S(2)}) async-start(bf16[4,16,8,1024]{3,2,1,0:T(8,128)(2,1)} %broadcast_in_dim.29), calls=%async_computation.1 | async-start | bytes 2097152 | tf_op jit(solution)/shard_map/all_to_all | solution.py:51
  28.8 0.6 collective-permute-start.4
  29.5 0.3 collective-permute-start.8
  29.8 0.2 collective-permute-start.7
  30.0 0.3 collective-permute-start.5
  30.3 0.2 collective-permute-done.6.refs_8_
  30.4 6.7 %collective-permute-done.4.refs_3_ = bf16[160,1024]{1,0:T(8,128)(2,1)S(1)} collective-permute-done((bf16[160,1024]{1,0:T(8,128)(2,1)S(1)}, bf16[160,1024]{1,0:T(8,128)(2,1)S(1)}, u32[]{:S(2)}, u32[]{:S(2)}) %collective-permute-start.4) | collective-permute-done | bytes 327712 | tf_op jit(solution)/shard_map/ppermute | solution.py:28
  37.2 1.2 %collective-permute-done.5.refs_7_ = bf16[160,1024]{1,0:T(8,128)(2,1)} collective-permute-done((bf16[160,1024]{1,0:T(8,128)(2,1)S(1)}, bf16[160,1024]{1,0:T(8,128)(2,1)}, u32[]{:S(2)}, u32[]{:S(2)}) %collective-permute-start.5) | collective-permute-done | bytes 327712 | tf_op jit(solution)/shard_map/ppermute | solution.py:28
  38.4 2.9 %all-to-all-done.1 = bf16[4,16,8,1024]{3,2,1,0:T(8,128)(2,1)} async-done(((bf16[4,16,8,1024]{3,2,1,0:T(8,128)(2,1)}), bf16[4,16,8,1024]{3,2,1,0:T(8,128)(2,1)}, u32[]{:S(2)}, u32[]{:S(2)}) %all-to-all-start.1) | async-done | bytes 1048608 | tf_op jit(solution)/shard_map/all_to_all | solution.py:51
  41.2 0.1 copy.16
  41.3 0.1 fusion.8
  41.4 0.6 gather_fusion.1
  42.1 0.6 gather_fusion
  42.6 0.1 stack.67
  42.8 0.2 and_reduce_fusion
  43.2 0.1 reshape.109.refs_13_
  43.4 0.5 collective-permute-start.9
  43.9 0.3 collective-permute-done.10
  44.2 1.7 %select_bitcast_fusion.1 = (bf16[16,1,4,8,1024]{4,3,0,2,1:T(8,128)(2,1)S(1)}, bf16[16,1,4,8,1024]{4,3,0,2,1:T(8,128)(2,1)S(1)}) fusion(bf16[4,16,8,1024]{3,2,1,0:T(8,128)(2,1)} %all-to-all-done.1, bf16[4,16,8,1024]{3,2,1,0:T(8,128)(2,1)} %collective-permute-done.10, pred[]{:T(512)S(6)} %eq.48), kind=kLoop, calls=%fused_computation.8 | loop fusion | flops 1048576 | bytes 4194305 | tf_op jit(solution)/shard_map/stack | solution.py:60
  45.9 0.2 pad_maximum_fusion
  46.2 0.2 copy.15
  46.4 0.7 copy-done.1
  47.1 0.1 copy-done.4
  47.2 0.1 copy-done.6
  47.3 0.1 copy-done.8
  47.4 0.1 copy-done.10
  47.5 0.1 copy-done.12
  47.6 8.0 %scores.1 = (bf16[1920,1024]{1,0:T(8,128)(2,1)S(1)}, bf16[1920,1024]{1,0:T(8,128)(2,1)S(1)}, bf16[1280,640]{1,0:T(8,128)(2,1)S(1)}, f32[8,256]{1,0:T(8,128)S(1)}, f32[8,256]{1,0:T(8,128)S(1)}) custom-call(bf16[160,1024]{1,0:T(8,128)(2,1)S(1)} %copy-done.1, bf16[160,1024]{1,0:T(8,128)(2,1)S(1)} %collective-permute-done.refs_1_, ...), custom_call_target="tpu_custom_call" | custom-call | flops 6000000000 | bytes 10000000 | tf_op jit(solution)/shard_map/scores/pallas_call | solution.py:178
  55.6 0.9 collective-permute-start.13
  56.6 2.3 %collective-permute-start.12 = (f32[8,256]{1,0:T(8,128)S(1)}, f32[8,256]{1,0:T(8,128)S(1)}, u32[]{:S(2)}, u32[]{:S(2)}) collective-permute-start(f32[8,256]{1,0:T(8,128)S(1)} %get-tuple-element.58.here), channel_id=1, source_target_pairs={{0,24},{4,12},{8,0},{12,20},{16,8},{20,28},{24,16},{28,4},{1,25},{... | collective-permute-start | bytes 24584 | tf_op jit(solution)/shard_map/ppermute | solution.py:28
  58.9 1.9 %fusion.query_sum = f32[640,1024]{1,0:T(8,128)S(1)} fusion(bf16[1280,640]{1,0:T(8,128)(2,1)S(1)} %get-tuple-element.59.probs, bf16[1920,1024]{1,0:T(8,128)(2,1)S(1)} %get-tuple-element.60.emb), kind=kOutput, calls=%fused_computation.2 | convolution fusion | flops 1677721600 | bytes 6881280 | tf_op jit(solution)/shard_map/dot_general | solution.py:41
  60.9 2.9 %collective-permute-done.11.before = f32[8,256]{1,0:T(8,128)S(1)} collective-permute-done((f32[8,256]{1,0:T(8,128)S(1)}, f32[8,256]{1,0:T(8,128)S(1)}, u32[]{:S(2)}, u32[]{:S(2)}) %collective-permute-start.11) | collective-permute-done | bytes 8224 | tf_op jit(solution)/shard_map/ppermute | solution.py:28
  63.8 7.8 %grads.1 = (f32[8,256]{1,0:T(8,128)S(1)}, f32[160,1024]{1,0:T(8,128)S(1)}, bf16[160,1024]{1,0:T(8,128)(2,1)S(1)}, f32[160,1024]{1,0:T(8,128)S(1)}, bf16[160,1024...) custom-call(s32[9]{0:T(128)S(1)} %pad_add_fusion.places, ...), custom_call_target="tpu_custom_call" | custom-call | flops 6000000000 | bytes 10000000 | tf_op jit(solution)/shard_map/grads/pallas_call | solution.py:200
  71.5 0.1 collective-permute-start.18
  71.6 0.5 collective-permute-start.17
  72.1 0.6 slice.43
  72.7 0.4 collective-permute-start.14
  73.0 1.7 %collective-permute-start.15 = (bf16[160,1024]{1,0:T(8,128)(2,1)S(1)}, bf16[160,1024]{1,0:T(8,128)(2,1)S(1)}, u32[]{:S(2)}, u32[]{:S(2)}) collective-permute-start(bf16[160,1024]{1,0:T(8,128)(2,1)S(1)} %get-tuple-element.71), channel_id=1, source_target_pairs={{0,8},{4,28},{8,16},{12,4},{16,24},{20,12},{24,0},{28,20},{1,9},{5... | collective-permute-start | bytes 983048 | tf_op jit(solution)/shard_map/ppermute | solution.py:28
  74.7 1.4 %collective-permute-done.17 = bf16[512,1024]{1,0:T(8,128)(2,1)S(1)} collective-permute-done((bf16[512,1024]{1,0:T(8,128)(2,1)S(1)}, bf16[512,1024]{1,0:T(8,128)(2,1)S(1)}, u32[]{:S(2)}, u32[]{:S(2)}) %collective-permute-start.17) | collective-permute-done | bytes 1048608 | tf_op jit(solution)/shard_map/ppermute | solution.py:21
  76.1 0.2 add_convert_fusion.6
  76.4 0.7 collective-permute-start.23
  77.1 1.0 add_convert_fusion.2
  78.0 5.6 %collective-permute-done.15 = bf16[160,1024]{1,0:T(8,128)(2,1)S(1)} collective-permute-done((bf16[160,1024]{1,0:T(8,128)(2,1)S(1)}, bf16[160,1024]{1,0:T(8,128)(2,1)S(1)}, u32[]{:S(2)}, u32[]{:S(2)}) %collective-permute-start.15) | collective-permute-done | bytes 327712 | tf_op jit(solution)/shard_map/ppermute | solution.py:28
  83.8 1.3 %collective-permute-start.22 = (bf16[128,1024]{1,0:T(8,128)(2,1)S(1)}, bf16[128,1024]{1,0:T(8,128)(2,1)S(1)}, u32[]{:S(2)}, u32[]{:S(2)}) collective-permute-start(bf16[128,1024]{1,0:T(8,128)(2,1)S(1)} %get-tuple-element.80), channel_id=1, source_target_pairs={{0,3},{4,5},{1,0},{5,6},{2,1},{6,7},{3,2},{7,4},{8,11},{12,13},{9,... | collective-permute-start | bytes 786440 | tf_op jit(solution)/shard_map/ppermute | solution.py:28
  85.0 0.9 collective-permute-start.19
  85.9 0.1 add_convert_fusion.5
  86.0 0.3 collective-permute-done.20
  86.3 0.6 collective-permute-start.24
  86.9 0.1 add_convert_fusion
  87.1 1.2 %collective-permute-start.21 = (bf16[160,1024]{1,0:T(8,128)(2,1)S(1)}, bf16[160,1024]{1,0:T(8,128)(2,1)}, u32[]{:S(2)}, u32[]{:S(2)}) collective-permute-start(bf16[160,1024]{1,0:T(8,128)(2,1)S(1)} %add_convert_fusion), channel_id=1, source_target_pairs={{0,32},{4,100},{32,64},{36,4},{64,96},{68,36},{96,0},{100,68},{1,3... | collective-permute-start | bytes 983048 | tf_op jit(solution)/shard_map/ppermute | solution.py:28
  88.3 3.7 %collective-permute-done.16 = bf16[160,1024]{1,0:T(8,128)(2,1)S(1)} collective-permute-done((bf16[160,1024]{1,0:T(8,128)(2,1)S(1)}, bf16[160,1024]{1,0:T(8,128)(2,1)S(1)}, u32[]{:S(2)}, u32[]{:S(2)}) %collective-permute-start.16) | collective-permute-done | bytes 327712 | tf_op jit(solution)/shard_map/ppermute | solution.py:28
  92.0 1.6 %convolution_convert_fusion.1 = bf16[160,1024]{1,0:T(8,128)(2,1)} fusion(bf16[1024,1024]{1,0:T(8,128)(2,1)S(1)} %bitcast.31, bf16[160,1024]{1,0:T(8,128)(2,1)S(1)} %collective-permute-done.16, f32[160,1024]{1,0:T(8,128)S(1)} %get-tuple-element.68, bf16[160,1024]{1,0:T(8,128)(2,1)S(1)} %collective-permute-done.14), kind=kOutput, calls=%fused_computation.6 | convolution fusion | flops 336691200 | bytes 3735552 | tf_op jit(solution)/shard_map/dot_general | solution.py:41
  93.6 0.6 collective-permute-done.24
  94.2 0.9 fusion.5
  95.1 4.6 %all-to-all-start.2 = ((bf16[16,8,1024]{2,1,0:T(8,128)(2,1)}), bf16[16,8,1024]{2,1,0:T(8,128)(2,1)S(1)}, u32[]{:S(2)}, u32[]{:S(2)}) async-start(bf16[16,8,1024]{2,1,0:T(8,128)(2,1)} %fusion.5), calls=%async_computation.2 | async-start | bytes 524288 | tf_op jit(solution)/shard_map/all_to_all | solution.py:246
  99.7 2.8 %convolution_convert_fusion = bf16[160,1024]{1,0:T(8,128)(2,1)} fusion(bf16[1024,1024]{1,0:T(8,128)(2,1)S(1)} %bitcast.32, bf16[160,1024]{1,0:T(8,128)(2,1)} %collective-permute-done.21, bf16[160,1024]{1,0:T(8,128)(2,1)} %collective-permute-done.19, f32[160,1024]{1,0:T(8,128)S(1)} %get-tuple-element.72, bf16[640,1024]{1,0:T(8,128)(2,1)} %copy-done.13), kind=kOutput, calls=%fused_computation.5 | convolution fusion | flops 337018880 | bytes 4063232 | tf_op jit(solution)/shard_map/dot_general | solution.py:41
  102.5 5.9 %all-to-all-done.2 = bf16[16,8,1024]{2,1,0:T(8,128)(2,1)S(1)} async-done(((bf16[16,8,1024]{2,1,0:T(8,128)(2,1)}), bf16[16,8,1024]{2,1,0:T(8,128)(2,1)S(1)}, u32[]{:S(2)}, u32[]{:S(2)}) %all-to-all-start.2) | async-done | bytes 262176 | tf_op jit(solution)/shard_map/all_to_all | solution.py:246
  108.4 0.7 convert_reduce_fusion
  (53 shorter events, 0.6 us)
Async XLA Ops:
  0.6 40.8 %copy-start = (s32[128]{0:T(128)S(1)}, s32[128]{0:T(128)}, u32[]{:S(2)}) copy-start(s32[128]{0:T(128)} %param.9) | copy-start | bytes 1540
  0.6 28.2 %copy-start.2 = (bf16[160,1024]{1,0:T(8,128)(2,1)S(1)}, bf16[160,1024]{1,0:T(8,128)(2,1)}, u32[]{:S(2)}) copy-start(bf16[160,1024]{1,0:T(8,128)(2,1)} %refs_4_.1) | copy-start | bytes 983044
  0.7 22.5 %collective-permute-start = (bf16[160,1024]{1,0:T(8,128)(2,1)}, bf16[160,1024]{1,0:T(8,128)(2,1)S(1)}, u32[]{:S(2)}, u32[]{:S(2)}) collective-permute-start(bf16[160,1024]{1,0:T(8,128)(2,1)} %refs_0_.1), channel_id=1, source_target_pairs={{0,8},{4,28},{8,16},{12,4},{16,24},{20,12},{24,0},{28,20},{1,9},{5... | collective-permute-start | bytes 983048 | tf_op jit(solution)/shard_map/ppermute | solution.py:28
  2.3 20.9 %collective-permute-start.1 = (bf16[160,1024]{1,0:T(8,128)(2,1)}, bf16[160,1024]{1,0:T(8,128)(2,1)S(1)}, u32[]{:S(2)}, u32[]{:S(2)}) collective-permute-start(bf16[160,1024]{1,0:T(8,128)(2,1)} %refs_0_.1), channel_id=1, source_target_pairs={{0,24},{4,12},{8,0},{12,20},{16,8},{20,28},{24,16},{28,4},{1,25},{... | collective-permute-start | bytes 983048 | tf_op jit(solution)/shard_map/ppermute | solution.py:28
  4.0 19.2 %collective-permute-start.3 = (bf16[160,1024]{1,0:T(8,128)(2,1)}, bf16[160,1024]{1,0:T(8,128)(2,1)S(1)}, u32[]{:S(2)}, u32[]{:S(2)}) collective-permute-start(bf16[160,1024]{1,0:T(8,128)(2,1)} %refs_4_.1), channel_id=1, source_target_pairs={{0,96},{4,36},{32,0},{36,68},{64,32},{68,100},{96,64},{100,4},{1,9... | collective-permute-start | bytes 983048 | tf_op jit(solution)/shard_map/ppermute | solution.py:28
  8.1 15.1 %collective-permute-start.2 = (bf16[160,1024]{1,0:T(8,128)(2,1)}, bf16[160,1024]{1,0:T(8,128)(2,1)S(1)}, u32[]{:S(2)}, u32[]{:S(2)}) collective-permute-start(bf16[160,1024]{1,0:T(8,128)(2,1)} %refs_4_.1), channel_id=1, source_target_pairs={{0,32},{4,100},{32,64},{36,4},{64,96},{68,36},{96,0},{100,68},{1,3... | collective-permute-start | bytes 983048 | tf_op jit(solution)/shard_map/ppermute | solution.py:28
  8.8 32.4 %copy-start.14 = (s32[128,32]{0,1:T(8,128)S(1)}, s32[128,32]{0,1:T(8,128)}, u32[]{:S(2)}) copy-start(s32[128,32]{0,1:T(8,128)} %param.8) | copy-start | bytes 49156
  23.2 18.8 %copy-start.3 = (bf16[160,1024]{1,0:T(8,128)(2,1)}, bf16[160,1024]{1,0:T(8,128)(2,1)S(1)}, u32[]{:S(2)}) copy-start(bf16[160,1024]{1,0:T(8,128)(2,1)S(1)} %collective-permute-done.2.refs_5_) | copy-start | bytes 983044
  24.4 16.9 %all-to-all-start.1 = ((bf16[4,16,8,1024]{3,2,1,0:T(8,128)(2,1)}), bf16[4,16,8,1024]{3,2,1,0:T(8,128)(2,1)}, u32[]{:S(2)}, u32[]{:S(2)}) async-start(bf16[4,16,8,1024]{3,2,1,0:T(8,128)(2,1)} %broadcast_in_dim.29), calls=%async_computation.1 | async-start | bytes 2097152 | tf_op jit(solution)/shard_map/all_to_all | solution.py:51
  28.8 1.6 %collective-permute-start.6 = (bf16[160,1024]{1,0:T(8,128)(2,1)S(1)}, bf16[160,1024]{1,0:T(8,128)(2,1)S(1)}, u32[]{:S(2)}, u32[]{:S(2)}) collective-permute-start(bf16[160,1024]{1,0:T(8,128)(2,1)S(1)} %copy-done.2), channel_id=1, source_target_pairs={{0,4},{4,0},{1,5},{5,1},{2,6},{6,2},{3,7},{7,3},{8,12},{12,8},{9,1... | collective-permute-start | bytes 983048 | tf_op jit(solution)/shard_map/ppermute | solution.py:21
  28.8 8.4 %collective-permute-start.4 = (bf16[160,1024]{1,0:T(8,128)(2,1)S(1)}, bf16[160,1024]{1,0:T(8,128)(2,1)S(1)}, u32[]{:S(2)}, u32[]{:S(2)}) collective-permute-start(bf16[160,1024]{1,0:T(8,128)(2,1)S(1)} %collective-permute-done.refs_1_), channel_id=1, source_target_pairs={{0,8},{4,28},{8,16},{12,4},{16,24},{20,12},{24,0},{28,20},{1,9},{5... | collective-permute-start | bytes 983048 | tf_op jit(solution)/shard_map/ppermute | solution.py:28
  29.5 7.7 %collective-permute-start.8 = (bf16[160,1024]{1,0:T(8,128)(2,1)S(1)}, bf16[160,1024]{1,0:T(8,128)(2,1)S(1)}, u32[]{:S(2)}, u32[]{:S(2)}) collective-permute-start(bf16[160,1024]{1,0:T(8,128)(2,1)S(1)} %collective-permute-done.3.refs_6_), channel_id=1, source_target_pairs={{0,4},{4,0},{1,5},{5,1},{2,6},{6,2},{3,7},{7,3},{8,12},{12,8},{9,1... | collective-permute-start | bytes 983048 | tf_op jit(solution)/shard_map/ppermute | solution.py:21
  29.8 7.4 %collective-permute-start.7 = (bf16[160,1024]{1,0:T(8,128)(2,1)S(1)}, bf16[160,1024]{1,0:T(8,128)(2,1)S(1)}, u32[]{:S(2)}, u32[]{:S(2)}) collective-permute-start(bf16[160,1024]{1,0:T(8,128)(2,1)S(1)} %collective-permute-done.2.refs_5_), channel_id=1, source_target_pairs={{0,4},{4,0},{1,5},{5,1},{2,6},{6,2},{3,7},{7,3},{8,12},{12,8},{9,1... | collective-permute-start | bytes 983048 | tf_op jit(solution)/shard_map/ppermute | solution.py:21
  30.0 8.4 %collective-permute-start.5 = (bf16[160,1024]{1,0:T(8,128)(2,1)S(1)}, bf16[160,1024]{1,0:T(8,128)(2,1)}, u32[]{:S(2)}, u32[]{:S(2)}) collective-permute-start(bf16[160,1024]{1,0:T(8,128)(2,1)S(1)} %collective-permute-done.2.refs_5_), channel_id=1, source_target_pairs={{0,32},{4,100},{32,64},{36,4},{64,96},{68,36},{96,0},{100,68},{1,3... | collective-permute-start | bytes 983048 | tf_op jit(solution)/shard_map/ppermute | solution.py:28
  30.4 15.5 %copy-start.5 = (bf16[160,1024]{1,0:T(8,128)(2,1)}, bf16[160,1024]{1,0:T(8,128)(2,1)S(1)}, u32[]{:S(2)}) copy-start(bf16[160,1024]{1,0:T(8,128)(2,1)S(1)} %collective-permute-done.6.refs_8_) | copy-start | bytes 983044
  37.2 8.7 %copy-start.7 = (bf16[160,1024]{1,0:T(8,128)(2,1)}, bf16[160,1024]{1,0:T(8,128)(2,1)S(1)}, u32[]{:S(2)}) copy-start(bf16[160,1024]{1,0:T(8,128)(2,1)S(1)} %collective-permute-done.4.refs_3_) | copy-start | bytes 983044
  37.2 8.7 %copy-start.9 = (bf16[160,1024]{1,0:T(8,128)(2,1)}, bf16[160,1024]{1,0:T(8,128)(2,1)S(1)}, u32[]{:S(2)}) copy-start(bf16[160,1024]{1,0:T(8,128)(2,1)S(1)} %collective-permute-done.8.refs_10_) | copy-start | bytes 983044
  37.2 8.7 %copy-start.11 = (bf16[160,1024]{1,0:T(8,128)(2,1)}, bf16[160,1024]{1,0:T(8,128)(2,1)S(1)}, u32[]{:S(2)}) copy-start(bf16[160,1024]{1,0:T(8,128)(2,1)S(1)} %collective-permute-done.7.refs_9_) | copy-start | bytes 983044
  41.2 3.0 %collective-permute-start.10 = (bf16[4,16,8,1024]{3,2,1,0:T(8,128)(2,1)}, bf16[4,16,8,1024]{3,2,1,0:T(8,128)(2,1)}, u32[]{:S(2)}, u32[]{:S(2)}) collective-permute-start(bf16[4,16,8,1024]{3,2,1,0:T(8,128)(2,1)} %all-to-all-done.1), channel_id=1, source_target_pairs={{0,4},{4,0},{1,5},{5,1},{2,6},{6,2},{3,7},{7,3},{8,12},{12,8},{9,1... | collective-permute-start | bytes 3145736 | tf_op jit(solution)/shard_map/ppermute | solution.py:21
  43.4 3.1 %collective-permute-start.9 = (bf16[160,1024]{1,0:T(8,128)(2,1)}, bf16[160,1024]{1,0:T(8,128)(2,1)S(1)}, u32[]{:S(2)}, u32[]{:S(2)}) collective-permute-start(bf16[160,1024]{1,0:T(8,128)(2,1)} %collective-permute-done.5.refs_7_), channel_id=1, source_target_pairs={{0,4},{4,0},{1,5},{5,1},{2,6},{6,2},{3,7},{7,3},{8,12},{12,8},{9,1... | collective-permute-start | bytes 983048 | tf_op jit(solution)/shard_map/ppermute | solution.py:21
  46.1 1.0 copy-start.1
  46.2 1.1 copy-start.4
  46.2 1.2 %copy-start.6 = (bf16[160,1024]{1,0:T(8,128)(2,1)S(1)}, bf16[160,1024]{1,0:T(8,128)(2,1)}, u32[]{:S(2)}) copy-start(bf16[160,1024]{1,0:T(8,128)(2,1)} %copy-done.5) | copy-start | bytes 983044
  46.2 1.2 %copy-start.8 = (bf16[160,1024]{1,0:T(8,128)(2,1)S(1)}, bf16[160,1024]{1,0:T(8,128)(2,1)}, u32[]{:S(2)}) copy-start(bf16[160,1024]{1,0:T(8,128)(2,1)} %copy-done.7) | copy-start | bytes 983044
  46.2 1.3 %copy-start.10 = (bf16[160,1024]{1,0:T(8,128)(2,1)S(1)}, bf16[160,1024]{1,0:T(8,128)(2,1)}, u32[]{:S(2)}) copy-start(bf16[160,1024]{1,0:T(8,128)(2,1)} %copy-done.9) | copy-start | bytes 983044
  46.2 1.4 %copy-start.12 = (bf16[160,1024]{1,0:T(8,128)(2,1)S(1)}, bf16[160,1024]{1,0:T(8,128)(2,1)}, u32[]{:S(2)}) copy-start(bf16[160,1024]{1,0:T(8,128)(2,1)} %copy-done.11) | copy-start | bytes 983044
  55.6 5.2 %collective-permute-start.13 = (f32[8,256]{1,0:T(8,128)S(1)}, f32[8,256]{1,0:T(8,128)S(1)}, u32[]{:S(2)}, u32[]{:S(2)}) collective-permute-start(f32[8,256]{1,0:T(8,128)S(1)} %get-tuple-element.58.here), channel_id=1, source_target_pairs={{0,16},{4,20},{8,24},{12,28},{16,0},{20,4},{24,8},{28,12},{1,17},{... | collective-permute-start | bytes 24584 | tf_op jit(solution)/shard_map/ppermute | solution.py:28
  56.6 4.3 %collective-permute-start.12 = (f32[8,256]{1,0:T(8,128)S(1)}, f32[8,256]{1,0:T(8,128)S(1)}, u32[]{:S(2)}, u32[]{:S(2)}) collective-permute-start(f32[8,256]{1,0:T(8,128)S(1)} %get-tuple-element.58.here), channel_id=1, source_target_pairs={{0,24},{4,12},{8,0},{12,20},{16,8},{20,28},{24,16},{28,4},{1,25},{... | collective-permute-start | bytes 24584 | tf_op jit(solution)/shard_map/ppermute | solution.py:28
  58.9 4.9 %collective-permute-start.11 = (f32[8,256]{1,0:T(8,128)S(1)}, f32[8,256]{1,0:T(8,128)S(1)}, u32[]{:S(2)}, u32[]{:S(2)}) collective-permute-start(f32[8,256]{1,0:T(8,128)S(1)} %get-tuple-element.58.here), channel_id=1, source_target_pairs={{0,8},{4,28},{8,16},{12,4},{16,24},{20,12},{24,0},{28,20},{1,9},{5... | collective-permute-start | bytes 24584 | tf_op jit(solution)/shard_map/ppermute | solution.py:28
  71.5 4.8 %collective-permute-start.18 = (bf16[640,1024]{1,0:T(8,128)(2,1)S(1)}, bf16[640,1024]{1,0:T(8,128)(2,1)S(1)}, u32[]{:S(2)}, u32[]{:S(2)}) collective-permute-start(bf16[640,1024]{1,0:T(8,128)(2,1)S(1)} %get-tuple-element.75), channel_id=1, source_target_pairs={{0,4},{4,0},{1,5},{5,1},{2,6},{6,2},{3,7},{7,3},{8,12},{12,8},{9,1... | collective-permute-start | bytes 3932168 | tf_op jit(solution)/shard_map/ppermute | solution.py:21
  71.6 4.5 %collective-permute-start.17 = (bf16[512,1024]{1,0:T(8,128)(2,1)S(1)}, bf16[512,1024]{1,0:T(8,128)(2,1)S(1)}, u32[]{:S(2)}, u32[]{:S(2)}) collective-permute-start(bf16[512,1024]{1,0:T(8,128)(2,1)S(1)} %get-tuple-element.74), channel_id=1, source_target_pairs={{0,4},{4,0},{1,5},{5,1},{2,6},{6,2},{3,7},{7,3},{8,12},{12,8},{9,1... | collective-permute-start | bytes 3145736 | tf_op jit(solution)/shard_map/ppermute | solution.py:21
  72.7 14.4 %collective-permute-start.14 = (bf16[160,1024]{1,0:T(8,128)(2,1)S(1)}, bf16[160,1024]{1,0:T(8,128)(2,1)S(1)}, u32[]{:S(2)}, u32[]{:S(2)}) collective-permute-start(bf16[160,1024]{1,0:T(8,128)(2,1)S(1)} %get-tuple-element.69), channel_id=1, source_target_pairs={{0,24},{4,12},{8,0},{12,20},{16,8},{20,28},{24,16},{28,4},{1,25},{... | collective-permute-start | bytes 983048 | tf_op jit(solution)/shard_map/ppermute | solution.py:28
  73.0 10.6 %collective-permute-start.15 = (bf16[160,1024]{1,0:T(8,128)(2,1)S(1)}, bf16[160,1024]{1,0:T(8,128)(2,1)S(1)}, u32[]{:S(2)}, u32[]{:S(2)}) collective-permute-start(bf16[160,1024]{1,0:T(8,128)(2,1)S(1)} %get-tuple-element.71), channel_id=1, source_target_pairs={{0,8},{4,28},{8,16},{12,4},{16,24},{20,12},{24,0},{28,20},{1,9},{5... | collective-permute-start | bytes 983048 | tf_op jit(solution)/shard_map/ppermute | solution.py:28
  76.4 17.3 %copy-start.13 = (bf16[640,1024]{1,0:T(8,128)(2,1)}, bf16[640,1024]{1,0:T(8,128)(2,1)S(1)}, u32[]{:S(2)}) copy-start(bf16[640,1024]{1,0:T(8,128)(2,1)S(1)} %collective-permute-done.18) | copy-start | bytes 3932164
  76.4 8.7 %collective-permute-start.23 = (bf16[128,1024]{1,0:T(8,128)(2,1)S(1)}, bf16[128,1024]{1,0:T(8,128)(2,1)S(1)}, u32[]{:S(2)}, u32[]{:S(2)}) collective-permute-start(bf16[128,1024]{1,0:T(8,128)(2,1)S(1)} %get-tuple-element.81), channel_id=1, source_target_pairs={{0,1},{4,7},{1,2},{5,4},{2,3},{6,5},{3,0},{7,6},{8,9},{12,15},{9,1... | collective-permute-start | bytes 786440 | tf_op jit(solution)/shard_map/ppermute | solution.py:28
  78.0 8.3 %collective-permute-start.20 = (bf16[160,1024]{1,0:T(8,128)(2,1)S(1)}, bf16[160,1024]{1,0:T(8,128)(2,1)S(1)}, u32[]{:S(2)}, u32[]{:S(2)}) collective-permute-start(bf16[160,1024]{1,0:T(8,128)(2,1)S(1)} %get-tuple-element.87), channel_id=1, source_target_pairs={{0,32},{4,100},{32,64},{36,4},{64,96},{68,36},{96,0},{100,68},{1,3... | collective-permute-start | bytes 983048 | tf_op jit(solution)/shard_map/ppermute | solution.py:28
  83.7 8.4 %collective-permute-start.16 = (bf16[160,1024]{1,0:T(8,128)(2,1)S(1)}, bf16[160,1024]{1,0:T(8,128)(2,1)S(1)}, u32[]{:S(2)}, u32[]{:S(2)}) collective-permute-start(bf16[160,1024]{1,0:T(8,128)(2,1)S(1)} %add_convert_fusion.3), channel_id=1, source_target_pairs={{0,8},{4,28},{8,16},{12,4},{16,24},{20,12},{24,0},{28,20},{1,9},{5... | collective-permute-start | bytes 983048 | tf_op jit(solution)/shard_map/ppermute | solution.py:28
  83.8 9.9 %collective-permute-start.22 = (bf16[128,1024]{1,0:T(8,128)(2,1)S(1)}, bf16[128,1024]{1,0:T(8,128)(2,1)S(1)}, u32[]{:S(2)}, u32[]{:S(2)}) collective-permute-start(bf16[128,1024]{1,0:T(8,128)(2,1)S(1)} %get-tuple-element.80), channel_id=1, source_target_pairs={{0,3},{4,5},{1,0},{5,6},{2,1},{6,7},{3,2},{7,4},{8,11},{12,13},{9,... | collective-permute-start | bytes 786440 | tf_op jit(solution)/shard_map/ppermute | solution.py:28
  85.0 14.7 %collective-permute-start.19 = (bf16[160,1024]{1,0:T(8,128)(2,1)}, bf16[160,1024]{1,0:T(8,128)(2,1)}, u32[]{:S(2)}, u32[]{:S(2)}) collective-permute-start(bf16[160,1024]{1,0:T(8,128)(2,1)} %get-tuple-element.86), channel_id=1, source_target_pairs={{0,96},{4,36},{32,0},{36,68},{64,32},{68,100},{96,64},{100,4},{1,9... | collective-permute-start | bytes 983048 | tf_op jit(solution)/shard_map/ppermute | solution.py:28
  86.3 7.9 %collective-permute-start.24 = (bf16[128,1024]{1,0:T(8,128)(2,1)S(1)}, bf16[128,1024]{1,0:T(8,128)(2,1)S(1)}, u32[]{:S(2)}, u32[]{:S(2)}) collective-permute-start(bf16[128,1024]{1,0:T(8,128)(2,1)S(1)} %add_convert_fusion.5), channel_id=1, source_target_pairs={{0,1},{4,7},{1,2},{5,4},{2,3},{6,5},{3,0},{7,6},{8,9},{12,15},{9,1... | collective-permute-start | bytes 786440 | tf_op jit(solution)/shard_map/ppermute | solution.py:28
  87.1 12.6 %collective-permute-start.21 = (bf16[160,1024]{1,0:T(8,128)(2,1)S(1)}, bf16[160,1024]{1,0:T(8,128)(2,1)}, u32[]{:S(2)}, u32[]{:S(2)}) collective-permute-start(bf16[160,1024]{1,0:T(8,128)(2,1)S(1)} %add_convert_fusion), channel_id=1, source_target_pairs={{0,32},{4,100},{32,64},{36,4},{64,96},{68,36},{96,0},{100,68},{1,3... | collective-permute-start | bytes 983048 | tf_op jit(solution)/shard_map/ppermute | solution.py:28
  95.1 13.3 %all-to-all-start.2 = ((bf16[16,8,1024]{2,1,0:T(8,128)(2,1)}), bf16[16,8,1024]{2,1,0:T(8,128)(2,1)S(1)}, u32[]{:S(2)}, u32[]{:S(2)}) async-start(bf16[16,8,1024]{2,1,0:T(8,128)(2,1)} %fusion.5), calls=%async_computation.2 | async-start | bytes 524288 | tf_op jit(solution)/shard_map/all_to_all | solution.py:246

commit v4 on v3

--- a/solution.py
+++ b/solution.py
@@ -43,11 +43,12 @@
 
 def gather_all(weight, queries, passages):
     rows, width = weight.shape
-    ring = [shift(queries, "x", 1), shift(queries, "x", -1), shift(passages, "z", 1), shift(passages, "z", -1)]
+    ring = [shift(queries, "x", 1), shift(passages, "z", 1), shift(passages, "z", -1)]
     part = lax.all_to_all(jnp.broadcast_to(weight, (16, rows, width)), ("z", "x"), 0, 0)
-    part, *ring = lax.optimization_barrier((part, *ring))
+    part, queries, *ring = lax.optimization_barrier((part, queries, *ring))
+    ring = [ring[0], shift(queries, "x", -1), *ring[1:]]
     last = [shift(ring[0], "x", 1), shift(ring[2], "z", 1)]
-    swapped = [swap(block) for block in (passages, *ring[2:])]
+    swapped = [swap(block) for block in (passages, ring[2])]
     part = lax.all_to_all(jnp.broadcast_to(part, (4, 16, rows, width)), "y", 0, 0)
     part, *near = lax.optimization_barrier((part, *ring, *last, *swapped))
     query_blocks = [queries, near[0], near[1], near[4]]
@@ -67,18 +68,18 @@
     for i, ref in enumerate(blocks):
         raw[pl.ds(i * rows, rows), :] = ref[...]
     for i in range(3):
-        for j in range(4):
-            cols = pl.ds(j * width // 4, width // 4)
+        for j in range(2):
+            cols = pl.ds(j * width // 2, width // 2)
             emb[pl.ds(i * part, part), cols] = dot(raw[pl.ds(i * part, part), :], weight[:, cols]).astype(BF16)
     query_emb = emb[pl.ds(0, part), :]
     scale = 1.0 / math.sqrt(width)
     top = jnp.full((1, part), -1e30, F32)
-    for i in range(4):
-        piece = scale * dot(emb[pl.ds(part + 2 * i * rows, 2 * rows), :], query_emb, LAST)
-        scores[pl.ds(2 * i * rows, 2 * rows), :] = piece
-        for j in range(2):
+    for i in range(2):
+        piece = scale * dot(emb[pl.ds((1 + i) * part, part), :], query_emb, LAST)
+        scores[pl.ds(i * part, part), :] = piece
+        for j in range(4):
             best = jnp.max(piece[j * rows : (j + 1) * rows], axis=0, keepdims=True)
-            top = jnp.maximum(top, jnp.where(live[pl.ds(2 * i + j, 1), :] > 0.0, best, -1e30))
+            top = jnp.maximum(top, jnp.where(live[pl.ds(4 * i + j, 1), :] > 0.0, best, -1e30))
     total = jnp.zeros((1, part), F32)
     stats[...] = jnp.zeros_like(stats)
     own_score[...] = jnp.zeros_like(own_score)
@@ -133,8 +134,9 @@
             value = value + own_factor * emb[pl.ds(part, rows), :].astype(F32)
         out[...] = value.astype(out.dtype)
         parts[span, :] = value.astype(BF16)
+    value_all = dot(probs[pl.ds(0, part), :], scaled[...])
     for i, out in enumerate((passage_own, passage_back, passage_next, passage_ahead)):
-        value = dot(probs[pl.ds(i * rows, rows), :], scaled[...])
+        value = value_all[i * rows : (i + 1) * rows]
         if i == 0:
             value = value + own_factor * emb[pl.ds(0, rows), :].astype(F32)
         out[...] = value.astype(out.dtype)
@@ -185,7 +187,7 @@
             shape((8, 256), F32),
         ),
         scratch_shapes=[pltpu.VMEM((8 * rows, 4 * rows), F32)],
-        compiler_params=pltpu.CompilerParams(vmem_limit_bytes=26 * 2**20),
+        compiler_params=pltpu.CompilerParams(vmem_limit_bytes=16 * 2**20),
         cost_estimate=pl.CostEstimate(flops=6 * 10**9, bytes_accessed=10**7, transcendentals=10**6),
         name="scores",
     )(*query_blocks, *passage_blocks, full_weight, hit)
@@ -208,7 +210,7 @@
         ),
         in_specs=[pl.BlockSpec(memory_space=pltpu.SMEM)] + [pl.BlockSpec(memory_space=pltpu.VMEM)] * 9,
         scratch_shapes=[pltpu.VMEM((4 * rows, width), BF16), pltpu.VMEM((12 * rows, width), BF16)],
-        compiler_params=pltpu.CompilerParams(vmem_limit_bytes=34 * 2**20),
+        compiler_params=pltpu.CompilerParams(vmem_limit_bytes=20 * 2**20),
         cost_estimate=pl.CostEstimate(flops=6 * 10**9, bytes_accessed=10**7, transcendentals=10**4),
         name="grads",
     )(places, stats, *came, own_score, raw, emb, probs, query_sum)

time: 110 us -> 109 us (level)
  waiting for transfers between devices: 31.7 us -> 28.4 us
  starting transfers between devices: 29.1 us -> 30.7 us
    all_to_all x1, waiting for transfers between devices: 2.85 us -> 0.01 us  [gather_all(): lax.all_to_all(jnp.broadcast_to(part, (4, 16, rows, width)), 'y', 0, 0)]
  transfers between devices with their start and end apart: 27 -> 27, of which waited for: 12 -> 11; matrix products, arithmetic and copies ran while one was open for 13% -> 13% of each run, Pallas kernels for 0% -> 0%
where the time goes in v4:
time: 109 us; the launch traced here: 108 us
  starting transfers between devices  30.7 us (28%)
  waiting for transfers between devices  28.4 us (26%)
  Pallas kernels  15.8 us (14%)
  blocking collectives  15.3 us (14%)
  matrix products  6.24 us (6%)
  local copies, waits for them, and re-layouts  5.41 us (5%)
  other arithmetic  5.34 us (5%)
  between operations  1.1 us (1%)
    ppermute x18, waiting for transfers between devices, shift(): return lax.ppermute(value, names, pairs)  20.8 us
    ppermute x18, starting transfers between devices, shift(): return lax.ppermute(value, names, pairs)  19 us
    all_to_all x1, blocking collectives, gather_all(): lax.all_to_all(jnp.broadcast_to(weight, (16, rows, width)), ('z', 'x'), 0...  15.3 us
    pallas_call x1, Pallas kernels, local(): pl.pallas_call(score_kernel, out_shape=(shape((12 * rows, width), BF16),...  8.02 us
    pallas_call x1, Pallas kernels, local(): pl.pallas_call(grad_kernel, out_shape=(shape((8, 256), F32), *(high, low,...  7.76 us
    dot_general x3, matrix products, dot(): return lax.dot_general(a, b, dims, preferred_element_type=F32)  6.24 us
    all_to_all x1, waiting for transfers between devices, local(): lax.all_to_all(weight_sum, ('z', 'x'), 0, 0).astype(F32)  5.91 us
    all_to_all x1, starting transfers between devices, local(): lax.all_to_all(weight_sum, ('z', 'x'), 0, 0).astype(F32)  5.03 us
  transfers between devices with their start and end apart: 27, of which 11 were waited for; matrix products, arithmetic and copies ran while one was open for 13% of the time, Pallas kernels for 0%

profile of v4, /device:TPU:0, one launch (start us, length us, event | category | flops | bytes accessed | tf_op | source)
XLA Modules:
  0.0 108.2 jit_solution(1700143908841591254)
XLA Ops:
  0.7 1.6 %collective-permute-start = (bf16[160,1024]{1,0:T(8,128)(2,1)}, bf16[160,1024]{1,0:T(8,128)(2,1)S(1)}, u32[]{:S(2)}, u32[]{:S(2)}) collective-permute-start(bf16[160,1024]{1,0:T(8,128)(2,1)} %refs_0_), channel_id=1, source_target_pairs={{0,8},{4,28},{8,16},{12,4},{16,24},{20,12},{24,0},{28,20},{1,9},{5... | collective-permute-start | bytes 983048 | tf_op jit(solution)/shard_map/ppermute | solution.py:28
  2.3 4.0 %collective-permute-start.2 = (bf16[160,1024]{1,0:T(8,128)(2,1)}, bf16[160,1024]{1,0:T(8,128)(2,1)S(1)}, u32[]{:S(2)}, u32[]{:S(2)}) collective-permute-start(bf16[160,1024]{1,0:T(8,128)(2,1)} %refs_4_.1), channel_id=1, source_target_pairs={{0,96},{4,36},{32,0},{36,68},{64,32},{68,100},{96,64},{100,4},{1,9... | collective-permute-start | bytes 983048 | tf_op jit(solution)/shard_map/ppermute | solution.py:28
  6.4 0.7 broadcast_in_dim.28
  7.1 15.3 %all_to_all.15 = bf16[16,8,1024]{2,1,0:T(8,128)(2,1)S(1)} all-to-all(bf16[16,8,1024]{2,1,0:T(8,128)(2,1)S(1)} %broadcast_in_dim.28), channel_id=1, replica_groups=mesh['z'=4,'x'=4,'c'=2,'y'=4] {'z','x'}, dimensions={0} | all-to-all | bytes 524288 | tf_op jit(solution)/shard_map/all_to_all | solution.py:47
  22.4 1.1 %broadcast_in_dim.29 = bf16[4,16,8,1024]{3,2,1,0:T(8,128)(2,1)} broadcast(bf16[16,8,1024]{2,1,0:T(8,128)(2,1)S(1)} %all_to_all.15), dimensions={1,2,3} | broadcast | bytes 1310720 | tf_op jit(solution)/shard_map/broadcast_in_dim | solution.py:52
  23.5 4.5 %all-to-all-start.1 = ((bf16[4,16,8,1024]{3,2,1,0:T(8,128)(2,1)}), bf16[4,16,8,1024]{3,2,1,0:T(8,128)(2,1)}, u32[]{:S(2)}, u32[]{:S(2)}) async-start(bf16[4,16,8,1024]{3,2,1,0:T(8,128)(2,1)} %broadcast_in_dim.29), calls=%async_computation.1 | async-start | bytes 2097152 | tf_op jit(solution)/shard_map/all_to_all | solution.py:52
  28.0 0.8 collective-permute-start.3
  28.8 1.3 %collective-permute-start.4 = (bf16[160,1024]{1,0:T(8,128)(2,1)S(1)}, bf16[160,1024]{1,0:T(8,128)(2,1)S(1)}, u32[]{:S(2)}, u32[]{:S(2)}) collective-permute-start(bf16[160,1024]{1,0:T(8,128)(2,1)S(1)} %collective-permute-done.refs_1_), channel_id=1, source_target_pairs={{0,8},{4,28},{8,16},{12,4},{16,24},{20,12},{24,0},{28,20},{1,9},{5... | collective-permute-start | bytes 983048 | tf_op jit(solution)/shard_map/ppermute | solution.py:28
  30.1 1.1 collective-permute-start.7
  31.2 7.2 %collective-permute-done.3.refs_2_ = bf16[160,1024]{1,0:T(8,128)(2,1)S(1)} collective-permute-done((bf16[160,1024]{1,0:T(8,128)(2,1)S(1)}, bf16[160,1024]{1,0:T(8,128)(2,1)S(1)}, u32[]{:S(2)}, u32[]{:S(2)}) %collective-permute-start.3) | collective-permute-done | bytes 327712 | tf_op jit(solution)/shard_map/ppermute | solution.py:28
  38.4 0.9 collective-permute-done.4.refs_3_
  39.3 0.2 collective-permute-done.5.refs_7_
  39.7 0.1 copy.16
  39.8 0.1 fusion.8
  39.9 0.6 gather_fusion.1
  40.6 0.6 gather_fusion
  41.1 0.1 stack.67
  41.3 0.2 and_reduce_fusion
  41.5 0.1 copy.17
  41.6 0.1 broadcast_in_dim.30
  41.7 0.1 reshape.109.refs_13_
  41.8 0.1 pad_add_fusion.places
  41.9 0.4 collective-permute-start.8
  42.2 0.1 collective-permute-start.9
  42.4 0.2 collective-permute-done.10
  42.6 1.7 %select_bitcast_fusion.1 = (bf16[16,1,4,8,1024]{4,3,0,2,1:T(8,128)(2,1)S(1)}, bf16[16,1,4,8,1024]{4,3,0,2,1:T(8,128)(2,1)S(1)}) fusion(bf16[4,16,8,1024]{3,2,1,0:T(8,128)(2,1)} %all-to-all-done.1, bf16[4,16,8,1024]{3,2,1,0:T(8,128)(2,1)} %collective-permute-done.10, pred[]{:T(512)S(6)} %eq.48), kind=kLoop, calls=%fused_computation.8 | loop fusion | flops 1048576 | bytes 4194305 | tf_op jit(solution)/shard_map/stack | solution.py:61
  44.3 0.2 pad_maximum_fusion
  44.6 0.2 copy.15
  44.8 0.7 copy-done.4
  45.5 0.1 copy-done.6
  45.6 0.1 copy-done.8
  45.7 0.1 copy-done.10
  45.8 0.1 copy-done.12
  45.9 8.0 %scores.1 = (bf16[1920,1024]{1,0:T(8,128)(2,1)S(1)}, bf16[1920,1024]{1,0:T(8,128)(2,1)S(1)}, bf16[1280,640]{1,0:T(8,128)(2,1)S(1)}, f32[8,256]{1,0:T(8,128)S(1)}, f32[8,256]{1,0:T(8,128)S(1)}) custom-call(bf16[160,1024]{1,0:T(8,128)(2,1)S(1)} %copy-done.1, bf16[160,1024]{1,0:T(8,128)(2,1)S(1)} %collective-permute-done.refs_1_, ...), custom_call_target="tpu_custom_call" | custom-call | flops 6000000000 | bytes 10000000 | tf_op jit(solution)/shard_map/scores/pallas_call | solution.py:180
  53.9 0.5 collective-permute-start.13
  54.4 2.3 %collective-permute-start.12 = (f32[8,256]{1,0:T(8,128)S(1)}, f32[8,256]{1,0:T(8,128)S(1)}, u32[]{:S(2)}, u32[]{:S(2)}) collective-permute-start(f32[8,256]{1,0:T(8,128)S(1)} %get-tuple-element.56.here), channel_id=1, source_target_pairs={{0,24},{4,12},{8,0},{12,20},{16,8},{20,28},{24,16},{28,4},{1,25},{... | collective-permute-start | bytes 24584 | tf_op jit(solution)/shard_map/ppermute | solution.py:28
  56.7 1.9 %fusion.query_sum = f32[640,1024]{1,0:T(8,128)S(1)} fusion(bf16[1280,640]{1,0:T(8,128)(2,1)S(1)} %get-tuple-element.57.probs, bf16[1920,1024]{1,0:T(8,128)(2,1)S(1)} %get-tuple-element.58.emb), kind=kOutput, calls=%fused_computation.2 | convolution fusion | flops 1677721600 | bytes 6881280 | tf_op jit(solution)/shard_map/dot_general | solution.py:41
  58.6 0.5 collective-permute-done.13.opposite
  59.1 2.4 %collective-permute-done.11.before = f32[8,256]{1,0:T(8,128)S(1)} collective-permute-done((f32[8,256]{1,0:T(8,128)S(1)}, f32[8,256]{1,0:T(8,128)S(1)}, u32[]{:S(2)}, u32[]{:S(2)}) %collective-permute-start.11) | collective-permute-done | bytes 8224 | tf_op jit(solution)/shard_map/ppermute | solution.py:28
  61.5 7.8 %grads.1 = (f32[8,256]{1,0:T(8,128)S(1)}, f32[160,1024]{1,0:T(8,128)S(1)}, bf16[160,1024]{1,0:T(8,128)(2,1)S(1)}, f32[160,1024]{1,0:T(8,128)S(1)}, bf16[160,1024...) custom-call(s32[9]{0:T(128)S(1)} %pad_add_fusion.places, ...), custom_call_target="tpu_custom_call" | custom-call | flops 6000000000 | bytes 10000000 | tf_op jit(solution)/shard_map/grads/pallas_call | solution.py:202
  69.3 0.1 collective-permute-start.18
  69.4 0.5 collective-permute-start.17
  69.9 0.6 slice.43
  70.4 0.3 collective-permute-start.14
  70.8 1.7 %collective-permute-start.15 = (bf16[160,1024]{1,0:T(8,128)(2,1)S(1)}, bf16[160,1024]{1,0:T(8,128)(2,1)S(1)}, u32[]{:S(2)}, u32[]{:S(2)}) collective-permute-start(bf16[160,1024]{1,0:T(8,128)(2,1)S(1)} %get-tuple-element.69), channel_id=1, source_target_pairs={{0,8},{4,28},{8,16},{12,4},{16,24},{20,12},{24,0},{28,20},{1,9},{5... | collective-permute-start | bytes 983048 | tf_op jit(solution)/shard_map/ppermute | solution.py:28
  72.5 1.4 %collective-permute-done.17 = bf16[512,1024]{1,0:T(8,128)(2,1)S(1)} collective-permute-done((bf16[512,1024]{1,0:T(8,128)(2,1)S(1)}, bf16[512,1024]{1,0:T(8,128)(2,1)S(1)}, u32[]{:S(2)}, u32[]{:S(2)}) %collective-permute-start.17) | collective-permute-done | bytes 1048608 | tf_op jit(solution)/shard_map/ppermute | solution.py:21
  73.9 0.2 add_convert_fusion.6
  74.1 1.5 %collective-permute-start.23 = (bf16[128,1024]{1,0:T(8,128)(2,1)S(1)}, bf16[128,1024]{1,0:T(8,128)(2,1)S(1)}, u32[]{:S(2)}, u32[]{:S(2)}) collective-permute-start(bf16[128,1024]{1,0:T(8,128)(2,1)S(1)} %get-tuple-element.79), channel_id=1, source_target_pairs={{0,1},{4,7},{1,2},{5,4},{2,3},{6,5},{3,0},{7,6},{8,9},{12,15},{9,1... | collective-permute-start | bytes 786440 | tf_op jit(solution)/shard_map/ppermute | solution.py:28
  75.6 1.0 add_convert_fusion.2
  76.6 4.8 %collective-permute-done.15 = bf16[160,1024]{1,0:T(8,128)(2,1)S(1)} collective-permute-done((bf16[160,1024]{1,0:T(8,128)(2,1)S(1)}, bf16[160,1024]{1,0:T(8,128)(2,1)S(1)}, u32[]{:S(2)}, u32[]{:S(2)}) %collective-permute-start.15) | collective-permute-done | bytes 327712 | tf_op jit(solution)/shard_map/ppermute | solution.py:28
  81.5 2.7 %collective-permute-start.22 = (bf16[128,1024]{1,0:T(8,128)(2,1)S(1)}, bf16[128,1024]{1,0:T(8,128)(2,1)S(1)}, u32[]{:S(2)}, u32[]{:S(2)}) collective-permute-start(bf16[128,1024]{1,0:T(8,128)(2,1)S(1)} %get-tuple-element.78), channel_id=1, source_target_pairs={{0,3},{4,5},{1,0},{5,6},{2,1},{6,7},{3,2},{7,4},{8,11},{12,13},{9,... | collective-permute-start | bytes 786440 | tf_op jit(solution)/shard_map/ppermute | solution.py:28
  84.2 1.0 collective-permute-start.19
  85.2 0.1 add_convert_fusion.5
  85.3 1.0 collective-permute-start.24
  86.3 0.1 add_convert_fusion
  86.5 0.2 collective-permute-start.21
  86.7 3.1 %collective-permute-done.16 = bf16[160,1024]{1,0:T(8,128)(2,1)S(1)} collective-permute-done((bf16[160,1024]{1,0:T(8,128)(2,1)S(1)}, bf16[160,1024]{1,0:T(8,128)(2,1)S(1)}, u32[]{:S(2)}, u32[]{:S(2)}) %collective-permute-start.16) | collective-permute-done | bytes 327712 | tf_op jit(solution)/shard_map/ppermute | solution.py:28
  89.8 1.6 %convolution_convert_fusion.1 = bf16[160,1024]{1,0:T(8,128)(2,1)} fusion(bf16[1024,1024]{1,0:T(8,128)(2,1)S(1)} %bitcast.31, bf16[160,1024]{1,0:T(8,128)(2,1)S(1)} %collective-permute-done.16, f32[160,1024]{1,0:T(8,128)S(1)} %get-tuple-element.66, bf16[160,1024]{1,0:T(8,128)(2,1)S(1)} %collective-permute-done.14), kind=kOutput, calls=%fused_computation.6 | convolution fusion | flops 336691200 | bytes 3735552 | tf_op jit(solution)/shard_map/dot_general | solution.py:41
  91.4 1.6 %collective-permute-done.24 = bf16[128,1024]{1,0:T(8,128)(2,1)S(1)} collective-permute-done((bf16[128,1024]{1,0:T(8,128)(2,1)S(1)}, bf16[128,1024]{1,0:T(8,128)(2,1)S(1)}, u32[]{:S(2)}, u32[]{:S(2)}) %collective-permute-start.24) | collective-permute-done | bytes 262176 | tf_op jit(solution)/shard_map/ppermute | solution.py:28
  93.0 0.9 fusion.5
  93.9 5.0 %all-to-all-start.2 = ((bf16[16,8,1024]{2,1,0:T(8,128)(2,1)}), bf16[16,8,1024]{2,1,0:T(8,128)(2,1)S(1)}, u32[]{:S(2)}, u32[]{:S(2)}) async-start(bf16[16,8,1024]{2,1,0:T(8,128)(2,1)} %fusion.5), calls=%async_computation.2 | async-start | bytes 524288 | tf_op jit(solution)/shard_map/all_to_all | solution.py:248
  98.9 2.8 %convolution_convert_fusion = bf16[160,1024]{1,0:T(8,128)(2,1)} fusion(bf16[1024,1024]{1,0:T(8,128)(2,1)S(1)} %bitcast.32, bf16[160,1024]{1,0:T(8,128)(2,1)} %collective-permute-done.21, bf16[160,1024]{1,0:T(8,128)(2,1)} %collective-permute-done.19, f32[160,1024]{1,0:T(8,128)S(1)} %get-tuple-element.70, bf16[640,1024]{1,0:T(8,128)(2,1)} %copy-done.13), kind=kOutput, calls=%fused_computation.5 | convolution fusion | flops 337018880 | bytes 4063232 | tf_op jit(solution)/shard_map/dot_general | solution.py:41
  101.7 5.9 %all-to-all-done.2 = bf16[16,8,1024]{2,1,0:T(8,128)(2,1)S(1)} async-done(((bf16[16,8,1024]{2,1,0:T(8,128)(2,1)}), bf16[16,8,1024]{2,1,0:T(8,128)(2,1)S(1)}, u32[]{:S(2)}, u32[]{:S(2)}) %all-to-all-start.2) | async-done | bytes 262176 | tf_op jit(solution)/shard_map/all_to_all | solution.py:248
  107.6 0.7 convert_reduce_fusion
  (53 shorter events, 0.4 us)
Async XLA Ops:
  0.6 39.3 %copy-start = (s32[128]{0:T(128)S(1)}, s32[128]{0:T(128)}, u32[]{:S(2)}) copy-start(s32[128]{0:T(128)} %param.9) | copy-start | bytes 1540
  0.6 27.3 %copy-start.1 = (bf16[160,1024]{1,0:T(8,128)(2,1)S(1)}, bf16[160,1024]{1,0:T(8,128)(2,1)}, u32[]{:S(2)}) copy-start(bf16[160,1024]{1,0:T(8,128)(2,1)} %refs_0_) | copy-start | bytes 983044
  0.7 27.3 %copy-start.2 = (bf16[160,1024]{1,0:T(8,128)(2,1)S(1)}, bf16[160,1024]{1,0:T(8,128)(2,1)}, u32[]{:S(2)}) copy-start(bf16[160,1024]{1,0:T(8,128)(2,1)} %refs_4_.1) | copy-start | bytes 983044
  0.7 21.7 %collective-permute-start = (bf16[160,1024]{1,0:T(8,128)(2,1)}, bf16[160,1024]{1,0:T(8,128)(2,1)S(1)}, u32[]{:S(2)}, u32[]{:S(2)}) collective-permute-start(bf16[160,1024]{1,0:T(8,128)(2,1)} %refs_0_), channel_id=1, source_target_pairs={{0,8},{4,28},{8,16},{12,4},{16,24},{20,12},{24,0},{28,20},{1,9},{5... | collective-permute-start | bytes 983048 | tf_op jit(solution)/shard_map/ppermute | solution.py:28
  2.3 20.1 %collective-permute-start.2 = (bf16[160,1024]{1,0:T(8,128)(2,1)}, bf16[160,1024]{1,0:T(8,128)(2,1)S(1)}, u32[]{:S(2)}, u32[]{:S(2)}) collective-permute-start(bf16[160,1024]{1,0:T(8,128)(2,1)} %refs_4_.1), channel_id=1, source_target_pairs={{0,96},{4,36},{32,0},{36,68},{64,32},{68,100},{96,64},{100,4},{1,9... | collective-permute-start | bytes 983048 | tf_op jit(solution)/shard_map/ppermute | solution.py:28
  6.3 16.0 %collective-permute-start.1 = (bf16[160,1024]{1,0:T(8,128)(2,1)}, bf16[160,1024]{1,0:T(8,128)(2,1)S(1)}, u32[]{:S(2)}, u32[]{:S(2)}) collective-permute-start(bf16[160,1024]{1,0:T(8,128)(2,1)} %refs_4_.1), channel_id=1, source_target_pairs={{0,32},{4,100},{32,64},{36,4},{64,96},{68,36},{96,0},{100,68},{1,3... | collective-permute-start | bytes 983048 | tf_op jit(solution)/shard_map/ppermute | solution.py:28
  7.1 32.6 %copy-start.14 = (s32[128,32]{0,1:T(8,128)S(1)}, s32[128,32]{0,1:T(8,128)}, u32[]{:S(2)}) copy-start(s32[128,32]{0,1:T(8,128)} %param.8) | copy-start | bytes 49156
  22.4 18.2 %copy-start.3 = (bf16[160,1024]{1,0:T(8,128)(2,1)}, bf16[160,1024]{1,0:T(8,128)(2,1)S(1)}, u32[]{:S(2)}) copy-start(bf16[160,1024]{1,0:T(8,128)(2,1)S(1)} %collective-permute-done.1.refs_5_) | copy-start | bytes 983044
  23.5 16.1 %all-to-all-start.1 = ((bf16[4,16,8,1024]{3,2,1,0:T(8,128)(2,1)}), bf16[4,16,8,1024]{3,2,1,0:T(8,128)(2,1)}, u32[]{:S(2)}, u32[]{:S(2)}) async-start(bf16[4,16,8,1024]{3,2,1,0:T(8,128)(2,1)} %broadcast_in_dim.29), calls=%async_computation.1 | async-start | bytes 2097152 | tf_op jit(solution)/shard_map/all_to_all | solution.py:52
  28.0 3.2 %collective-permute-start.6 = (bf16[160,1024]{1,0:T(8,128)(2,1)S(1)}, bf16[160,1024]{1,0:T(8,128)(2,1)S(1)}, u32[]{:S(2)}, u32[]{:S(2)}) collective-permute-start(bf16[160,1024]{1,0:T(8,128)(2,1)S(1)} %copy-done.2), channel_id=1, source_target_pairs={{0,4},{4,0},{1,5},{5,1},{2,6},{6,2},{3,7},{7,3},{8,12},{12,8},{9,1... | collective-permute-start | bytes 983048 | tf_op jit(solution)/shard_map/ppermute | solution.py:21
  28.0 10.4 %collective-permute-start.3 = (bf16[160,1024]{1,0:T(8,128)(2,1)S(1)}, bf16[160,1024]{1,0:T(8,128)(2,1)S(1)}, u32[]{:S(2)}, u32[]{:S(2)}) collective-permute-start(bf16[160,1024]{1,0:T(8,128)(2,1)S(1)} %copy-done.1), channel_id=1, source_target_pairs={{0,24},{4,12},{8,0},{12,20},{16,8},{20,28},{24,16},{28,4},{1,25},{... | collective-permute-start | bytes 983048 | tf_op jit(solution)/shard_map/ppermute | solution.py:28
  28.8 10.5 %collective-permute-start.4 = (bf16[160,1024]{1,0:T(8,128)(2,1)S(1)}, bf16[160,1024]{1,0:T(8,128)(2,1)S(1)}, u32[]{:S(2)}, u32[]{:S(2)}) collective-permute-start(bf16[160,1024]{1,0:T(8,128)(2,1)S(1)} %collective-permute-done.refs_1_), channel_id=1, source_target_pairs={{0,8},{4,28},{8,16},{12,4},{16,24},{20,12},{24,0},{28,20},{1,9},{5... | collective-permute-start | bytes 983048 | tf_op jit(solution)/shard_map/ppermute | solution.py:28
  30.1 9.2 %collective-permute-start.7 = (bf16[160,1024]{1,0:T(8,128)(2,1)S(1)}, bf16[160,1024]{1,0:T(8,128)(2,1)S(1)}, u32[]{:S(2)}, u32[]{:S(2)}) collective-permute-start(bf16[160,1024]{1,0:T(8,128)(2,1)S(1)} %collective-permute-done.1.refs_5_), channel_id=1, source_target_pairs={{0,4},{4,0},{1,5},{5,1},{2,6},{6,2},{3,7},{7,3},{8,12},{12,8},{9,1... | collective-permute-start | bytes 983048 | tf_op jit(solution)/shard_map/ppermute | solution.py:21
  31.2 8.4 %collective-permute-start.5 = (bf16[160,1024]{1,0:T(8,128)(2,1)S(1)}, bf16[160,1024]{1,0:T(8,128)(2,1)}, u32[]{:S(2)}, u32[]{:S(2)}) collective-permute-start(bf16[160,1024]{1,0:T(8,128)(2,1)S(1)} %collective-permute-done.1.refs_5_), channel_id=1, source_target_pairs={{0,32},{4,100},{32,64},{36,4},{64,96},{68,36},{96,0},{100,68},{1,3... | collective-permute-start | bytes 983048 | tf_op jit(solution)/shard_map/ppermute | solution.py:28
  31.2 13.1 %copy-start.5 = (bf16[160,1024]{1,0:T(8,128)(2,1)}, bf16[160,1024]{1,0:T(8,128)(2,1)S(1)}, u32[]{:S(2)}) copy-start(bf16[160,1024]{1,0:T(8,128)(2,1)S(1)} %collective-permute-done.6.refs_8_) | copy-start | bytes 983044
  38.4 5.9 %copy-start.7 = (bf16[160,1024]{1,0:T(8,128)(2,1)}, bf16[160,1024]{1,0:T(8,128)(2,1)S(1)}, u32[]{:S(2)}) copy-start(bf16[160,1024]{1,0:T(8,128)(2,1)S(1)} %collective-permute-done.3.refs_2_) | copy-start | bytes 983044
  39.3 5.0 %copy-start.9 = (bf16[160,1024]{1,0:T(8,128)(2,1)}, bf16[160,1024]{1,0:T(8,128)(2,1)S(1)}, u32[]{:S(2)}) copy-start(bf16[160,1024]{1,0:T(8,128)(2,1)S(1)} %collective-permute-done.4.refs_3_) | copy-start | bytes 983044
  39.3 5.0 %copy-start.11 = (bf16[160,1024]{1,0:T(8,128)(2,1)}, bf16[160,1024]{1,0:T(8,128)(2,1)S(1)}, u32[]{:S(2)}) copy-start(bf16[160,1024]{1,0:T(8,128)(2,1)S(1)} %collective-permute-done.7.refs_9_) | copy-start | bytes 983044
  39.6 3.0 %collective-permute-start.10 = (bf16[4,16,8,1024]{3,2,1,0:T(8,128)(2,1)}, bf16[4,16,8,1024]{3,2,1,0:T(8,128)(2,1)}, u32[]{:S(2)}, u32[]{:S(2)}) collective-permute-start(bf16[4,16,8,1024]{3,2,1,0:T(8,128)(2,1)} %all-to-all-done.1), channel_id=1, source_target_pairs={{0,4},{4,0},{1,5},{5,1},{2,6},{6,2},{3,7},{7,3},{8,12},{12,8},{9,1... | collective-permute-start | bytes 3145736 | tf_op jit(solution)/shard_map/ppermute | solution.py:21
  41.9 2.9 %collective-permute-start.8 = (bf16[160,1024]{1,0:T(8,128)(2,1)S(1)}, bf16[160,1024]{1,0:T(8,128)(2,1)S(1)}, u32[]{:S(2)}, u32[]{:S(2)}) collective-permute-start(bf16[160,1024]{1,0:T(8,128)(2,1)S(1)} %collective-permute-done.2.refs_6_), channel_id=1, source_target_pairs={{0,4},{4,0},{1,5},{5,1},{2,6},{6,2},{3,7},{7,3},{8,12},{12,8},{9,1... | collective-permute-start | bytes 983048 | tf_op jit(solution)/shard_map/ppermute | solution.py:21
  42.2 2.5 %collective-permute-start.9 = (bf16[160,1024]{1,0:T(8,128)(2,1)}, bf16[160,1024]{1,0:T(8,128)(2,1)S(1)}, u32[]{:S(2)}, u32[]{:S(2)}) collective-permute-start(bf16[160,1024]{1,0:T(8,128)(2,1)} %collective-permute-done.5.refs_7_), channel_id=1, source_target_pairs={{0,4},{4,0},{1,5},{5,1},{2,6},{6,2},{3,7},{7,3},{8,12},{12,8},{9,1... | collective-permute-start | bytes 983048 | tf_op jit(solution)/shard_map/ppermute | solution.py:21
  44.5 1.0 copy-start.4
  44.5 1.1 copy-start.6
  44.5 1.2 %copy-start.8 = (bf16[160,1024]{1,0:T(8,128)(2,1)S(1)}, bf16[160,1024]{1,0:T(8,128)(2,1)}, u32[]{:S(2)}) copy-start(bf16[160,1024]{1,0:T(8,128)(2,1)} %copy-done.7) | copy-start | bytes 983044
  44.5 1.2 %copy-start.10 = (bf16[160,1024]{1,0:T(8,128)(2,1)S(1)}, bf16[160,1024]{1,0:T(8,128)(2,1)}, u32[]{:S(2)}) copy-start(bf16[160,1024]{1,0:T(8,128)(2,1)} %copy-done.9) | copy-start | bytes 983044
  44.5 1.3 %copy-start.12 = (bf16[160,1024]{1,0:T(8,128)(2,1)S(1)}, bf16[160,1024]{1,0:T(8,128)(2,1)}, u32[]{:S(2)}) copy-start(bf16[160,1024]{1,0:T(8,128)(2,1)} %copy-done.11) | copy-start | bytes 983044
  53.9 5.2 %collective-permute-start.13 = (f32[8,256]{1,0:T(8,128)S(1)}, f32[8,256]{1,0:T(8,128)S(1)}, u32[]{:S(2)}, u32[]{:S(2)}) collective-permute-start(f32[8,256]{1,0:T(8,128)S(1)} %get-tuple-element.56.here), channel_id=1, source_target_pairs={{0,16},{4,20},{8,24},{12,28},{16,0},{20,4},{24,8},{28,12},{1,17},{... | collective-permute-start | bytes 24584 | tf_op jit(solution)/shard_map/ppermute | solution.py:28
  54.4 4.7 %collective-permute-start.12 = (f32[8,256]{1,0:T(8,128)S(1)}, f32[8,256]{1,0:T(8,128)S(1)}, u32[]{:S(2)}, u32[]{:S(2)}) collective-permute-start(f32[8,256]{1,0:T(8,128)S(1)} %get-tuple-element.56.here), channel_id=1, source_target_pairs={{0,24},{4,12},{8,0},{12,20},{16,8},{20,28},{24,16},{28,4},{1,25},{... | collective-permute-start | bytes 24584 | tf_op jit(solution)/shard_map/ppermute | solution.py:28
  56.7 4.9 %collective-permute-start.11 = (f32[8,256]{1,0:T(8,128)S(1)}, f32[8,256]{1,0:T(8,128)S(1)}, u32[]{:S(2)}, u32[]{:S(2)}) collective-permute-start(f32[8,256]{1,0:T(8,128)S(1)} %get-tuple-element.56.here), channel_id=1, source_target_pairs={{0,8},{4,28},{8,16},{12,4},{16,24},{20,12},{24,0},{28,20},{1,9},{5... | collective-permute-start | bytes 24584 | tf_op jit(solution)/shard_map/ppermute | solution.py:28
  69.3 4.8 %collective-permute-start.18 = (bf16[640,1024]{1,0:T(8,128)(2,1)S(1)}, bf16[640,1024]{1,0:T(8,128)(2,1)S(1)}, u32[]{:S(2)}, u32[]{:S(2)}) collective-permute-start(bf16[640,1024]{1,0:T(8,128)(2,1)S(1)} %get-tuple-element.73), channel_id=1, source_target_pairs={{0,4},{4,0},{1,5},{5,1},{2,6},{6,2},{3,7},{7,3},{8,12},{12,8},{9,1... | collective-permute-start | bytes 3932168 | tf_op jit(solution)/shard_map/ppermute | solution.py:21
  69.4 4.5 %collective-permute-start.17 = (bf16[512,1024]{1,0:T(8,128)(2,1)S(1)}, bf16[512,1024]{1,0:T(8,128)(2,1)S(1)}, u32[]{:S(2)}, u32[]{:S(2)}) collective-permute-start(bf16[512,1024]{1,0:T(8,128)(2,1)S(1)} %get-tuple-element.72), channel_id=1, source_target_pairs={{0,4},{4,0},{1,5},{5,1},{2,6},{6,2},{3,7},{7,3},{8,12},{12,8},{9,1... | collective-permute-start | bytes 3145736 | tf_op jit(solution)/shard_map/ppermute | solution.py:21
  70.4 16.0 %collective-permute-start.14 = (bf16[160,1024]{1,0:T(8,128)(2,1)S(1)}, bf16[160,1024]{1,0:T(8,128)(2,1)S(1)}, u32[]{:S(2)}, u32[]{:S(2)}) collective-permute-start(bf16[160,1024]{1,0:T(8,128)(2,1)S(1)} %get-tuple-element.67), channel_id=1, source_target_pairs={{0,24},{4,12},{8,0},{12,20},{16,8},{20,28},{24,16},{28,4},{1,25},{... | collective-permute-start | bytes 983048 | tf_op jit(solution)/shard_map/ppermute | solution.py:28
  70.8 10.6 %collective-permute-start.15 = (bf16[160,1024]{1,0:T(8,128)(2,1)S(1)}, bf16[160,1024]{1,0:T(8,128)(2,1)S(1)}, u32[]{:S(2)}, u32[]{:S(2)}) collective-permute-start(bf16[160,1024]{1,0:T(8,128)(2,1)S(1)} %get-tuple-element.69), channel_id=1, source_target_pairs={{0,8},{4,28},{8,16},{12,4},{16,24},{20,12},{24,0},{28,20},{1,9},{5... | collective-permute-start | bytes 983048 | tf_op jit(solution)/shard_map/ppermute | solution.py:28
  74.1 17.3 %copy-start.13 = (bf16[640,1024]{1,0:T(8,128)(2,1)}, bf16[640,1024]{1,0:T(8,128)(2,1)S(1)}, u32[]{:S(2)}) copy-start(bf16[640,1024]{1,0:T(8,128)(2,1)S(1)} %collective-permute-done.18) | copy-start | bytes 3932164
  74.1 10.1 %collective-permute-start.23 = (bf16[128,1024]{1,0:T(8,128)(2,1)S(1)}, bf16[128,1024]{1,0:T(8,128)(2,1)S(1)}, u32[]{:S(2)}, u32[]{:S(2)}) collective-permute-start(bf16[128,1024]{1,0:T(8,128)(2,1)S(1)} %get-tuple-element.79), channel_id=1, source_target_pairs={{0,1},{4,7},{1,2},{5,4},{2,3},{6,5},{3,0},{7,6},{8,9},{12,15},{9,1... | collective-permute-start | bytes 786440 | tf_op jit(solution)/shard_map/ppermute | solution.py:28
  76.6 8.8 %collective-permute-start.20 = (bf16[160,1024]{1,0:T(8,128)(2,1)S(1)}, bf16[160,1024]{1,0:T(8,128)(2,1)S(1)}, u32[]{:S(2)}, u32[]{:S(2)}) collective-permute-start(bf16[160,1024]{1,0:T(8,128)(2,1)S(1)} %get-tuple-element.85), channel_id=1, source_target_pairs={{0,32},{4,100},{32,64},{36,4},{64,96},{68,36},{96,0},{100,68},{1,3... | collective-permute-start | bytes 983048 | tf_op jit(solution)/shard_map/ppermute | solution.py:28
  81.4 8.4 %collective-permute-start.16 = (bf16[160,1024]{1,0:T(8,128)(2,1)S(1)}, bf16[160,1024]{1,0:T(8,128)(2,1)S(1)}, u32[]{:S(2)}, u32[]{:S(2)}) collective-permute-start(bf16[160,1024]{1,0:T(8,128)(2,1)S(1)} %add_convert_fusion.3), channel_id=1, source_target_pairs={{0,8},{4,28},{8,16},{12,4},{16,24},{20,12},{24,0},{28,20},{1,9},{5... | collective-permute-start | bytes 983048 | tf_op jit(solution)/shard_map/ppermute | solution.py:28
  81.5 9.8 %collective-permute-start.22 = (bf16[128,1024]{1,0:T(8,128)(2,1)S(1)}, bf16[128,1024]{1,0:T(8,128)(2,1)S(1)}, u32[]{:S(2)}, u32[]{:S(2)}) collective-permute-start(bf16[128,1024]{1,0:T(8,128)(2,1)S(1)} %get-tuple-element.78), channel_id=1, source_target_pairs={{0,3},{4,5},{1,0},{5,6},{2,1},{6,7},{3,2},{7,4},{8,11},{12,13},{9,... | collective-permute-start | bytes 786440 | tf_op jit(solution)/shard_map/ppermute | solution.py:28
  84.2 14.7 %collective-permute-start.19 = (bf16[160,1024]{1,0:T(8,128)(2,1)}, bf16[160,1024]{1,0:T(8,128)(2,1)}, u32[]{:S(2)}, u32[]{:S(2)}) collective-permute-start(bf16[160,1024]{1,0:T(8,128)(2,1)} %get-tuple-element.84), channel_id=1, source_target_pairs={{0,96},{4,36},{32,0},{36,68},{64,32},{68,100},{96,64},{100,4},{1,9... | collective-permute-start | bytes 983048 | tf_op jit(solution)/shard_map/ppermute | solution.py:28
  85.3 7.7 %collective-permute-start.24 = (bf16[128,1024]{1,0:T(8,128)(2,1)S(1)}, bf16[128,1024]{1,0:T(8,128)(2,1)S(1)}, u32[]{:S(2)}, u32[]{:S(2)}) collective-permute-start(bf16[128,1024]{1,0:T(8,128)(2,1)S(1)} %add_convert_fusion.5), channel_id=1, source_target_pairs={{0,1},{4,7},{1,2},{5,4},{2,3},{6,5},{3,0},{7,6},{8,9},{12,15},{9,1... | collective-permute-start | bytes 786440 | tf_op jit(solution)/shard_map/ppermute | solution.py:28
  86.5 12.4 %collective-permute-start.21 = (bf16[160,1024]{1,0:T(8,128)(2,1)S(1)}, bf16[160,1024]{1,0:T(8,128)(2,1)}, u32[]{:S(2)}, u32[]{:S(2)}) collective-permute-start(bf16[160,1024]{1,0:T(8,128)(2,1)S(1)} %add_convert_fusion), channel_id=1, source_target_pairs={{0,32},{4,100},{32,64},{36,4},{64,96},{68,36},{96,0},{100,68},{1,3... | collective-permute-start | bytes 983048 | tf_op jit(solution)/shard_map/ppermute | solution.py:28
  93.9 13.7 %all-to-all-start.2 = ((bf16[16,8,1024]{2,1,0:T(8,128)(2,1)}), bf16[16,8,1024]{2,1,0:T(8,128)(2,1)S(1)}, u32[]{:S(2)}, u32[]{:S(2)}) async-start(bf16[16,8,1024]{2,1,0:T(8,128)(2,1)} %fusion.5), calls=%async_computation.2 | async-start | bytes 524288 | tf_op jit(solution)/shard_map/all_to_all | solution.py:248

commit v5 on v4

--- a/solution.py
+++ b/solution.py
@@ -227,7 +227,7 @@
     def finish(part, last):
         return dot((scale * (part + last.astype(F32))).astype(BF16), full_weight, LAST).astype(BF16)
 
-    queries_part = begin(query_part, "x")
+    queries_part = (*query_part[:3], shift(query_part[3], "x", 1))
     theirs, passage_other = swap(theirs), swap(passage_other)
     weight_part = [
         (mine[i : i + width // 8].astype(F32) + theirs[i : i + width // 8].astype(F32)).astype(kind)
@@ -242,6 +242,9 @@
         ],
         "z",
     )
+    ahead, back = lax.optimization_barrier((weight_part[3], queries_part[1]))
+    weight_part = (*weight_part[:3], ahead)
+    queries_part = (queries_part[0], shift(back, "x", -1), *queries_part[2:])
     weight_sum, weight_last = go_on(weight_part, "y")
     (query_sum, query_last), (passage_sum, passage_last) = go_on(queries_part, "x"), go_on(passages_part, "z")
     weight_sum = (weight_sum + weight_last.astype(F32)).astype(BF16).reshape(16, -1, width)

time: 109 us -> 108 us (level)
  other arithmetic: 5.34 us -> 7.76 us
  waiting for transfers between devices: 28.4 us -> 26 us
  starting transfers between devices: 30.7 us -> 28.7 us
    all_to_all x1, waiting for transfers between devices: 5.91 us -> 3.3 us  [local(): lax.all_to_all(weight_sum, ('z', 'x'), 0, 0).astype(F32)]
    ppermute x18, starting transfers between devices: 19 us -> 16.9 us  [shift(): return lax.ppermute(value, names, pairs)]
    ppermute x7, waiting for transfers between devices: 1.64 us -> 3.66 us  [swap(): return lax.ppermute(value, 'c', [(0, 1), (1, 0)])]
    ppermute x18, waiting for transfers between devices: 20.8 us -> 19 us  [shift(): return lax.ppermute(value, names, pairs)]
    convert_element_type x3, other arithmetic: 0.33 us -> 1.79 us  [go_on(): last = shift((following + ahead.astype(F32)).astype(BF16), axis, 1)]
  transfers between devices with their start and end apart: 27 -> 27, of which waited for: 11 -> 12; matrix products, arithmetic and copies ran while one was open for 13% -> 15% of each run, Pallas kernels for 0% -> 0%
where the time goes in v5:
time: 108 us; the launch traced here: 107 us
  starting transfers between devices  28.7 us (27%)
  waiting for transfers between devices  26 us (24%)
  Pallas kernels  15.8 us (15%)
  blocking collectives  15.3 us (14%)
  other arithmetic  7.76 us (7%)
  matrix products  7.33 us (7%)
  local copies, waits for them, and re-layouts  5.41 us (5%)
  between operations  1.08 us (1%)
    ppermute x18, waiting for transfers between devices, shift(): return lax.ppermute(value, names, pairs)  19 us
    ppermute x18, starting transfers between devices, shift(): return lax.ppermute(value, names, pairs)  16.9 us
    all_to_all x1, blocking collectives, gather_all(): lax.all_to_all(jnp.broadcast_to(weight, (16, rows, width)), ('z', 'x'), 0...  15.3 us
    pallas_call x1, Pallas kernels, local(): pl.pallas_call(score_kernel, out_shape=(shape((12 * rows, width), BF16),...  8.02 us
    pallas_call x1, Pallas kernels, local(): pl.pallas_call(grad_kernel, out_shape=(shape((8, 256), F32), *(high, low,...  7.77 us
    dot_general x3, matrix products, dot(): return lax.dot_general(a, b, dims, preferred_element_type=F32)  7.33 us
    all_to_all x1, starting transfers between devices, local(): lax.all_to_all(weight_sum, ('z', 'x'), 0, 0).astype(F32)  5.16 us
    all_to_all x1, starting transfers between devices, gather_all(): lax.all_to_all(jnp.broadcast_to(part, (4, 16, rows, width)), 'y', 0, 0)  4.46 us
  transfers between devices with their start and end apart: 27, of which 12 were waited for; matrix products, arithmetic and copies ran while one was open for 15% of the time, Pallas kernels for 0%

profile of v5, /device:TPU:0, one launch (start us, length us, event | category | flops | bytes accessed | tf_op | source)
XLA Modules:
  0.0 107.3 jit_solution(17989159042545705603)
XLA Ops:
  0.7 1.6 %collective-permute-start = (bf16[160,1024]{1,0:T(8,128)(2,1)}, bf16[160,1024]{1,0:T(8,128)(2,1)S(1)}, u32[]{:S(2)}, u32[]{:S(2)}) collective-permute-start(bf16[160,1024]{1,0:T(8,128)(2,1)} %refs_0_), channel_id=1, source_target_pairs={{0,8},{4,28},{8,16},{12,4},{16,24},{20,12},{24,0},{28,20},{1,9},{5... | collective-permute-start | bytes 983048 | tf_op jit(solution)/shard_map/ppermute | solution.py:28
  2.3 4.0 %collective-permute-start.2 = (bf16[160,1024]{1,0:T(8,128)(2,1)}, bf16[160,1024]{1,0:T(8,128)(2,1)S(1)}, u32[]{:S(2)}, u32[]{:S(2)}) collective-permute-start(bf16[160,1024]{1,0:T(8,128)(2,1)} %refs_4_.1), channel_id=1, source_target_pairs={{0,96},{4,36},{32,0},{36,68},{64,32},{68,100},{96,64},{100,4},{1,9... | collective-permute-start | bytes 983048 | tf_op jit(solution)/shard_map/ppermute | solution.py:28
  6.4 0.7 broadcast_in_dim.28
  7.1 15.3 %all_to_all.15 = bf16[16,8,1024]{2,1,0:T(8,128)(2,1)S(1)} all-to-all(bf16[16,8,1024]{2,1,0:T(8,128)(2,1)S(1)} %broadcast_in_dim.28), channel_id=1, replica_groups=mesh['z'=4,'x'=4,'c'=2,'y'=4] {'z','x'}, dimensions={0} | all-to-all | bytes 524288 | tf_op jit(solution)/shard_map/all_to_all | solution.py:47
  22.4 1.1 %broadcast_in_dim.29 = bf16[4,16,8,1024]{3,2,1,0:T(8,128)(2,1)} broadcast(bf16[16,8,1024]{2,1,0:T(8,128)(2,1)S(1)} %all_to_all.15), dimensions={1,2,3} | broadcast | bytes 1310720 | tf_op jit(solution)/shard_map/broadcast_in_dim | solution.py:52
  23.5 4.5 %all-to-all-start.1 = ((bf16[4,16,8,1024]{3,2,1,0:T(8,128)(2,1)}), bf16[4,16,8,1024]{3,2,1,0:T(8,128)(2,1)}, u32[]{:S(2)}, u32[]{:S(2)}) async-start(bf16[4,16,8,1024]{3,2,1,0:T(8,128)(2,1)} %broadcast_in_dim.29), calls=%async_computation.1 | async-start | bytes 2097152 | tf_op jit(solution)/shard_map/all_to_all | solution.py:52
  28.0 0.8 collective-permute-start.3
  28.8 1.3 %collective-permute-start.4 = (bf16[160,1024]{1,0:T(8,128)(2,1)S(1)}, bf16[160,1024]{1,0:T(8,128)(2,1)S(1)}, u32[]{:S(2)}, u32[]{:S(2)}) collective-permute-start(bf16[160,1024]{1,0:T(8,128)(2,1)S(1)} %collective-permute-done.refs_1_), channel_id=1, source_target_pairs={{0,8},{4,28},{8,16},{12,4},{16,24},{20,12},{24,0},{28,20},{1,9},{5... | collective-permute-start | bytes 983048 | tf_op jit(solution)/shard_map/ppermute | solution.py:28
  30.1 1.1 %collective-permute-start.7 = (bf16[160,1024]{1,0:T(8,128)(2,1)S(1)}, bf16[160,1024]{1,0:T(8,128)(2,1)S(1)}, u32[]{:S(2)}, u32[]{:S(2)}) collective-permute-start(bf16[160,1024]{1,0:T(8,128)(2,1)S(1)} %collective-permute-done.1.refs_5_), channel_id=1, source_target_pairs={{0,4},{4,0},{1,5},{5,1},{2,6},{6,2},{3,7},{7,3},{8,12},{12,8},{9,1... | collective-permute-start | bytes 983048 | tf_op jit(solution)/shard_map/ppermute | solution.py:21
  31.2 7.2 %collective-permute-done.3.refs_2_ = bf16[160,1024]{1,0:T(8,128)(2,1)S(1)} collective-permute-done((bf16[160,1024]{1,0:T(8,128)(2,1)S(1)}, bf16[160,1024]{1,0:T(8,128)(2,1)S(1)}, u32[]{:S(2)}, u32[]{:S(2)}) %collective-permute-start.3) | collective-permute-done | bytes 327712 | tf_op jit(solution)/shard_map/ppermute | solution.py:28
  38.4 0.9 collective-permute-done.4.refs_3_
  39.3 0.2 collective-permute-done.5.refs_7_
  39.7 0.1 copy.16
  39.8 0.1 fusion.8
  39.9 0.6 gather_fusion.1
  40.6 0.6 gather_fusion
  41.1 0.1 stack.67
  41.3 0.2 and_reduce_fusion
  41.5 0.1 copy.17
  41.6 0.1 broadcast_in_dim.30
  41.7 0.1 reshape.109.refs_13_
  41.8 0.1 pad_add_fusion.places
  41.9 0.4 collective-permute-start.8
  42.2 0.1 collective-permute-start.9
  42.4 0.2 collective-permute-done.10
  42.6 1.7 %select_bitcast_fusion.1 = (bf16[16,1,4,8,1024]{4,3,0,2,1:T(8,128)(2,1)S(1)}, bf16[16,1,4,8,1024]{4,3,0,2,1:T(8,128)(2,1)S(1)}) fusion(bf16[4,16,8,1024]{3,2,1,0:T(8,128)(2,1)} %all-to-all-done.1, bf16[4,16,8,1024]{3,2,1,0:T(8,128)(2,1)} %collective-permute-done.10, pred[]{:T(512)S(6)} %eq.48), kind=kLoop, calls=%fused_computation.8 | loop fusion | flops 1048576 | bytes 4194305 | tf_op jit(solution)/shard_map/stack | solution.py:61
  44.3 0.2 pad_maximum_fusion
  44.6 0.2 copy.15
  44.8 0.7 copy-done.4
  45.5 0.1 copy-done.6
  45.6 0.1 copy-done.8
  45.7 0.1 copy-done.10
  45.8 0.1 copy-done.12
  45.9 8.0 %scores.1 = (bf16[1920,1024]{1,0:T(8,128)(2,1)S(1)}, bf16[1920,1024]{1,0:T(8,128)(2,1)S(1)}, bf16[1280,640]{1,0:T(8,128)(2,1)S(1)}, f32[8,256]{1,0:T(8,128)S(1)}, f32[8,256]{1,0:T(8,128)S(1)}) custom-call(bf16[160,1024]{1,0:T(8,128)(2,1)S(1)} %copy-done.1, bf16[160,1024]{1,0:T(8,128)(2,1)S(1)} %collective-permute-done.refs_1_, ...), custom_call_target="tpu_custom_call" | custom-call | flops 6000000000 | bytes 10000000 | tf_op jit(solution)/shard_map/scores/pallas_call | solution.py:180
  53.9 0.5 collective-permute-start.13
  54.4 2.3 %collective-permute-start.12 = (f32[8,256]{1,0:T(8,128)S(1)}, f32[8,256]{1,0:T(8,128)S(1)}, u32[]{:S(2)}, u32[]{:S(2)}) collective-permute-start(f32[8,256]{1,0:T(8,128)S(1)} %get-tuple-element.58.here), channel_id=1, source_target_pairs={{0,24},{4,12},{8,0},{12,20},{16,8},{20,28},{24,16},{28,4},{1,25},{... | collective-permute-start | bytes 24584 | tf_op jit(solution)/shard_map/ppermute | solution.py:28
  56.7 1.9 %fusion.query_sum = f32[640,1024]{1,0:T(8,128)S(1)} fusion(bf16[1280,640]{1,0:T(8,128)(2,1)S(1)} %get-tuple-element.59.probs, bf16[1920,1024]{1,0:T(8,128)(2,1)S(1)} %get-tuple-element.60.emb), kind=kOutput, calls=%fused_computation.2 | convolution fusion | flops 1677721600 | bytes 6881280 | tf_op jit(solution)/shard_map/dot_general | solution.py:41
  58.6 0.5 collective-permute-done.13.opposite
  59.1 2.4 %collective-permute-done.11.before = f32[8,256]{1,0:T(8,128)S(1)} collective-permute-done((f32[8,256]{1,0:T(8,128)S(1)}, f32[8,256]{1,0:T(8,128)S(1)}, u32[]{:S(2)}, u32[]{:S(2)}) %collective-permute-start.11) | collective-permute-done | bytes 8224 | tf_op jit(solution)/shard_map/ppermute | solution.py:28
  61.5 7.8 %grads.1 = (f32[8,256]{1,0:T(8,128)S(1)}, f32[160,1024]{1,0:T(8,128)S(1)}, bf16[160,1024]{1,0:T(8,128)(2,1)}, f32[160,1024]{1,0:T(8,128)S(1)}, bf16[160,1024]{1,...) custom-call(s32[9]{0:T(128)S(1)} %pad_add_fusion.places, ...), custom_call_target="tpu_custom_call" | custom-call | flops 6000000000 | bytes 10000000 | tf_op jit(solution)/shard_map/grads/pallas_call | solution.py:202
  69.3 0.1 collective-permute-start.15
  69.4 0.5 collective-permute-start.14
  69.9 0.6 slice.43
  70.4 3.5 %collective-permute-done.14 = bf16[512,1024]{1,0:T(8,128)(2,1)S(1)} collective-permute-done((bf16[512,1024]{1,0:T(8,128)(2,1)S(1)}, bf16[512,1024]{1,0:T(8,128)(2,1)S(1)}, u32[]{:S(2)}, u32[]{:S(2)}) %collective-permute-start.14) | collective-permute-done | bytes 1048608 | tf_op jit(solution)/shard_map/ppermute | solution.py:21
  73.9 0.2 add_convert_fusion.6
  74.1 1.5 %collective-permute-start.16 = (bf16[128,1024]{1,0:T(8,128)(2,1)S(1)}, bf16[128,1024]{1,0:T(8,128)(2,1)S(1)}, u32[]{:S(2)}, u32[]{:S(2)}) collective-permute-start(bf16[128,1024]{1,0:T(8,128)(2,1)S(1)} %get-tuple-element.72), channel_id=1, source_target_pairs={{0,1},{4,7},{1,2},{5,4},{2,3},{6,5},{3,0},{7,6},{8,9},{12,15},{9,1... | collective-permute-start | bytes 786440 | tf_op jit(solution)/shard_map/ppermute | solution.py:28
  75.6 1.0 add_convert_fusion.2
  76.6 2.1 %collective-permute-done.18 = bf16[160,1024]{1,0:T(8,128)(2,1)S(1)} collective-permute-done((bf16[160,1024]{1,0:T(8,128)(2,1)S(1)}, bf16[160,1024]{1,0:T(8,128)(2,1)S(1)}, u32[]{:S(2)}, u32[]{:S(2)}) %collective-permute-start.18) | collective-permute-done | bytes 327712 | tf_op jit(solution)/shard_map/ppermute | solution.py:28
  78.7 0.8 add_convert_fusion.3
  79.5 2.6 %collective-permute-start.23 = (bf16[128,1024]{1,0:T(8,128)(2,1)S(1)}, bf16[128,1024]{1,0:T(8,128)(2,1)S(1)}, u32[]{:S(2)}, u32[]{:S(2)}) collective-permute-start(bf16[128,1024]{1,0:T(8,128)(2,1)S(1)} %get-tuple-element.82), channel_id=1, source_target_pairs={{0,3},{4,5},{1,0},{5,6},{2,1},{6,7},{3,2},{7,4},{8,11},{12,13},{9,... | collective-permute-start | bytes 786440 | tf_op jit(solution)/shard_map/ppermute | solution.py:28
  82.2 1.0 collective-permute-start.20
  83.1 0.1 add_convert_fusion.5
  83.3 0.1 collective-permute-start.24
  83.4 2.2 %collective-permute-done.21 = bf16[160,1024]{1,0:T(8,128)(2,1)S(1)} collective-permute-done((bf16[160,1024]{1,0:T(8,128)(2,1)S(1)}, bf16[160,1024]{1,0:T(8,128)(2,1)S(1)}, u32[]{:S(2)}, u32[]{:S(2)}) %collective-permute-start.21) | collective-permute-done | bytes 327712 | tf_op jit(solution)/shard_map/ppermute | solution.py:28
  85.6 1.2 %collective-permute-start.17 = (bf16[160,1024]{1,0:T(8,128)(2,1)}, bf16[160,1024]{1,0:T(8,128)(2,1)}, u32[]{:S(2)}, u32[]{:S(2)}) collective-permute-start(bf16[160,1024]{1,0:T(8,128)(2,1)} %get-tuple-element.74), channel_id=1, source_target_pairs={{0,24},{4,12},{8,0},{12,20},{16,8},{20,28},{24,16},{28,4},{1,25},{... | collective-permute-start | bytes 983048 | tf_op jit(solution)/shard_map/ppermute | solution.py:28
  86.8 0.9 add_convert_fusion
  87.6 1.0 collective-permute-done.23
  88.7 2.3 %collective-permute-done.24 = bf16[128,1024]{1,0:T(8,128)(2,1)S(1)} collective-permute-done((bf16[128,1024]{1,0:T(8,128)(2,1)S(1)}, bf16[128,1024]{1,0:T(8,128)(2,1)S(1)}, u32[]{:S(2)}, u32[]{:S(2)}) %collective-permute-start.24) | collective-permute-done | bytes 262176 | tf_op jit(solution)/shard_map/ppermute | solution.py:28
  90.9 0.9 fusion.5
  91.8 5.2 %all-to-all-start.2 = ((bf16[16,8,1024]{2,1,0:T(8,128)(2,1)}), bf16[16,8,1024]{2,1,0:T(8,128)(2,1)}, u32[]{:S(2)}, u32[]{:S(2)}) async-start(bf16[16,8,1024]{2,1,0:T(8,128)(2,1)} %fusion.5), calls=%async_computation.2 | async-start | bytes 524288 | tf_op jit(solution)/shard_map/all_to_all | solution.py:251
  97.0 2.7 %convolution_convert_fusion.1 = bf16[160,1024]{1,0:T(8,128)(2,1)} fusion(bf16[1024,1024]{1,0:T(8,128)(2,1)S(1)} %bitcast.31, bf16[160,1024]{1,0:T(8,128)(2,1)} %collective-permute-done.19, f32[160,1024]{1,0:T(8,128)S(1)} %get-tuple-element.68, bf16[160,1024]{1,0:T(8,128)(2,1)} %collective-permute-done.17), kind=kOutput, calls=%fused_computation.6 | convolution fusion | flops 336691200 | bytes 3735552 | tf_op jit(solution)/shard_map/dot_general | solution.py:41
  99.7 2.8 %convolution_convert_fusion = bf16[160,1024]{1,0:T(8,128)(2,1)} fusion(bf16[1024,1024]{1,0:T(8,128)(2,1)S(1)} %bitcast.32, bf16[160,1024]{1,0:T(8,128)(2,1)} %collective-permute-done.22, bf16[160,1024]{1,0:T(8,128)(2,1)} %collective-permute-done.20, f32[160,1024]{1,0:T(8,128)S(1)} %get-tuple-element.77, bf16[640,1024]{1,0:T(8,128)(2,1)} %copy-done.13), kind=kOutput, calls=%fused_computation.5 | convolution fusion | flops 337018880 | bytes 4063232 | tf_op jit(solution)/shard_map/dot_general | solution.py:41
  102.4 3.3 %all-to-all-done.2 = bf16[16,8,1024]{2,1,0:T(8,128)(2,1)} async-done(((bf16[16,8,1024]{2,1,0:T(8,128)(2,1)}), bf16[16,8,1024]{2,1,0:T(8,128)(2,1)}, u32[]{:S(2)}, u32[]{:S(2)}) %all-to-all-start.2) | async-done | bytes 262176 | tf_op jit(solution)/shard_map/all_to_all | solution.py:251
  105.7 1.6 %convert_reduce_fusion = f32[8,1024]{1,0:T(8,128)} fusion(bf16[16,8,1024]{2,1,0:T(8,128)(2,1)} %all-to-all-done.2), kind=kLoop, calls=%fused_computation.15 | loop fusion | flops 253952 | bytes 294912 | tf_op jit(solution)/shard_map/reduce_sum | solution.py:251
  (53 shorter events, 0.2 us)
Async XLA Ops:
  0.6 39.3 %copy-start = (s32[128]{0:T(128)S(1)}, s32[128]{0:T(128)}, u32[]{:S(2)}) copy-start(s32[128]{0:T(128)} %param.9) | copy-start | bytes 1540
  0.6 27.3 %copy-start.1 = (bf16[160,1024]{1,0:T(8,128)(2,1)S(1)}, bf16[160,1024]{1,0:T(8,128)(2,1)}, u32[]{:S(2)}) copy-start(bf16[160,1024]{1,0:T(8,128)(2,1)} %refs_0_) | copy-start | bytes 983044
  0.7 27.3 %copy-start.2 = (bf16[160,1024]{1,0:T(8,128)(2,1)S(1)}, bf16[160,1024]{1,0:T(8,128)(2,1)}, u32[]{:S(2)}) copy-start(bf16[160,1024]{1,0:T(8,128)(2,1)} %refs_4_.1) | copy-start | bytes 983044
  0.7 21.7 %collective-permute-start = (bf16[160,1024]{1,0:T(8,128)(2,1)}, bf16[160,1024]{1,0:T(8,128)(2,1)S(1)}, u32[]{:S(2)}, u32[]{:S(2)}) collective-permute-start(bf16[160,1024]{1,0:T(8,128)(2,1)} %refs_0_), channel_id=1, source_target_pairs={{0,8},{4,28},{8,16},{12,4},{16,24},{20,12},{24,0},{28,20},{1,9},{5... | collective-permute-start | bytes 983048 | tf_op jit(solution)/shard_map/ppermute | solution.py:28
  2.3 20.1 %collective-permute-start.2 = (bf16[160,1024]{1,0:T(8,128)(2,1)}, bf16[160,1024]{1,0:T(8,128)(2,1)S(1)}, u32[]{:S(2)}, u32[]{:S(2)}) collective-permute-start(bf16[160,1024]{1,0:T(8,128)(2,1)} %refs_4_.1), channel_id=1, source_target_pairs={{0,96},{4,36},{32,0},{36,68},{64,32},{68,100},{96,64},{100,4},{1,9... | collective-permute-start | bytes 983048 | tf_op jit(solution)/shard_map/ppermute | solution.py:28
  6.3 16.0 %collective-permute-start.1 = (bf16[160,1024]{1,0:T(8,128)(2,1)}, bf16[160,1024]{1,0:T(8,128)(2,1)S(1)}, u32[]{:S(2)}, u32[]{:S(2)}) collective-permute-start(bf16[160,1024]{1,0:T(8,128)(2,1)} %refs_4_.1), channel_id=1, source_target_pairs={{0,32},{4,100},{32,64},{36,4},{64,96},{68,36},{96,0},{100,68},{1,3... | collective-permute-start | bytes 983048 | tf_op jit(solution)/shard_map/ppermute | solution.py:28
  7.1 32.6 %copy-start.14 = (s32[128,32]{0,1:T(8,128)S(1)}, s32[128,32]{0,1:T(8,128)}, u32[]{:S(2)}) copy-start(s32[128,32]{0,1:T(8,128)} %param.8) | copy-start | bytes 49156
  22.4 18.2 %copy-start.3 = (bf16[160,1024]{1,0:T(8,128)(2,1)}, bf16[160,1024]{1,0:T(8,128)(2,1)S(1)}, u32[]{:S(2)}) copy-start(bf16[160,1024]{1,0:T(8,128)(2,1)S(1)} %collective-permute-done.1.refs_5_) | copy-start | bytes 983044
  23.5 16.1 %all-to-all-start.1 = ((bf16[4,16,8,1024]{3,2,1,0:T(8,128)(2,1)}), bf16[4,16,8,1024]{3,2,1,0:T(8,128)(2,1)}, u32[]{:S(2)}, u32[]{:S(2)}) async-start(bf16[4,16,8,1024]{3,2,1,0:T(8,128)(2,1)} %broadcast_in_dim.29), calls=%async_computation.1 | async-start | bytes 2097152 | tf_op jit(solution)/shard_map/all_to_all | solution.py:52
  28.0 3.2 %collective-permute-start.6 = (bf16[160,1024]{1,0:T(8,128)(2,1)S(1)}, bf16[160,1024]{1,0:T(8,128)(2,1)S(1)}, u32[]{:S(2)}, u32[]{:S(2)}) collective-permute-start(bf16[160,1024]{1,0:T(8,128)(2,1)S(1)} %copy-done.2), channel_id=1, source_target_pairs={{0,4},{4,0},{1,5},{5,1},{2,6},{6,2},{3,7},{7,3},{8,12},{12,8},{9,1... | collective-permute-start | bytes 983048 | tf_op jit(solution)/shard_map/ppermute | solution.py:21
  28.0 10.4 %collective-permute-start.3 = (bf16[160,1024]{1,0:T(8,128)(2,1)S(1)}, bf16[160,1024]{1,0:T(8,128)(2,1)S(1)}, u32[]{:S(2)}, u32[]{:S(2)}) collective-permute-start(bf16[160,1024]{1,0:T(8,128)(2,1)S(1)} %copy-done.1), channel_id=1, source_target_pairs={{0,24},{4,12},{8,0},{12,20},{16,8},{20,28},{24,16},{28,4},{1,25},{... | collective-permute-start | bytes 983048 | tf_op jit(solution)/shard_map/ppermute | solution.py:28
  28.8 10.5 %collective-permute-start.4 = (bf16[160,1024]{1,0:T(8,128)(2,1)S(1)}, bf16[160,1024]{1,0:T(8,128)(2,1)S(1)}, u32[]{:S(2)}, u32[]{:S(2)}) collective-permute-start(bf16[160,1024]{1,0:T(8,128)(2,1)S(1)} %collective-permute-done.refs_1_), channel_id=1, source_target_pairs={{0,8},{4,28},{8,16},{12,4},{16,24},{20,12},{24,0},{28,20},{1,9},{5... | collective-permute-start | bytes 983048 | tf_op jit(solution)/shard_map/ppermute | solution.py:28
  30.1 9.2 %collective-permute-start.7 = (bf16[160,1024]{1,0:T(8,128)(2,1)S(1)}, bf16[160,1024]{1,0:T(8,128)(2,1)S(1)}, u32[]{:S(2)}, u32[]{:S(2)}) collective-permute-start(bf16[160,1024]{1,0:T(8,128)(2,1)S(1)} %collective-permute-done.1.refs_5_), channel_id=1, source_target_pairs={{0,4},{4,0},{1,5},{5,1},{2,6},{6,2},{3,7},{7,3},{8,12},{12,8},{9,1... | collective-permute-start | bytes 983048 | tf_op jit(solution)/shard_map/ppermute | solution.py:21
  31.2 8.4 %collective-permute-start.5 = (bf16[160,1024]{1,0:T(8,128)(2,1)S(1)}, bf16[160,1024]{1,0:T(8,128)(2,1)}, u32[]{:S(2)}, u32[]{:S(2)}) collective-permute-start(bf16[160,1024]{1,0:T(8,128)(2,1)S(1)} %collective-permute-done.1.refs_5_), channel_id=1, source_target_pairs={{0,32},{4,100},{32,64},{36,4},{64,96},{68,36},{96,0},{100,68},{1,3... | collective-permute-start | bytes 983048 | tf_op jit(solution)/shard_map/ppermute | solution.py:28
  31.2 13.1 %copy-start.5 = (bf16[160,1024]{1,0:T(8,128)(2,1)}, bf16[160,1024]{1,0:T(8,128)(2,1)S(1)}, u32[]{:S(2)}) copy-start(bf16[160,1024]{1,0:T(8,128)(2,1)S(1)} %collective-permute-done.6.refs_8_) | copy-start | bytes 983044
  38.4 5.9 %copy-start.7 = (bf16[160,1024]{1,0:T(8,128)(2,1)}, bf16[160,1024]{1,0:T(8,128)(2,1)S(1)}, u32[]{:S(2)}) copy-start(bf16[160,1024]{1,0:T(8,128)(2,1)S(1)} %collective-permute-done.3.refs_2_) | copy-start | bytes 983044
  39.3 5.0 %copy-start.9 = (bf16[160,1024]{1,0:T(8,128)(2,1)}, bf16[160,1024]{1,0:T(8,128)(2,1)S(1)}, u32[]{:S(2)}) copy-start(bf16[160,1024]{1,0:T(8,128)(2,1)S(1)} %collective-permute-done.4.refs_3_) | copy-start | bytes 983044
  39.3 5.0 %copy-start.11 = (bf16[160,1024]{1,0:T(8,128)(2,1)}, bf16[160,1024]{1,0:T(8,128)(2,1)S(1)}, u32[]{:S(2)}) copy-start(bf16[160,1024]{1,0:T(8,128)(2,1)S(1)} %collective-permute-done.7.refs_9_) | copy-start | bytes 983044
  39.6 3.0 %collective-permute-start.10 = (bf16[4,16,8,1024]{3,2,1,0:T(8,128)(2,1)}, bf16[4,16,8,1024]{3,2,1,0:T(8,128)(2,1)}, u32[]{:S(2)}, u32[]{:S(2)}) collective-permute-start(bf16[4,16,8,1024]{3,2,1,0:T(8,128)(2,1)} %all-to-all-done.1), channel_id=1, source_target_pairs={{0,4},{4,0},{1,5},{5,1},{2,6},{6,2},{3,7},{7,3},{8,12},{12,8},{9,1... | collective-permute-start | bytes 3145736 | tf_op jit(solution)/shard_map/ppermute | solution.py:21
  41.9 2.9 %collective-permute-start.8 = (bf16[160,1024]{1,0:T(8,128)(2,1)S(1)}, bf16[160,1024]{1,0:T(8,128)(2,1)S(1)}, u32[]{:S(2)}, u32[]{:S(2)}) collective-permute-start(bf16[160,1024]{1,0:T(8,128)(2,1)S(1)} %collective-permute-done.2.refs_6_), channel_id=1, source_target_pairs={{0,4},{4,0},{1,5},{5,1},{2,6},{6,2},{3,7},{7,3},{8,12},{12,8},{9,1... | collective-permute-start | bytes 983048 | tf_op jit(solution)/shard_map/ppermute | solution.py:21
  42.2 2.5 %collective-permute-start.9 = (bf16[160,1024]{1,0:T(8,128)(2,1)}, bf16[160,1024]{1,0:T(8,128)(2,1)S(1)}, u32[]{:S(2)}, u32[]{:S(2)}) collective-permute-start(bf16[160,1024]{1,0:T(8,128)(2,1)} %collective-permute-done.5.refs_7_), channel_id=1, source_target_pairs={{0,4},{4,0},{1,5},{5,1},{2,6},{6,2},{3,7},{7,3},{8,12},{12,8},{9,1... | collective-permute-start | bytes 983048 | tf_op jit(solution)/shard_map/ppermute | solution.py:21
  44.5 1.0 copy-start.4
  44.5 1.1 copy-start.6
  44.5 1.2 %copy-start.8 = (bf16[160,1024]{1,0:T(8,128)(2,1)S(1)}, bf16[160,1024]{1,0:T(8,128)(2,1)}, u32[]{:S(2)}) copy-start(bf16[160,1024]{1,0:T(8,128)(2,1)} %copy-done.7) | copy-start | bytes 983044
  44.5 1.2 %copy-start.10 = (bf16[160,1024]{1,0:T(8,128)(2,1)S(1)}, bf16[160,1024]{1,0:T(8,128)(2,1)}, u32[]{:S(2)}) copy-start(bf16[160,1024]{1,0:T(8,128)(2,1)} %copy-done.9) | copy-start | bytes 983044
  44.5 1.3 %copy-start.12 = (bf16[160,1024]{1,0:T(8,128)(2,1)S(1)}, bf16[160,1024]{1,0:T(8,128)(2,1)}, u32[]{:S(2)}) copy-start(bf16[160,1024]{1,0:T(8,128)(2,1)} %copy-done.11) | copy-start | bytes 983044
  53.9 5.2 %collective-permute-start.13 = (f32[8,256]{1,0:T(8,128)S(1)}, f32[8,256]{1,0:T(8,128)S(1)}, u32[]{:S(2)}, u32[]{:S(2)}) collective-permute-start(f32[8,256]{1,0:T(8,128)S(1)} %get-tuple-element.58.here), channel_id=1, source_target_pairs={{0,16},{4,20},{8,24},{12,28},{16,0},{20,4},{24,8},{28,12},{1,17},{... | collective-permute-start | bytes 24584 | tf_op jit(solution)/shard_map/ppermute | solution.py:28
  54.4 4.7 %collective-permute-start.12 = (f32[8,256]{1,0:T(8,128)S(1)}, f32[8,256]{1,0:T(8,128)S(1)}, u32[]{:S(2)}, u32[]{:S(2)}) collective-permute-start(f32[8,256]{1,0:T(8,128)S(1)} %get-tuple-element.58.here), channel_id=1, source_target_pairs={{0,24},{4,12},{8,0},{12,20},{16,8},{20,28},{24,16},{28,4},{1,25},{... | collective-permute-start | bytes 24584 | tf_op jit(solution)/shard_map/ppermute | solution.py:28
  56.7 4.9 %collective-permute-start.11 = (f32[8,256]{1,0:T(8,128)S(1)}, f32[8,256]{1,0:T(8,128)S(1)}, u32[]{:S(2)}, u32[]{:S(2)}) collective-permute-start(f32[8,256]{1,0:T(8,128)S(1)} %get-tuple-element.58.here), channel_id=1, source_target_pairs={{0,8},{4,28},{8,16},{12,4},{16,24},{20,12},{24,0},{28,20},{1,9},{5... | collective-permute-start | bytes 24584 | tf_op jit(solution)/shard_map/ppermute | solution.py:28
  69.3 4.8 %collective-permute-start.15 = (bf16[640,1024]{1,0:T(8,128)(2,1)S(1)}, bf16[640,1024]{1,0:T(8,128)(2,1)S(1)}, u32[]{:S(2)}, u32[]{:S(2)}) collective-permute-start(bf16[640,1024]{1,0:T(8,128)(2,1)S(1)} %get-tuple-element.71), channel_id=1, source_target_pairs={{0,4},{4,0},{1,5},{5,1},{2,6},{6,2},{3,7},{7,3},{8,12},{12,8},{9,1... | collective-permute-start | bytes 3932168 | tf_op jit(solution)/shard_map/ppermute | solution.py:21
  69.4 4.5 %collective-permute-start.14 = (bf16[512,1024]{1,0:T(8,128)(2,1)S(1)}, bf16[512,1024]{1,0:T(8,128)(2,1)S(1)}, u32[]{:S(2)}, u32[]{:S(2)}) collective-permute-start(bf16[512,1024]{1,0:T(8,128)(2,1)S(1)} %get-tuple-element.70), channel_id=1, source_target_pairs={{0,4},{4,0},{1,5},{5,1},{2,6},{6,2},{3,7},{7,3},{8,12},{12,8},{9,1... | collective-permute-start | bytes 3145736 | tf_op jit(solution)/shard_map/ppermute | solution.py:21
  70.4 8.3 %collective-permute-start.18 = (bf16[160,1024]{1,0:T(8,128)(2,1)S(1)}, bf16[160,1024]{1,0:T(8,128)(2,1)S(1)}, u32[]{:S(2)}, u32[]{:S(2)}) collective-permute-start(bf16[160,1024]{1,0:T(8,128)(2,1)S(1)} %get-tuple-element.76), channel_id=1, source_target_pairs={{0,8},{4,28},{8,16},{12,4},{16,24},{20,12},{24,0},{28,20},{1,9},{5... | collective-permute-start | bytes 983048 | tf_op jit(solution)/shard_map/ppermute | solution.py:28
  74.1 12.6 %copy-start.13 = (bf16[640,1024]{1,0:T(8,128)(2,1)}, bf16[640,1024]{1,0:T(8,128)(2,1)S(1)}, u32[]{:S(2)}) copy-start(bf16[640,1024]{1,0:T(8,128)(2,1)S(1)} %collective-permute-done.15) | copy-start | bytes 3932164
  74.1 9.0 %collective-permute-start.16 = (bf16[128,1024]{1,0:T(8,128)(2,1)S(1)}, bf16[128,1024]{1,0:T(8,128)(2,1)S(1)}, u32[]{:S(2)}, u32[]{:S(2)}) collective-permute-start(bf16[128,1024]{1,0:T(8,128)(2,1)S(1)} %get-tuple-element.72), channel_id=1, source_target_pairs={{0,1},{4,7},{1,2},{5,4},{2,3},{6,5},{3,0},{7,6},{8,9},{12,15},{9,1... | collective-permute-start | bytes 786440 | tf_op jit(solution)/shard_map/ppermute | solution.py:28
  76.6 9.0 %collective-permute-start.21 = (bf16[160,1024]{1,0:T(8,128)(2,1)S(1)}, bf16[160,1024]{1,0:T(8,128)(2,1)S(1)}, u32[]{:S(2)}, u32[]{:S(2)}) collective-permute-start(bf16[160,1024]{1,0:T(8,128)(2,1)S(1)} %get-tuple-element.89), channel_id=1, source_target_pairs={{0,32},{4,100},{32,64},{36,4},{64,96},{68,36},{96,0},{100,68},{1,3... | collective-permute-start | bytes 983048 | tf_op jit(solution)/shard_map/ppermute | solution.py:28
  79.5 17.4 %collective-permute-start.19 = (bf16[160,1024]{1,0:T(8,128)(2,1)}, bf16[160,1024]{1,0:T(8,128)(2,1)}, u32[]{:S(2)}, u32[]{:S(2)}) collective-permute-start(bf16[160,1024]{1,0:T(8,128)(2,1)} %add_convert_fusion.3), channel_id=1, source_target_pairs={{0,8},{4,28},{8,16},{12,4},{16,24},{20,12},{24,0},{28,20},{1,9},{5... | collective-permute-start | bytes 983048 | tf_op jit(solution)/shard_map/ppermute | solution.py:28
  79.5 9.1 %collective-permute-start.23 = (bf16[128,1024]{1,0:T(8,128)(2,1)S(1)}, bf16[128,1024]{1,0:T(8,128)(2,1)S(1)}, u32[]{:S(2)}, u32[]{:S(2)}) collective-permute-start(bf16[128,1024]{1,0:T(8,128)(2,1)S(1)} %get-tuple-element.82), channel_id=1, source_target_pairs={{0,3},{4,5},{1,0},{5,6},{2,1},{6,7},{3,2},{7,4},{8,11},{12,13},{9,... | collective-permute-start | bytes 786440 | tf_op jit(solution)/shard_map/ppermute | solution.py:28
  82.2 17.5 %collective-permute-start.20 = (bf16[160,1024]{1,0:T(8,128)(2,1)}, bf16[160,1024]{1,0:T(8,128)(2,1)}, u32[]{:S(2)}, u32[]{:S(2)}) collective-permute-start(bf16[160,1024]{1,0:T(8,128)(2,1)} %get-tuple-element.88), channel_id=1, source_target_pairs={{0,96},{4,36},{32,0},{36,68},{64,32},{68,100},{96,64},{100,4},{1,9... | collective-permute-start | bytes 983048 | tf_op jit(solution)/shard_map/ppermute | solution.py:28
  83.3 7.7 %collective-permute-start.24 = (bf16[128,1024]{1,0:T(8,128)(2,1)S(1)}, bf16[128,1024]{1,0:T(8,128)(2,1)S(1)}, u32[]{:S(2)}, u32[]{:S(2)}) collective-permute-start(bf16[128,1024]{1,0:T(8,128)(2,1)S(1)} %add_convert_fusion.5), channel_id=1, source_target_pairs={{0,1},{4,7},{1,2},{5,4},{2,3},{6,5},{3,0},{7,6},{8,9},{12,15},{9,1... | collective-permute-start | bytes 786440 | tf_op jit(solution)/shard_map/ppermute | solution.py:28
  85.6 11.4 %collective-permute-start.17 = (bf16[160,1024]{1,0:T(8,128)(2,1)}, bf16[160,1024]{1,0:T(8,128)(2,1)}, u32[]{:S(2)}, u32[]{:S(2)}) collective-permute-start(bf16[160,1024]{1,0:T(8,128)(2,1)} %get-tuple-element.74), channel_id=1, source_target_pairs={{0,24},{4,12},{8,0},{12,20},{16,8},{20,28},{24,16},{28,4},{1,25},{... | collective-permute-start | bytes 983048 | tf_op jit(solution)/shard_map/ppermute | solution.py:28
  88.6 11.0 %collective-permute-start.22 = (bf16[160,1024]{1,0:T(8,128)(2,1)}, bf16[160,1024]{1,0:T(8,128)(2,1)}, u32[]{:S(2)}, u32[]{:S(2)}) collective-permute-start(bf16[160,1024]{1,0:T(8,128)(2,1)} %add_convert_fusion), channel_id=1, source_target_pairs={{0,32},{4,100},{32,64},{36,4},{64,96},{68,36},{96,0},{100,68},{1,3... | collective-permute-start | bytes 983048 | tf_op jit(solution)/shard_map/ppermute | solution.py:28
  91.8 13.9 %all-to-all-start.2 = ((bf16[16,8,1024]{2,1,0:T(8,128)(2,1)}), bf16[16,8,1024]{2,1,0:T(8,128)(2,1)}, u32[]{:S(2)}, u32[]{:S(2)}) async-start(bf16[16,8,1024]{2,1,0:T(8,128)(2,1)} %fusion.5), calls=%async_computation.2 | async-start | bytes 524288 | tf_op jit(solution)/shard_map/all_to_all | solution.py:251
